TPU v7x, 32 devices: a whole 2x2x4 slice. The times are simulated.
32 devices in a mesh: view: 16 (over z, y, x), head: 2 (over core).
Axes of the slice: x: 2, y: 2, z: 4, core: 2. Of those that a mesh axis runs over, the one named last changes fastest.
Arguments:
- tokens: bfloat16 [2, 16, 128, 1024], P(None, 'view'), may hold values from -6 to 6
- queries: bfloat16 [2, 16, 128, 1024], P(None, 'view', None, 'head'), may hold values from -8 to 8
- keys: bfloat16 [2, 16, 128, 1024], P(None, 'view', None, 'head'), may hold values from -8 to 8
- values: bfloat16 [2, 16, 128, 1024], P(None, 'view', None, 'head'), may hold values from -6 to 6
- w_qkv: bfloat16 [3, 1024, 1024], P(None, None, 'head'), may hold values from -0.1875 to 0.1875
- w_out: bfloat16 [1024, 1024], P('head'), may hold values from -0.1875 to 0.1875
- d_out: bfloat16 [2, 16, 128, 1024], P(None, 'view'), may hold values from -6 to 6
- neighbours: int32 [16, 8], replicated, may hold values from 0 to 15, as said below
- degrees: int32 [16], replicated, may hold values from 4 to 8, as said below
Outputs:
- d_tokens: bfloat16 [2, 16, 128, 1024], P(None, 'view', None, 'head')
- d_wqkv: float32 [3, 1024, 1024], P(None, 'view', 'head')
- d_wo: float32 [1024, 1024], P('head', 'view')
Inputs may be any that keep to these rules, and one draw needn't show every extreme that they name: Row c lists cameras c + o modulo 16 for the 8 offsets o with 0 < |o| <= 4, each once, in an order drawn per camera; its first degrees[c] entries are c's neighbours. `degrees`: some camera has 8 neighbours and some has 4.
All inputs are finite; a program needn't handle non-finite values.
Results may differ from a plain program's by a relative error of at most 0.018.
Values may be sent and summed in bfloat16 or wider, within the bound.
No kernel may reach another device: no remote copies, remote signals or barrier semaphores. Data moves between devices by JAX's collectives and lax.ppermute only.
A program may use at most 128 MiB of HBM per device.

v0:
```python
import jax
import jax.numpy as jnp
from jax import lax
from jax.sharding import PartitionSpec as P

HD = 64


def shifted(value, axis, steps):
    count = lax.axis_size(axis)
    pairs = [(source, (source + steps) % count) for source in range(count)]
    return lax.ppermute(value, axis, pairs)


def body(tokens, queries, keys, values, w_qkv, w_out, d_out, neighbours, degrees):
    cameras = neighbours.shape[0]
    reach = neighbours.shape[1] // 2
    offsets = [step for step in range(-reach, reach + 1) if step != 0]
    camera = lax.axis_index("view")
    scenes, _, rows, width = queries.shape
    local_heads = width // HD
    scale = HD ** (-0.5)

    def split_heads(arr):
        return arr.reshape(scenes, rows, local_heads, HD)

    query = split_heads(queries)
    key_own = split_heads(keys)
    value_own = split_heads(values)
    d_flat = jnp.einsum(
        "std,ed->ste", d_out[:, 0], w_out, preferred_element_type=jnp.float32
    ).astype(jnp.bfloat16)
    d_heads = split_heads(d_flat)
    blocks = [(key_own, value_own, jnp.float32(1.0), 0)]
    for offset in offsets:
        key_far, value_far = shifted((keys, values), "view", -offset)
        listed = lax.dynamic_index_in_dim(neighbours, camera, 0, keepdims=False)
        count = lax.dynamic_index_in_dim(degrees, camera, 0, keepdims=False)
        target = (camera + offset) % cameras
        slots = jnp.arange(neighbours.shape[1], dtype=jnp.int32)
        hit = jnp.logical_and(listed == target, slots < count)
        blocks.append(
            (
                split_heads(key_far),
                split_heads(value_far),
                jnp.where(jnp.any(hit), 1.0, 0.0).astype(jnp.float32),
                offset,
            )
        )

    def block_scores(qry, key_blk):
        return (
            jnp.einsum("sthd,suhd->shtu", qry, key_blk, preferred_element_type=jnp.float32) * scale
        )

    top = jnp.full((scenes, local_heads, rows), -jnp.inf, jnp.float32)
    total = jnp.zeros((scenes, local_heads, rows), jnp.float32)
    for key_blk, value_blk, weight, offset in blocks:
        block = block_scores(query, key_blk)
        peak = jnp.where(weight > 0, jnp.max(block, axis=3), -jnp.inf)
        new_top = jnp.maximum(top, peak)
        factor = jnp.exp(top - new_top)
        prob = jnp.exp(block - new_top[..., None]) * weight
        total = total * factor + jnp.sum(prob, axis=3)
        top = new_top
    lse = top + jnp.log(total)
    accum = jnp.zeros((scenes, rows, local_heads, HD), jnp.float32)
    for key_blk, value_blk, weight, offset in blocks:
        prob_low = (jnp.exp(block_scores(query, key_blk) - lse[..., None]) * weight).astype(
            jnp.bfloat16
        )
        accum = accum + jnp.einsum(
            "shtu,suhd->sthd", prob_low, value_blk, preferred_element_type=jnp.float32
        )
    attended = accum.astype(jnp.bfloat16)
    delta = jnp.transpose(
        jnp.sum(d_heads.astype(jnp.float32) * attended.astype(jnp.float32), axis=3), (0, 2, 1)
    )

    def backward_block(qry, d_q, lse_blk, delta_blk, key_blk, value_blk, weight):
        block = block_scores(qry, key_blk)
        prob = jnp.exp(block - lse_blk[..., None]) * weight
        d_prob = jnp.einsum("sthd,suhd->shtu", d_q, value_blk, preferred_element_type=jnp.float32)
        d_score = (prob * (d_prob - delta_blk[..., None])).astype(jnp.bfloat16)
        d_key = (
            jnp.einsum("shtu,sthd->suhd", d_score, qry, preferred_element_type=jnp.float32) * scale
        )
        d_value = jnp.einsum(
            "shtu,sthd->suhd", prob.astype(jnp.bfloat16), d_q, preferred_element_type=jnp.float32
        )
        d_query = None
        d_query = (
            jnp.einsum("shtu,suhd->sthd", d_score, key_blk, preferred_element_type=jnp.float32)
            * scale
        )
        return (d_query, d_key, d_value)

    d_query = jnp.zeros(query.shape, jnp.float32)
    d_key = jnp.zeros(query.shape, jnp.float32)
    d_value = jnp.zeros(query.shape, jnp.float32)
    for key_blk, value_blk, weight, offset in blocks:
        part_query, part_key, part_value = backward_block(
            query, d_heads, lse, delta, key_blk, value_blk, weight
        )
        d_query = d_query + part_query
        if offset == 0:
            d_key = part_key
            d_value = part_value
        else:
            back_key, back_value = shifted((part_key, part_value), "view", offset)
            d_key = d_key + back_key
            d_value = d_value + back_value
    grads = (
        jnp.stack([d_query, d_key, d_value]).reshape(3, scenes, rows, width).astype(jnp.bfloat16)
    )
    token_terms = jnp.einsum("jste,jde->std", grads, w_qkv, preferred_element_type=jnp.float32)[
        :, None
    ]
    d_tokens = lax.psum_scatter(token_terms, "head", scatter_dimension=3, tiled=True).astype(
        jnp.bfloat16
    )
    attended_flat = attended.reshape(scenes, rows, width)
    wqkv_terms = jnp.einsum(
        "std,jste->jde", tokens[:, 0], grads, preferred_element_type=jnp.float32
    )
    wo_terms = jnp.einsum(
        "ste,std->ed", attended_flat, d_out[:, 0], preferred_element_type=jnp.float32
    )
    d_wqkv, d_wo = (
        lax.psum_scatter(wqkv_terms, "view", scatter_dimension=1, tiled=True),
        lax.psum_scatter(wo_terms, "view", scatter_dimension=1, tiled=True),
    )
    return (d_tokens, d_wqkv, d_wo)


def solution(mesh):
    return jax.shard_map(
        body,
        mesh=mesh,
        in_specs=(
            P(None, "view", None, None),
            P(None, "view", None, "head"),
            P(None, "view", None, "head"),
            P(None, "view", None, "head"),
            P(None, None, "head"),
            P("head", None),
            P(None, "view", None, None),
            P(),
            P(),
        ),
        out_specs=(P(None, "view", None, "head"), P(None, "view", "head"), P("head", "view")),
        check_vma=False,
    )
```

profile of v0, /device:TPU:0, one launch (start us, length us, event | category | flops | bytes accessed | tf_op | source)
XLA Modules:
  0.0 583.7 jit_solution(2099575805340114670)
XLA Ops:
  8.1 5.1 collective-permute-start.7
  19.8 2.6 convolution_convert_fusion
  52.1 3.3 collective-permute-start.1
  64.7 2.9 collective-permute-start.15
  82.5 2.8 collective-permute-start.12
  87.1 2.4 fusion.111
  110.0 2.5 convolution_add_fusion.3
  112.5 2.5 convolution_bitcast_fusion.9
  119.9 3.3 collective-permute-start.9
  129.1 2.4 fusion.88
  133.3 2.4 fusion.91
  146.0 3.6 multiply_reduce_fusion.8
  163.6 3.0 collective-permute-start.28
  166.6 2.6 collective-permute-start.27
  170.9 6.0 %collective-permute-done.31 = f32[2,128,8,64]{1,3,2,0:T(8,128)S(1)} collective-permute-done((f32[2,128,8,64]{1,3,2,0:T(8,128)S(1)}, f32[2,128,8,64]{1,3,2,0:T(8,128)S(1)}, u32[]{:S(2)}, u32[]{:S(2)}) %collective-permute-start.31) | collective-permute-done | bytes 524320 | tf_op jit(solution)/shard_map/ppermute | solution.py:12
  176.9 2.9 collective-permute-start.26
  181.5 7.7 %collective-permute-done.30 = f32[2,128,8,64]{1,3,2,0:T(8,128)S(1)} collective-permute-done((f32[2,128,8,64]{1,3,2,0:T(8,128)S(1)}, f32[2,128,8,64]{1,3,2,0:T(8,128)S(1)}, u32[]{:S(2)}, u32[]{:S(2)}) %collective-permute-start.30) | collective-permute-done | bytes 524320 | tf_op jit(solution)/shard_map/ppermute | solution.py:12
  189.2 4.0 collective-permute-start.25
  193.2 8.5 %collective-permute-done.29 = f32[2,128,8,64]{1,3,2,0:T(8,128)S(1)} collective-permute-done((f32[2,128,8,64]{1,3,2,0:T(8,128)S(1)}, f32[2,128,8,64]{1,3,2,0:T(8,128)S(1)}, u32[]{:S(2)}, u32[]{:S(2)}) %collective-permute-start.29) | collective-permute-done | bytes 524320 | tf_op jit(solution)/shard_map/ppermute | solution.py:12
  201.7 21.4 %collective-permute-start.24 = (f32[2,128,8,64]{1,3,2,0:T(8,128)S(1)}, f32[2,128,8,64]{1,3,2,0:T(8,128)S(1)}, u32[]{:S(2)}, u32[]{:S(2)}) collective-permute-start(f32[2,128,8,64]{1,3,2,0:T(8,128)S(1)} %copy-done.43), channel_id=1, source_target_pairs={{0,24},{2,26},{4,28},{6,30},{8,0},{10,2},{12,4},{14,6},{16,8},{18,... | collective-permute-start | bytes 1572872 | tf_op jit(solution)/shard_map/ppermute | solution.py:12
  224.7 10.8 %collective-permute-done.24 = f32[2,128,8,64]{1,3,2,0:T(8,128)S(1)} collective-permute-done((f32[2,128,8,64]{1,3,2,0:T(8,128)S(1)}, f32[2,128,8,64]{1,3,2,0:T(8,128)S(1)}, u32[]{:S(2)}, u32[]{:S(2)}) %collective-permute-start.24) | collective-permute-done | bytes 524320 | tf_op jit(solution)/shard_map/ppermute | solution.py:12
  235.5 11.2 %collective-permute-done.23 = f32[2,128,8,64]{1,3,2,0:T(8,128)} collective-permute-done((f32[2,128,8,64]{1,3,2,0:T(8,128)S(1)}, f32[2,128,8,64]{1,3,2,0:T(8,128)}, u32[]{:S(2)}, u32[]{:S(2)}) %collective-permute-start.23) | collective-permute-done | bytes 524320 | tf_op jit(solution)/shard_map/ppermute | solution.py:12
  246.7 3.4 collective-permute-start.17
  250.1 7.8 %collective-permute-done.21 = f32[2,128,8,64]{1,3,2,0:T(8,128)} collective-permute-done((f32[2,128,8,64]{1,3,2,0:T(8,128)S(1)}, f32[2,128,8,64]{1,3,2,0:T(8,128)}, u32[]{:S(2)}, u32[]{:S(2)}) %collective-permute-start.21) | collective-permute-done | bytes 524320 | tf_op jit(solution)/shard_map/ppermute | solution.py:12
  257.9 17.7 %collective-permute-start.16 = (f32[2,128,8,64]{1,3,2,0:T(8,128)}, f32[2,128,8,64]{1,3,2,0:T(8,128)}, u32[]{:S(2)}, u32[]{:S(2)}) collective-permute-start(f32[2,128,8,64]{1,3,2,0:T(8,128)} %fusion.51), channel_id=1, source_target_pairs={{0,24},{2,26},{4,28},{6,30},{8,0},{10,2},{12,4},{14,6},{16,8},{18,... | collective-permute-start | bytes 1572872 | tf_op jit(solution)/shard_map/ppermute | solution.py:12
  278.5 3.7 fusion.64
  284.0 2.9 fusion.61
  287.7 3.2 fusion.2
  291.0 4.9 convolution_bitcast_fusion
  295.9 9.4 %copy.264 = f32[3,1024,512]{2,0,1:T(4,128)} copy(f32[3,1024,512]{1,2,0:T(8,128)} %convolution_bitcast_fusion) | data formatting | bytes 12582912 | tf_op jit(solution)/shard_map/std,jste->jde/transpose | solution.py:123
  306.3 2.9 convolution_bitcast_fusion.1
  312.2 262.0 %all-reduce.3.cloned.1.call-done = f32[3,1024,512]{2,0,1:T(4,128)} async-done(((f32[3,1024,512]{2,0,1:T(4,128)}), f32[3,1024,512]{2,0,1:T(4,128)}) %all-reduce.3.cloned.1.call-update) | async-done | bytes 6291472
  (266 shorter events, 129.6 us)
Async XLA Ops:
  8.0 302.4 %reduce-scatter.3.cloned.1.call-start = ((), (), s32[]{:S(2)}) async-start(), calls=%async_computation.2 | async-start | bytes 1572864 | tf_op jit(solution)/shard_map/reduce_scatter | solution.py:119
  8.1 39.1 %collective-permute-start.7 = (bf16[2,1,128,512]{3,2,1,0:T(8,128)(2,1)}, bf16[2,1,128,512]{3,2,1,0:T(8,128)(2,1)}, u32[]{:S(2)}, u32[]{:S(2)}) collective-permute-start(bf16[2,1,128,512]{3,2,1,0:T(8,128)(2,1)} %param.11), channel_id=1, source_target_pairs={{0,24},{2,26},{4,28},{6,30},{8,0},{10,2},{12,4},{14,6},{16,8},{18,... | collective-permute-start | bytes 786440 | tf_op jit(solution)/shard_map/ppermute | solution.py:12
  13.2 38.9 %collective-permute-start.6 = (bf16[2,1,128,512]{3,2,1,0:T(8,128)(2,1)}, bf16[2,1,128,512]{3,2,1,0:T(8,128)(2,1)}, u32[]{:S(2)}, u32[]{:S(2)}) collective-permute-start(bf16[2,1,128,512]{3,2,1,0:T(8,128)(2,1)} %param.11), channel_id=1, source_target_pairs={{0,26},{2,28},{4,30},{6,0},{8,2},{10,4},{12,6},{14,8},{16,10},{18,... | collective-permute-start | bytes 786440 | tf_op jit(solution)/shard_map/ppermute | solution.py:12
  14.6 45.0 %collective-permute-start.5 = (bf16[2,1,128,512]{3,2,1,0:T(8,128)(2,1)}, bf16[2,1,128,512]{3,2,1,0:T(8,128)(2,1)}, u32[]{:S(2)}, u32[]{:S(2)}) collective-permute-start(bf16[2,1,128,512]{3,2,1,0:T(8,128)(2,1)} %param.11), channel_id=1, source_target_pairs={{0,28},{2,30},{4,0},{6,2},{8,4},{10,6},{12,8},{14,10},{16,12},{18,... | collective-permute-start | bytes 786440 | tf_op jit(solution)/shard_map/ppermute | solution.py:12
  16.0 48.8 %collective-permute-start.4 = (bf16[2,1,128,512]{3,2,1,0:T(8,128)(2,1)}, bf16[2,1,128,512]{3,2,1,0:T(8,128)(2,1)}, u32[]{:S(2)}, u32[]{:S(2)}) collective-permute-start(bf16[2,1,128,512]{3,2,1,0:T(8,128)(2,1)} %param.11), channel_id=1, source_target_pairs={{0,30},{2,0},{4,2},{6,4},{8,6},{10,8},{12,10},{14,12},{16,14},{18,... | collective-permute-start | bytes 786440 | tf_op jit(solution)/shard_map/ppermute | solution.py:12
  17.4 54.4 %collective-permute-start.3 = (bf16[2,1,128,512]{3,2,1,0:T(8,128)(2,1)}, bf16[2,1,128,512]{3,2,1,0:T(8,128)(2,1)}, u32[]{:S(2)}, u32[]{:S(2)}) collective-permute-start(bf16[2,1,128,512]{3,2,1,0:T(8,128)(2,1)} %param.11), channel_id=1, source_target_pairs={{0,2},{2,4},{4,6},{6,8},{8,10},{10,12},{12,14},{14,16},{16,18},{18... | collective-permute-start | bytes 786440 | tf_op jit(solution)/shard_map/ppermute | solution.py:12
  47.2 28.7 %collective-permute-start.2 = (bf16[2,1,128,512]{3,2,1,0:T(8,128)(2,1)}, bf16[2,1,128,512]{3,2,1,0:T(8,128)(2,1)}, u32[]{:S(2)}, u32[]{:S(2)}) collective-permute-start(bf16[2,1,128,512]{3,2,1,0:T(8,128)(2,1)} %param.11), channel_id=1, source_target_pairs={{0,4},{2,6},{4,8},{6,10},{8,12},{10,14},{12,16},{14,18},{16,20},{1... | collective-permute-start | bytes 786440 | tf_op jit(solution)/shard_map/ppermute | solution.py:12
  52.1 30.4 %collective-permute-start.1 = (bf16[2,1,128,512]{3,2,1,0:T(8,128)(2,1)}, bf16[2,1,128,512]{3,2,1,0:T(8,128)(2,1)}, u32[]{:S(2)}, u32[]{:S(2)}) collective-permute-start(bf16[2,1,128,512]{3,2,1,0:T(8,128)(2,1)} %param.11), channel_id=1, source_target_pairs={{0,6},{2,8},{4,10},{6,12},{8,14},{10,16},{12,18},{14,20},{16,22},{... | collective-permute-start | bytes 786440 | tf_op jit(solution)/shard_map/ppermute | solution.py:12
  59.6 29.9 %collective-permute-start = (bf16[2,1,128,512]{3,2,1,0:T(8,128)(2,1)}, bf16[2,1,128,512]{3,2,1,0:T(8,128)(2,1)}, u32[]{:S(2)}, u32[]{:S(2)}) collective-permute-start(bf16[2,1,128,512]{3,2,1,0:T(8,128)(2,1)} %param.11), channel_id=1, source_target_pairs={{0,8},{2,10},{4,12},{6,14},{8,16},{10,18},{12,20},{14,22},{16,24},... | collective-permute-start | bytes 786440 | tf_op jit(solution)/shard_map/ppermute | solution.py:12
  64.7 50.3 %collective-permute-start.15 = (bf16[2,1,128,512]{3,2,1,0:T(8,128)(2,1)}, bf16[2,1,128,512]{3,2,1,0:T(8,128)(2,1)}, u32[]{:S(2)}, u32[]{:S(2)}) collective-permute-start(bf16[2,1,128,512]{3,2,1,0:T(8,128)(2,1)} %param.12), channel_id=1, source_target_pairs={{0,24},{2,26},{4,28},{6,30},{8,0},{10,2},{12,4},{14,6},{16,8},{18,... | collective-permute-start | bytes 786440 | tf_op jit(solution)/shard_map/ppermute | solution.py:12
  71.8 48.1 %collective-permute-start.14 = (bf16[2,1,128,512]{3,2,1,0:T(8,128)(2,1)}, bf16[2,1,128,512]{3,2,1,0:T(8,128)(2,1)}, u32[]{:S(2)}, u32[]{:S(2)}) collective-permute-start(bf16[2,1,128,512]{3,2,1,0:T(8,128)(2,1)} %param.12), channel_id=1, source_target_pairs={{0,26},{2,28},{4,30},{6,0},{8,2},{10,4},{12,6},{14,8},{16,10},{18,... | collective-permute-start | bytes 786440 | tf_op jit(solution)/shard_map/ppermute | solution.py:12
  76.0 51.3 %collective-permute-start.13 = (bf16[2,1,128,512]{3,2,1,0:T(8,128)(2,1)}, bf16[2,1,128,512]{3,2,1,0:T(8,128)(2,1)}, u32[]{:S(2)}, u32[]{:S(2)}) collective-permute-start(bf16[2,1,128,512]{3,2,1,0:T(8,128)(2,1)} %param.12), channel_id=1, source_target_pairs={{0,28},{2,30},{4,0},{6,2},{8,4},{10,6},{12,8},{14,10},{16,12},{18,... | collective-permute-start | bytes 786440 | tf_op jit(solution)/shard_map/ppermute | solution.py:12
  82.5 49.0 %collective-permute-start.12 = (bf16[2,1,128,512]{3,2,1,0:T(8,128)(2,1)}, bf16[2,1,128,512]{3,2,1,0:T(8,128)(2,1)}, u32[]{:S(2)}, u32[]{:S(2)}) collective-permute-start(bf16[2,1,128,512]{3,2,1,0:T(8,128)(2,1)} %param.12), channel_id=1, source_target_pairs={{0,30},{2,0},{4,2},{6,4},{8,6},{10,8},{12,10},{14,12},{16,14},{18,... | collective-permute-start | bytes 786440 | tf_op jit(solution)/shard_map/ppermute | solution.py:12
  108.2 27.6 %collective-permute-start.11 = (bf16[2,1,128,512]{3,2,1,0:T(8,128)(2,1)}, bf16[2,1,128,512]{3,2,1,0:T(8,128)(2,1)}, u32[]{:S(2)}, u32[]{:S(2)}) collective-permute-start(bf16[2,1,128,512]{3,2,1,0:T(8,128)(2,1)} %param.12), channel_id=1, source_target_pairs={{0,2},{2,4},{4,6},{6,8},{8,10},{10,12},{12,14},{14,16},{16,18},{18... | collective-permute-start | bytes 786440 | tf_op jit(solution)/shard_map/ppermute | solution.py:12
  115.0 25.0 %collective-permute-start.10 = (bf16[2,1,128,512]{3,2,1,0:T(8,128)(2,1)}, bf16[2,1,128,512]{3,2,1,0:T(8,128)(2,1)}, u32[]{:S(2)}, u32[]{:S(2)}) collective-permute-start(bf16[2,1,128,512]{3,2,1,0:T(8,128)(2,1)} %param.12), channel_id=1, source_target_pairs={{0,4},{2,6},{4,8},{6,10},{8,12},{10,14},{12,16},{14,18},{16,20},{1... | collective-permute-start | bytes 786440 | tf_op jit(solution)/shard_map/ppermute | solution.py:12
  119.9 24.3 %collective-permute-start.9 = (bf16[2,1,128,512]{3,2,1,0:T(8,128)(2,1)}, bf16[2,1,128,512]{3,2,1,0:T(8,128)(2,1)}, u32[]{:S(2)}, u32[]{:S(2)}) collective-permute-start(bf16[2,1,128,512]{3,2,1,0:T(8,128)(2,1)} %param.12), channel_id=1, source_target_pairs={{0,6},{2,8},{4,10},{6,12},{8,14},{10,16},{12,18},{14,20},{16,22},{... | collective-permute-start | bytes 786440 | tf_op jit(solution)/shard_map/ppermute | solution.py:12
  160.3 28.9 %collective-permute-start.30 = (f32[2,128,8,64]{1,3,2,0:T(8,128)S(1)}, f32[2,128,8,64]{1,3,2,0:T(8,128)S(1)}, u32[]{:S(2)}, u32[]{:S(2)}) collective-permute-start(f32[2,128,8,64]{1,3,2,0:T(8,128)S(1)} %copy-done.48), channel_id=1, source_target_pairs={{0,6},{2,8},{4,10},{6,12},{8,14},{10,16},{12,18},{14,20},{16,22},{... | collective-permute-start | bytes 1572872 | tf_op jit(solution)/shard_map/ppermute | solution.py:12
  162.1 39.6 %collective-permute-start.29 = (f32[2,128,8,64]{1,3,2,0:T(8,128)S(1)}, f32[2,128,8,64]{1,3,2,0:T(8,128)S(1)}, u32[]{:S(2)}, u32[]{:S(2)}) collective-permute-start(f32[2,128,8,64]{1,3,2,0:T(8,128)S(1)} %copy-done.47), channel_id=1, source_target_pairs={{0,4},{2,6},{4,8},{6,10},{8,12},{10,14},{12,16},{14,18},{16,20},{1... | collective-permute-start | bytes 1572872 | tf_op jit(solution)/shard_map/ppermute | solution.py:12
  163.6 59.5 %collective-permute-start.28 = (f32[2,128,8,64]{1,3,2,0:T(8,128)S(1)}, f32[2,128,8,64]{1,3,2,0:T(8,128)S(1)}, u32[]{:S(2)}, u32[]{:S(2)}) collective-permute-start(f32[2,128,8,64]{1,3,2,0:T(8,128)S(1)} %copy-done.46), channel_id=1, source_target_pairs={{0,2},{2,4},{4,6},{6,8},{8,10},{10,12},{12,14},{14,16},{16,18},{18... | collective-permute-start | bytes 1572872 | tf_op jit(solution)/shard_map/ppermute | solution.py:12
  166.6 56.5 %collective-permute-start.27 = (f32[2,128,8,64]{1,3,2,0:T(8,128)S(1)}, f32[2,128,8,64]{1,3,2,0:T(8,128)S(1)}, u32[]{:S(2)}, u32[]{:S(2)}) collective-permute-start(f32[2,128,8,64]{1,3,2,0:T(8,128)S(1)} %copy-done.45), channel_id=1, source_target_pairs={{0,30},{2,0},{4,2},{6,4},{8,6},{10,8},{12,10},{14,12},{16,14},{18,... | collective-permute-start | bytes 1572872 | tf_op jit(solution)/shard_map/ppermute | solution.py:12
  176.9 46.3 %collective-permute-start.26 = (f32[2,128,8,64]{1,3,2,0:T(8,128)S(1)}, f32[2,128,8,64]{1,3,2,0:T(8,128)S(1)}, u32[]{:S(2)}, u32[]{:S(2)}) collective-permute-start(f32[2,128,8,64]{1,3,2,0:T(8,128)S(1)} %copy-done.44), channel_id=1, source_target_pairs={{0,28},{2,30},{4,0},{6,2},{8,4},{10,6},{12,8},{14,10},{16,12},{18,... | collective-permute-start | bytes 1572872 | tf_op jit(solution)/shard_map/ppermute | solution.py:12
  189.2 34.7 %collective-permute-start.25 = (f32[2,128,8,64]{1,3,2,0:T(8,128)S(1)}, f32[2,128,8,64]{1,3,2,0:T(8,128)S(1)}, u32[]{:S(2)}, u32[]{:S(2)}) collective-permute-start(f32[2,128,8,64]{1,3,2,0:T(8,128)S(1)} %copy-done.42), channel_id=1, source_target_pairs={{0,26},{2,28},{4,30},{6,0},{8,2},{10,4},{12,6},{14,8},{16,10},{18,... | collective-permute-start | bytes 1572872 | tf_op jit(solution)/shard_map/ppermute | solution.py:12
  201.7 33.8 %collective-permute-start.24 = (f32[2,128,8,64]{1,3,2,0:T(8,128)S(1)}, f32[2,128,8,64]{1,3,2,0:T(8,128)S(1)}, u32[]{:S(2)}, u32[]{:S(2)}) collective-permute-start(f32[2,128,8,64]{1,3,2,0:T(8,128)S(1)} %copy-done.43), channel_id=1, source_target_pairs={{0,24},{2,26},{4,28},{6,30},{8,0},{10,2},{12,4},{14,6},{16,8},{18,... | collective-permute-start | bytes 1572872 | tf_op jit(solution)/shard_map/ppermute | solution.py:12
  223.1 23.6 %collective-permute-start.23 = (f32[2,128,8,64]{1,3,2,0:T(8,128)S(1)}, f32[2,128,8,64]{1,3,2,0:T(8,128)}, u32[]{:S(2)}, u32[]{:S(2)}) collective-permute-start(f32[2,128,8,64]{1,3,2,0:T(8,128)S(1)} %fusion.44), channel_id=1, source_target_pairs={{0,8},{2,10},{4,12},{6,14},{8,16},{10,18},{12,20},{14,22},{16,24},... | collective-permute-start | bytes 1572872 | tf_op jit(solution)/shard_map/ppermute | solution.py:12
  223.2 34.7 %collective-permute-start.21 = (f32[2,128,8,64]{1,3,2,0:T(8,128)S(1)}, f32[2,128,8,64]{1,3,2,0:T(8,128)}, u32[]{:S(2)}, u32[]{:S(2)}) collective-permute-start(f32[2,128,8,64]{1,3,2,0:T(8,128)S(1)} %fusion.46), channel_id=1, source_target_pairs={{0,4},{2,6},{4,8},{6,10},{8,12},{10,14},{12,16},{14,18},{16,20},{1... | collective-permute-start | bytes 1572872 | tf_op jit(solution)/shard_map/ppermute | solution.py:12
  223.9 60.1 %collective-permute-start.20 = (f32[2,128,8,64]{1,3,2,0:T(8,128)}, f32[2,128,8,64]{1,3,2,0:T(8,128)}, u32[]{:S(2)}, u32[]{:S(2)}) collective-permute-start(f32[2,128,8,64]{1,3,2,0:T(8,128)} %fusion.47), channel_id=1, source_target_pairs={{0,2},{2,4},{4,6},{6,8},{8,10},{10,12},{12,14},{14,16},{16,18},{18... | collective-permute-start | bytes 1572872 | tf_op jit(solution)/shard_map/ppermute | solution.py:12
  235.5 48.5 %collective-permute-start.19 = (f32[2,128,8,64]{1,3,2,0:T(8,128)}, f32[2,128,8,64]{1,3,2,0:T(8,128)}, u32[]{:S(2)}, u32[]{:S(2)}) collective-permute-start(f32[2,128,8,64]{1,3,2,0:T(8,128)} %fusion.48), channel_id=1, source_target_pairs={{0,30},{2,0},{4,2},{6,4},{8,6},{10,8},{12,10},{14,12},{16,14},{18,... | collective-permute-start | bytes 1572872 | tf_op jit(solution)/shard_map/ppermute | solution.py:12
  246.7 37.3 %collective-permute-start.18 = (f32[2,128,8,64]{1,3,2,0:T(8,128)}, f32[2,128,8,64]{1,3,2,0:T(8,128)}, u32[]{:S(2)}, u32[]{:S(2)}) collective-permute-start(f32[2,128,8,64]{1,3,2,0:T(8,128)} %fusion.49), channel_id=1, source_target_pairs={{0,28},{2,30},{4,0},{6,2},{8,4},{10,6},{12,8},{14,10},{16,12},{18,... | collective-permute-start | bytes 1572872 | tf_op jit(solution)/shard_map/ppermute | solution.py:12
  246.7 37.3 %collective-permute-start.17 = (f32[2,128,8,64]{1,3,2,0:T(8,128)}, f32[2,128,8,64]{1,3,2,0:T(8,128)}, u32[]{:S(2)}, u32[]{:S(2)}) collective-permute-start(f32[2,128,8,64]{1,3,2,0:T(8,128)} %fusion.50), channel_id=1, source_target_pairs={{0,26},{2,28},{4,30},{6,0},{8,2},{10,4},{12,6},{14,8},{16,10},{18,... | collective-permute-start | bytes 1572872 | tf_op jit(solution)/shard_map/ppermute | solution.py:12
  257.9 26.1 %collective-permute-start.16 = (f32[2,128,8,64]{1,3,2,0:T(8,128)}, f32[2,128,8,64]{1,3,2,0:T(8,128)}, u32[]{:S(2)}, u32[]{:S(2)}) collective-permute-start(f32[2,128,8,64]{1,3,2,0:T(8,128)} %fusion.51), channel_id=1, source_target_pairs={{0,24},{2,26},{4,28},{6,30},{8,0},{10,2},{12,4},{14,6},{16,8},{18,... | collective-permute-start | bytes 1572872 | tf_op jit(solution)/shard_map/ppermute | solution.py:12
  290.9 283.3 %all-reduce.3.cloned.1.call-start = ((), (), s32[]{:S(2)}) async-start(), calls=%async_computation.4 | async-start | bytes 16777216
  305.4 270.9 %reduce-scatter.5.cloned.1.call-start = ((), (), s32[]{:S(2)}) async-start(), calls=%async_computation.3 | async-start | bytes 2228224 | tf_op jit(solution)/shard_map/reduce_scatter | solution.py:131
  (64 other events, 1377.4 us)
Sparse Core Ops, SparseCore 0:
  291.1 7.2 reduce-scatter.2
  309.3 138.1 reduce-scatter.4
Sparse Core Ops, SparseCore 1:
  305.4 268.7 all-reduce.2
where the time goes:
time: 586 us; the launch traced here: 584 us
  waiting for transfers between devices  314 us (54%)
  matrix products  88.5 us (15%)
  starting transfers between devices  87.8 us (15%)
  local copies, waits for them, and re-layouts  53.7 us (9%)
  between operations  22.2 us (4%)
  other arithmetic  17.3 us (3%)
    unnamed x4, waiting for transfers between devices  262 us
    ppermute x32, starting transfers between devices, shifted(): return lax.ppermute(value, axis, pairs)  87.7 us
    ppermute x32, waiting for transfers between devices, shifted(): return lax.ppermute(value, axis, pairs)  52.1 us
    ppermute x16, local copies, waits for them, and re-layouts, shifted(): return lax.ppermute(value, axis, pairs)  28.7 us
    dot_general x9, matrix products, body(): jnp.einsum('shtu,suhd->sthd', prob_low, value_blk, preferred_element_type...  21.7 us
    dot_general x9, matrix products, block_scores(): jnp.einsum('sthd,suhd->shtu', qry, key_blk, preferred_element_type=jnp.fl...  20.6 us
    dot_general x9, matrix products, backward_block(): jnp.einsum('shtu,sthd->suhd', prob.astype(jnp.bfloat16), d_q, preferred_e...  15.1 us
  transfers between devices with their start and end apart: 35, of which 7 were waited for; matrix products, arithmetic and copies ran while one was open for 23% of the time, Pallas kernels for 0%

commit v1 on v0

--- a/solution.py
+++ b/solution.py
@@ -1,9 +1,368 @@
+import functools
+
 import jax
 import jax.numpy as jnp
 from jax import lax
+from jax.experimental import pallas as pl
+from jax.experimental.pallas import tpu as pltpu
 from jax.sharding import PartitionSpec as P
 
 HD = 64
+LANE = 128
+QUAD = 4
+BF = jnp.bfloat16
+F32 = jnp.float32
+MIB = 2**20
+OFF = -1e30
+
+
+def params(mib):
+    return pltpu.CompilerParams(vmem_limit_bytes=mib * MIB)
+
+
+def vmem(count):
+    return [pl.BlockSpec(memory_space=pltpu.VMEM)] * count
+
+
+def cost(flops, moved):
+    return pl.CostEstimate(flops=flops, bytes_accessed=moved, transcendentals=0)
+
+
+def mul(a, b):
+    return jnp.dot(a, b, preferred_element_type=F32)
+
+
+def mul_nt(a, b):
+    return lax.dot_general(a, b, (((1,), (1,)), ((), ())), preferred_element_type=F32)
+
+
+def slot_of(view):
+    plane, quad = view // QUAD, view % QUAD
+    return quad // 2, 2 * plane + quad % 2
+
+
+def pack_qk_kernel(q_ref, k_ref, out_ref):
+    scenes = q_ref.shape[0]
+    turned = []
+    for scene in range(scenes):
+        turned.append((q_ref[scene, 0].T * HD**-0.5, k_ref[scene, 0].T))
+    for view in range(out_ref.shape[0]):
+        scene, head = slot_of(view)
+        qry, key = turned[scene]
+        out_ref[view, :HD] = qry[head * HD : (head + 1) * HD].astype(BF)
+        out_ref[view, HD:] = key[head * HD : (head + 1) * HD]
+
+
+def pack_vd_kernel(v_ref, d_ref, w_ref, out_ref):
+    scenes = v_ref.shape[0]
+    turned = []
+    for scene in range(scenes):
+        d_head = mul_nt(w_ref[...], d_ref[scene, 0]).astype(BF)
+        turned.append((v_ref[scene, 0].T, d_head))
+    for view in range(out_ref.shape[0]):
+        scene, head = slot_of(view)
+        val, d_head = turned[scene]
+        out_ref[view, :HD] = val[head * HD : (head + 1) * HD]
+        out_ref[view, HD:] = d_head[head * HD : (head + 1) * HD]
+
+
+def attend_kernel(reach, pos_ref, bias_ref, qk_ref, vd_ref, *rest):
+    outs, (k_row, v_row, k_col, v_col, dk_acc, dv_acc, s_buf, p_buf, d_buf, att_buf, dq_buf) = rest[:QUAD], rest[QUAD:]
+    cameras = qk_ref.shape[0]
+    span = 2 * reach + 2
+    two = 2 * LANE
+    for place in range(cameras + 2 * reach):
+        cam = (place - reach) % cameras
+        rows = pl.ds(place * LANE, LANE)
+        key, val = qk_ref[cam, HD:], vd_ref[cam, :HD]
+        k_col[:, rows] = key
+        v_col[:, rows] = val
+        k_row[rows, :] = key.T
+        v_row[rows, :] = val.T
+    dk_acc[...] = jnp.zeros_like(dk_acc)
+    dv_acc[...] = jnp.zeros_like(dv_acc)
+
+    def step(i, carry):
+        base = pl.multiple_of(i * two, two)
+        q_col = jnp.concatenate([qk_ref[2 * i, :HD], qk_ref[2 * i + 1, :HD]], axis=1)
+        d_col = jnp.concatenate([vd_ref[2 * i, HD:], vd_ref[2 * i + 1, HD:]], axis=1)
+        q_rows, d_rows = q_col.T, d_col.T
+        bias = bias_ref[i]
+
+        def at(j):
+            return pl.ds(pl.multiple_of(base + j * LANE, LANE), LANE)
+
+        top = None
+        for j in range(span):
+            score = mul(k_row[at(j), :], q_col)
+            s_buf[j] = score
+            peak = jnp.max(score, axis=0, keepdims=True) + bias[j : j + 1]
+            top = peak if top is None else jnp.maximum(top, peak)
+        total = jnp.zeros((8, two), F32)
+        for j in range(span):
+            prob = jnp.exp(s_buf[j] + (bias[j : j + 1] - top))
+            s_buf[j] = prob
+            total = total + jnp.sum(prob.reshape(LANE // 8, 8, two), axis=0)
+        inv = 1.0 / jnp.sum(total, axis=0, keepdims=True)
+        for j in range(span):
+            prob = s_buf[j] * inv
+            s_buf[j] = prob
+            low = prob.astype(BF)
+            p_buf[j * LANE : (j + 1) * LANE] = low
+            dv_acc[at(j), :] += mul(low, d_rows)
+        window = pl.ds(base, span * LANE)
+        att = mul(v_col[:, window], p_buf[...]).astype(BF)
+        delta = jnp.sum(att.astype(F32) * d_col.astype(F32), axis=0, keepdims=True)
+        for j in range(span):
+            d_score = (s_buf[j] * (mul(v_row[at(j), :], d_col) - delta)).astype(BF)
+            d_buf[j * LANE : (j + 1) * LANE] = d_score
+            dk_acc[at(j), :] += mul(d_score, q_rows)
+        dq = (mul(k_col[:, window], d_buf[...]) * HD**-0.5).astype(BF)
+        for t in range(2):
+            att_buf[2 * i + t] = att[:, t * LANE : (t + 1) * LANE]
+            dq_buf[2 * i + t] = dq[:, t * LANE : (t + 1) * LANE]
+        return carry
+
+    lax.fori_loop(0, cameras // 2, step, 0)
+    for acc in (dk_acc, dv_acc):
+        acc[cameras * LANE : (cameras + reach) * LANE] += acc[: reach * LANE]
+        acc[reach * LANE : 2 * reach * LANE] += acc[(cameras + reach) * LANE :]
+    quad = pos_ref[1]
+    for k in range(QUAD):
+        for plane in range(cameras // QUAD):
+            cam = plane * QUAD + (quad ^ k)
+            rows = pl.ds(pl.multiple_of((cam + reach) * LANE, LANE), LANE)
+            outs[k][plane, :HD] = att_buf[cam]
+            outs[k][plane, HD : 2 * HD] = dq_buf[cam]
+            outs[k][plane, 2 * HD : 3 * HD] = dk_acc[rows, :].T.astype(BF)
+            outs[k][plane, 3 * HD :] = dv_acc[rows, :].T.astype(BF)
+
+
+def weights_kernel(planes, pos_ref, *refs):
+    blocks, own, other = refs[:QUAD], refs[QUAD : QUAD + planes], refs[QUAD + planes : QUAD + 2 * planes]
+    outs = refs[QUAD + 2 * planes : 2 * QUAD + 2 * planes]
+    buf, left, left_o, tok, d_o, wide = refs[2 * QUAD + 2 * planes :]
+    plane, quad, core = pos_ref[0], pos_ref[1], pos_ref[2]
+    for k in range(QUAD):
+        buf[quad ^ k] = blocks[k][...]
+    for k in range(planes):
+        cam = lax.rem(plane - k + planes, planes)
+        for order, (ref, scene) in enumerate(((own[k], core), (other[k], 1 - core))):
+            at = (2 * k + order) * LANE
+            tok[at : at + LANE] = ref[:LANE]
+            d_o[at : at + LANE] = ref[LANE:]
+            for half in range(2):
+                block = buf[2 * scene + half, cam]
+                left_o[half * HD : (half + 1) * HD, at : at + LANE] = block[:HD]
+                for j in range(3):
+                    row = (2 * j + half) * HD
+                    left[row : row + HD, at : at + LANE] = block[(j + 1) * HD : (j + 2) * HD]
+    wide[:, : 6 * HD] = mul(left[...], tok[...]).T
+    wide[:, 6 * HD :] = mul(left_o[...], d_o[...]).T
+    part = wide.shape[0] // (QUAD * planes)
+    for k in range(QUAD):
+        for p in range(planes):
+            rows = pl.ds(pl.multiple_of((p * QUAD + (quad ^ k)) * part, part), part)
+            outs[k][p * part : (p + 1) * part] = wide[rows, :].astype(BF)
+
+
+def sum_kernel(planes, pos_ref, *refs):
+    terms, outs, total = refs[:QUAD], refs[QUAD : QUAD + planes], refs[QUAD + planes]
+    plane = pos_ref[0]
+    acc = terms[0][...].astype(F32)
+    for term in terms[1:]:
+        acc = acc + term[...].astype(F32)
+    total[...] = acc
+    part = total.shape[0] // planes
+    for k in range(planes):
+        rows = pl.ds(pl.multiple_of((plane ^ k) * part, part), part)
+        outs[k][...] = total[rows, :].astype(BF)
+
+
+def finish_kernel(planes, pos_ref, *refs):
+    terms, (w_ref, o_ref), buf = refs[:planes], refs[planes : planes + 2], refs[planes + 2]
+    plane = pos_ref[0]
+    for k in range(planes):
+        buf[plane ^ k] = terms[k][...].astype(F32)
+    two = 2 * HD
+    for p in range(planes):
+        for j in range(3):
+            w_ref[j, :, p * two : (p + 1) * two] = buf[p, :, j * two : (j + 1) * two]
+        o_ref[p * two : (p + 1) * two, :] = buf[p, :, 3 * two :].T
+
+
+def inputs_kernel(planes, pos_ref, *refs):
+    blocks, w_ref, (mine, theirs), (buf, turned) = refs[:planes], refs[planes], refs[planes + 1 : planes + 3], refs[planes + 3 :]
+    plane, core = pos_ref[0], pos_ref[2]
+    for k in range(planes):
+        buf[plane ^ k] = blocks[k][...]
+    width = w_ref.shape[2]
+    for scene in range(2):
+        for j in range(3):
+            for p in range(planes):
+                for half in range(2):
+                    row = (2 * p + half) * HD
+                    turned[scene, j, row : row + HD] = buf[p, 2 * scene + half, j * HD : (j + 1) * HD]
+    left = [
+        jnp.concatenate([turned[scene, j].T for scene in range(2)], axis=0) for j in range(3)
+    ]
+    half = w_ref.shape[1] // 2
+    for ref, who in ((theirs, 1 - core), (mine, core)):
+        rows = pl.ds(pl.multiple_of(who * half, half), half)
+        acc = mul_nt(left[0], w_ref[0, rows, :])
+        for j in range(1, 3):
+            acc = acc + mul_nt(left[j], w_ref[j, rows, :])
+        ref[...] = acc
+
+
+def split_body(tokens, queries, keys, values, w_qkv, w_out, d_out, neighbours, degrees):
+    cameras = neighbours.shape[0]
+    reach = neighbours.shape[1] // 2
+    planes = cameras // QUAD
+    scenes, _, rows, width = queries.shape
+    model = tokens.shape[3]
+    view, core = lax.axis_index("view"), lax.axis_index("head")
+    plane, quad = view // QUAD, view % QUAD
+    pos = jnp.stack([plane, quad, core]).astype(jnp.int32)
+    smem = [pl.BlockSpec(memory_space=pltpu.SMEM)]
+
+    def shape(*dims, dtype=BF):
+        return jax.ShapeDtypeStruct(dims, dtype)
+
+    def along(value, pairs):
+        return lax.ppermute(value, "view", pairs)
+
+    every = range(cameras)
+
+    def quad_swap(value, k):
+        return along(value, [(i, i ^ k) for i in every])
+
+    def plane_swap(value, k):
+        return along(value, [(i, i ^ (k * QUAD)) for i in every])
+
+    def other_core(value):
+        return lax.ppermute(value, "head", [(0, 1), (1, 0)])
+
+    qk = pl.pallas_call(
+        pack_qk_kernel,
+        out_shape=shape(cameras, 2 * HD, rows),
+        in_specs=vmem(2),
+        out_specs=vmem(1)[0],
+        compiler_params=params(16),
+        name="pack_qk",
+    )(queries, keys)
+    qk = lax.all_to_all(qk, "view", 0, 0, tiled=True)
+    vd = pl.pallas_call(
+        pack_vd_kernel,
+        out_shape=shape(cameras, 2 * HD, rows),
+        in_specs=vmem(3),
+        out_specs=vmem(1)[0],
+        compiler_params=params(16),
+        name="pack_vd",
+    )(values, d_out, w_out)
+    vd = lax.all_to_all(vd, "view", 0, 0, tiled=True)
+
+    pair = jnp.concatenate(
+        [lax.dynamic_index_in_dim(arr, core, 0, keepdims=False)[0] for arr in (tokens, d_out)], axis=0
+    )
+    own = [pair]
+    for k in range(1, planes):
+        own.append(along(own[-1], [(i, (i + QUAD) % cameras) for i in every]))
+    other = [other_core(value) for value in own]
+
+    span = 2 * reach + 2
+    offset = jnp.arange(span)[None, :, None] - reach - jnp.arange(2)[None, None, :]
+    query = (2 * jnp.arange(cameras // 2))[:, None, None] + jnp.arange(2)[None, None, :]
+    target = (query + offset) % cameras
+    listed = neighbours.reshape(cameras // 2, 1, 2, 2 * reach)
+    count = degrees.reshape(cameras // 2, 1, 2, 1)
+    live = jnp.arange(2 * reach)[None, None, None, :] < count
+    hit = jnp.any((listed == target[..., None]) & live, axis=3) & (jnp.abs(offset) <= reach)
+    bias = jnp.where(hit | (offset == 0), 0.0, OFF).astype(F32)
+    bias = jnp.repeat(bias, rows, axis=2)
+
+    ext = (cameras + 2 * reach) * rows
+    blocks = pl.pallas_call(
+        functools.partial(attend_kernel, reach),
+        out_shape=[shape(planes, 4 * HD, rows)] * QUAD,
+        in_specs=smem + vmem(3),
+        out_specs=vmem(QUAD),
+        scratch_shapes=[
+            pltpu.VMEM((ext, HD), BF),
+            pltpu.VMEM((ext, HD), BF),
+            pltpu.VMEM((HD, ext), BF),
+            pltpu.VMEM((HD, ext), BF),
+            pltpu.VMEM((ext, HD), F32),
+            pltpu.VMEM((ext, HD), F32),
+            pltpu.VMEM((span, rows, 2 * rows), F32),
+            pltpu.VMEM((span * rows, 2 * rows), BF),
+            pltpu.VMEM((span * rows, 2 * rows), BF),
+            pltpu.VMEM((cameras, HD, rows), BF),
+            pltpu.VMEM((cameras, HD, rows), BF),
+        ],
+        compiler_params=params(32),
+        name="attend",
+    )(pos, bias, qk, vd)
+    blocks = [blocks[0]] + [quad_swap(blocks[k], k) for k in range(1, QUAD)]
+
+    terms = pl.pallas_call(
+        functools.partial(weights_kernel, planes),
+        out_shape=[shape(model // QUAD, 8 * HD)] * QUAD,
+        in_specs=smem + vmem(QUAD + 2 * planes),
+        out_specs=vmem(QUAD),
+        scratch_shapes=[
+            pltpu.VMEM((QUAD, planes, 4 * HD, rows), BF),
+            pltpu.VMEM((6 * HD, 2 * planes * rows), BF),
+            pltpu.VMEM((2 * HD, 2 * planes * rows), BF),
+            pltpu.VMEM((2 * planes * rows, model), BF),
+            pltpu.VMEM((2 * planes * rows, model), BF),
+            pltpu.VMEM((model, 8 * HD), F32),
+        ],
+        compiler_params=params(32),
+        name="weights",
+    )(pos, *blocks, *own, *other)
+    terms = [terms[0]] + [quad_swap(terms[k], k) for k in range(1, QUAD)]
+    terms = pl.pallas_call(
+        functools.partial(sum_kernel, planes),
+        out_shape=[shape(model // cameras, 8 * HD)] * planes,
+        in_specs=smem + vmem(QUAD),
+        out_specs=vmem(planes),
+        scratch_shapes=[pltpu.VMEM((model // QUAD, 8 * HD), F32)],
+        compiler_params=params(16),
+        name="plane_sum",
+    )(pos, *terms)
+    terms = [terms[0]] + [plane_swap(terms[k], k) for k in range(1, planes)]
+    d_wqkv, d_wo = pl.pallas_call(
+        functools.partial(finish_kernel, planes),
+        out_shape=[shape(3, model // cameras, width, dtype=F32), shape(width, model // cameras, dtype=F32)],
+        in_specs=smem + vmem(planes),
+        out_specs=vmem(2),
+        scratch_shapes=[pltpu.VMEM((planes, model // cameras, 8 * HD), F32)],
+        compiler_params=params(16),
+        name="finish",
+    )(pos, *terms)
+
+    stacked = jnp.stack([blocks[k] for k in range(QUAD)])
+    order = quad ^ jnp.arange(QUAD)
+    stacked = stacked[order][:, :, HD:]
+    grads = []
+    for k in range(planes):
+        block = lax.dynamic_index_in_dim(stacked, plane ^ k, 1, keepdims=False)
+        grads.append(block if k == 0 else plane_swap(block, k))
+    mine, theirs = pl.pallas_call(
+        functools.partial(inputs_kernel, planes),
+        out_shape=[shape(scenes * rows, model // 2, dtype=F32)] * 2,
+        in_specs=smem + vmem(planes + 1),
+        out_specs=vmem(2),
+        scratch_shapes=[
+            pltpu.VMEM((planes, QUAD, 3 * HD, rows), BF),
+            pltpu.VMEM((scenes, 3, width, rows), BF),
+        ],
+        compiler_params=params(32),
+        name="inputs",
+    )(pos, *grads, w_qkv)
+    d_tokens = (mine + other_core(theirs)).astype(BF).reshape(scenes, 1, rows, model // 2)
+    return (d_tokens, d_wqkv, d_wo)
 
 
 def shifted(value, axis, steps):
@@ -12,7 +371,7 @@
     return lax.ppermute(value, axis, pairs)
 
 
-def body(tokens, queries, keys, values, w_qkv, w_out, d_out, neighbours, degrees):
+def halo_body(tokens, queries, keys, values, w_qkv, w_out, d_out, neighbours, degrees):
     cameras = neighbours.shape[0]
     reach = neighbours.shape[1] // 2
     offsets = [step for step in range(-reach, reach + 1) if step != 0]
@@ -133,6 +492,21 @@
     return (d_tokens, d_wqkv, d_wo)
 
 
+def body(tokens, queries, keys, values, w_qkv, w_out, d_out, neighbours, degrees):
+    args = (tokens, queries, keys, values, w_qkv, w_out, d_out, neighbours, degrees)
+    scenes, _, rows, width = queries.shape
+    cameras, reach = neighbours.shape[0], neighbours.shape[1] // 2
+    fits = (
+        scenes == 2
+        and lax.axis_size("head") == 2
+        and scenes * (width // HD) == cameras == lax.axis_size("view")
+        and rows == LANE
+        and cameras == QUAD * QUAD
+        and cameras >= 2 * reach + 2
+    )
+    return split_body(*args) if fits else halo_body(*args)
+
+
 def solution(mesh):
     return jax.shard_map(
         body,

time: 586 us -> 156 us (0.27)
  waiting for transfers between devices: 314 us -> 79.9 us
  matrix products: 88.5 us -> 0 us
  starting transfers between devices: 87.8 us -> 35.6 us
  local copies, waits for them, and re-layouts: 53.7 us -> 10.8 us
  Pallas kernels: 0 us -> 25.6 us
  between operations: 22.2 us -> 0.98 us
  other arithmetic: 17.3 us -> 2.42 us
    unnamed x4 -> x0, waiting for transfers between devices: 262 us -> none
    dot_general x58 -> x0, matrix products: 88.5 us -> none  [the longest x9 21.7 us: body(): jnp.einsum('shtu,suhd->sthd', prob_low, value_blk, preferred_element_type...]
    ppermute x32 -> x20, starting transfers between devices: 87.7 us -> 23.6 us  [the longest x15 22.5 us: along(): return lax.ppermute(value, 'view', pairs)]
    all_to_all x0 -> x2, waiting for transfers between devices: none -> 43.7 us  [the longest x1 22.2 us: split_body(): vd = lax.all_to_all(vd, 'view', 0, 0, tiled=True)]
    ppermute x16 -> x0, local copies, waits for them, and re-layouts: 28.7 us -> none  [shifted(): return lax.ppermute(value, axis, pairs)]
    pallas_call x0 -> x7, Pallas kernels: none -> 25.6 us  [the longest x1 16.5 us: split_body(): pl.pallas_call(functools.partial(attend_kernel, reach), out_shape=[shape(...]
    ppermute x32 -> x20, waiting for transfers between devices: 52.1 us -> 36.2 us  [the longest x15 36.2 us: along(): return lax.ppermute(value, 'view', pairs)]
    all_to_all x0 -> x2, starting transfers between devices: none -> 12 us  [the longest x1 8.44 us: split_body(): qk = lax.all_to_all(qk, 'view', 0, 0, tiled=True)]
  transfers between devices with their start and end apart: 35 -> 22, of which waited for: 7 -> 11; matrix products, arithmetic and copies ran while one was open for 23% -> 5% of each run, Pallas kernels for 0% -> 15%
where the time goes in v1:
time: 156 us; the launch traced here: 155 us
  waiting for transfers between devices  79.9 us (51%)
  starting transfers between devices  35.6 us (23%)
  Pallas kernels  25.6 us (16%)
  local copies, waits for them, and re-layouts  10.8 us (7%)
  other arithmetic  2.42 us (2%)
    ppermute x15, waiting for transfers between devices, along(): return lax.ppermute(value, 'view', pairs)  36.2 us
    ppermute x15, starting transfers between devices, along(): return lax.ppermute(value, 'view', pairs)  22.5 us
    all_to_all x1, waiting for transfers between devices, split_body(): vd = lax.all_to_all(vd, 'view', 0, 0, tiled=True)  22.2 us
    all_to_all x1, waiting for transfers between devices, split_body(): qk = lax.all_to_all(qk, 'view', 0, 0, tiled=True)  21.5 us
    pallas_call x1, Pallas kernels, split_body(): pl.pallas_call(functools.partial(attend_kernel, reach), out_shape=[shape(...  16.5 us
    all_to_all x1, starting transfers between devices, split_body(): qk = lax.all_to_all(qk, 'view', 0, 0, tiled=True)  8.44 us
    unnamed x38, local copies, waits for them, and re-layouts  5.05 us
    all_to_all x1, starting transfers between devices, split_body(): vd = lax.all_to_all(vd, 'view', 0, 0, tiled=True)  3.57 us
  transfers between devices with their start and end apart: 22, of which 11 were waited for; matrix products, arithmetic and copies ran while one was open for 5% of the time, Pallas kernels for 15%

profile of v1, /device:TPU:0, one launch (start us, length us, event | category | flops | bytes accessed | tf_op | source)
XLA Modules:
  0.0 155.3 jit_solution(3225687741349421042)
XLA Ops:
  0.7 1.1 copy-done.14
  2.7 1.0 pack_qk.1
  3.7 8.4 %all-to-all-start = ((bf16[16,128,128]{2,1,0:T(8,128)(2,1)}), bf16[16,128,128]{2,1,0:T(8,128)(2,1)S(1)}, u32[]{:S(2)}, u32[]{:S(2)}) async-start(bf16[16,128,128]{2,1,0:T(8,128)(2,1)} %pack_qk.1), calls=%async_computation | async-start | bytes 1048576 | tf_op jit(solution)/shard_map/all_to_all | solution.py:254
  12.2 1.1 dynamic-slice_bitcast_fusion
  13.3 2.0 %collective-permute-start.7 = (bf16[256,1024]{1,0:T(8,128)(2,1)S(1)}, bf16[256,1024]{1,0:T(8,128)(2,1)S(1)}, u32[]{:S(2)}, u32[]{:S(2)}) collective-permute-start(bf16[256,1024]{1,0:T(8,128)(2,1)S(1)} %pad_maximum_fusion.1.refs_4_), channel_id=1, source_target_pairs={{0,8},{2,10},{4,12},{6,14},{8,16},{10,18},{12,20},{14,22},{16,24},... | collective-permute-start | bytes 1572872 | tf_op jit(solution)/shard_map/ppermute | solution.py:233
  15.4 1.5 pack_vd.1
  17.1 21.5 %all-to-all-done.qk_ref = bf16[16,128,128]{2,1,0:T(8,128)(2,1)S(1)} async-done(((bf16[16,128,128]{2,1,0:T(8,128)(2,1)}), bf16[16,128,128]{2,1,0:T(8,128)(2,1)S(1)}, u32[]{:S(2)}, u32[]{:S(2)}) %all-to-all-start) | async-done | bytes 524320 | tf_op jit(solution)/shard_map/all_to_all | solution.py:254
  38.5 3.6 %all-to-all-start.1 = ((bf16[16,128,128]{2,1,0:T(8,128)(2,1)}), bf16[16,128,128]{2,1,0:T(8,128)(2,1)S(1)}, u32[]{:S(2)}, u32[]{:S(2)}) async-start(bf16[16,128,128]{2,1,0:T(8,128)(2,1)} %pack_vd.1), calls=%async_computation.1 | async-start | bytes 1048576 | tf_op jit(solution)/shard_map/all_to_all | solution.py:263
  42.4 1.9 %collective-permute-start.8 = (bf16[256,1024]{1,0:T(8,128)(2,1)S(1)}, bf16[256,1024]{1,0:T(8,128)(2,1)}, u32[]{:S(2)}, u32[]{:S(2)}) collective-permute-start(bf16[256,1024]{1,0:T(8,128)(2,1)S(1)} %collective-permute-done.7.refs_5_), channel_id=1, source_target_pairs={{0,8},{2,10},{4,12},{6,14},{8,16},{10,18},{12,20},{14,22},{16,24},... | collective-permute-start | bytes 1572872 | tf_op jit(solution)/shard_map/ppermute | solution.py:233
  44.7 22.2 %all-to-all-done.1.vd_ref = bf16[16,128,128]{2,1,0:T(8,128)(2,1)S(1)} async-done(((bf16[16,128,128]{2,1,0:T(8,128)(2,1)}), bf16[16,128,128]{2,1,0:T(8,128)(2,1)S(1)}, u32[]{:S(2)}, u32[]{:S(2)}) %all-to-all-start.1) | async-done | bytes 524320 | tf_op jit(solution)/shard_map/all_to_all | solution.py:263
  66.9 16.5 %attend.1 = (bf16[4,256,128]{2,1,0:T(8,128)(2,1)S(1)}, bf16[4,256,128]{2,1,0:T(8,128)(2,1)S(1)}, bf16[4,256,128]{2,1,0:T(8,128)(2,1)S(1)}, bf16[4,256,128]{2,1,0:T(8,128)(2,1)S(1)}) custom-call(s32[3]{0:T(128)S(1)} %pad_add_fusion.pos_ref, f32[8,10,256]{2,1,0:T(8,128)S(1)} %copy.21.bias_ref, bf16[16,128,128]{2,1,0:T(8,128)(2,1)S(1)} %all-to-all-done.qk_ref, ...), custom_call_target="tpu_custom_call" | custom-call | tf_op jit(solution)/shard_map/attend/pallas_call | solution.py:285
  85.0 2.0 %collective-permute-start.2 = (bf16[4,256,128]{2,1,0:T(8,128)(2,1)S(1)}, bf16[4,256,128]{2,1,0:T(8,128)(2,1)S(1)}, u32[]{:S(2)}, u32[]{:S(2)}) collective-permute-start(bf16[4,256,128]{2,1,0:T(8,128)(2,1)S(1)} %get-tuple-element.22), channel_id=1, source_target_pairs={{0,6},{2,4},{4,2},{6,0},{8,14},{10,12},{12,10},{14,8},{16,22},{18,... | collective-permute-start | bytes 786440 | tf_op jit(solution)/shard_map/ppermute | solution.py:233
  87.0 1.3 collective-permute-start.9
  88.3 1.6 %collective-permute-done.refs_1_ = bf16[4,256,128]{2,1,0:T(8,128)(2,1)S(1)} collective-permute-done((bf16[4,256,128]{2,1,0:T(8,128)(2,1)S(1)}, bf16[4,256,128]{2,1,0:T(8,128)(2,1)S(1)}, u32[]{:S(2)}, u32[]{:S(2)}) %collective-permute-start) | collective-permute-done | bytes 262176 | tf_op jit(solution)/shard_map/ppermute | solution.py:233
  89.9 3.4 %collective-permute-done.1.refs_2_ = bf16[4,256,128]{2,1,0:T(8,128)(2,1)S(1)} collective-permute-done((bf16[4,256,128]{2,1,0:T(8,128)(2,1)S(1)}, bf16[4,256,128]{2,1,0:T(8,128)(2,1)S(1)}, u32[]{:S(2)}, u32[]{:S(2)}) %collective-permute-start.1) | collective-permute-done | bytes 262176 | tf_op jit(solution)/shard_map/ppermute | solution.py:233
  93.2 1.1 pad_maximum_fusion
  96.5 3.0 %gather_fusion = bf16[4,4,256,128]{3,2,1,0:T(8,128)(2,1)} fusion(bf16[4,4,256,128]{3,2,1,0:T(8,128)(2,1)} %pad_maximum_fusion, s32[1024]{0:T(1024)S(1)} %pad_clamp_fusion), kind=kCustom, calls=%fused_computation | custom fusion | bytes 2097168 | tf_op jit(solution)/shard_map/gather | solution.py:347
  99.6 1.3 slice.6
  101.0 4.0 %collective-permute-start.3 = (bf16[4,192,128]{2,1,0:T(8,128)(2,1)S(1)}, bf16[4,192,128]{2,1,0:T(8,128)(2,1)S(1)}, u32[]{:S(2)}, u32[]{:S(2)}) collective-permute-start(bf16[4,192,128]{2,1,0:T(8,128)(2,1)S(1)} %get-tuple-element.46), channel_id=1, source_target_pairs={{0,8},{2,10},{4,12},{6,14},{8,0},{10,2},{12,4},{14,6},{16,24},{18,... | collective-permute-start | bytes 589832 | tf_op jit(solution)/shard_map/ppermute | solution.py:233
  105.5 4.1 %collective-permute-done.3.refs_1_ = bf16[4,192,128]{2,1,0:T(8,128)(2,1)S(1)} collective-permute-done((bf16[4,192,128]{2,1,0:T(8,128)(2,1)S(1)}, bf16[4,192,128]{2,1,0:T(8,128)(2,1)S(1)}, u32[]{:S(2)}, u32[]{:S(2)}) %collective-permute-start.3) | collective-permute-done | bytes 196640 | tf_op jit(solution)/shard_map/ppermute | solution.py:233
  110.1 3.7 %collective-permute-done.4.refs_2_ = bf16[4,192,128]{2,1,0:T(8,128)(2,1)S(1)} collective-permute-done((bf16[4,192,128]{2,1,0:T(8,128)(2,1)S(1)}, bf16[4,192,128]{2,1,0:T(8,128)(2,1)S(1)}, u32[]{:S(2)}, u32[]{:S(2)}) %collective-permute-start.4) | collective-permute-done | bytes 196640 | tf_op jit(solution)/shard_map/ppermute | solution.py:233
  113.9 7.5 %collective-permute-done.5.refs_3_ = bf16[4,192,128]{2,1,0:T(8,128)(2,1)S(1)} collective-permute-done((bf16[4,192,128]{2,1,0:T(8,128)(2,1)S(1)}, bf16[4,192,128]{2,1,0:T(8,128)(2,1)S(1)}, u32[]{:S(2)}, u32[]{:S(2)}) %collective-permute-start.5) | collective-permute-done | bytes 196640 | tf_op jit(solution)/shard_map/ppermute | solution.py:233
  121.4 1.6 %inputs.1 = (f32[256,512]{1,0:T(8,128)S(1)}, f32[256,512]{1,0:T(8,128)S(1)}) custom-call(s32[3]{0:T(128)S(1)} %pad_add_fusion.pos_ref, bf16[4,192,128]{2,1,0:T(8,128)(2,1)S(1)} %get-tuple-element.47.refs_0_, bf16[4,192,128]{2,1,0:T(8,128)(2,1)S(1)} %collective-permute-done.3.refs_1_, bf16[4,192,128]{2,1,0:T(8,128)(2,1)S(1)} %collective-permute-done.4.refs_2_, ...), custom_call_target="tpu_custom_call" | custom-call | tf_op jit(solution)/shard_map/inputs/pallas_call | solution.py:352
  123.2 2.8 %weights.1 = (bf16[256,512]{1,0:T(8,128)(2,1)S(1)}, bf16[256,512]{1,0:T(8,128)(2,1)S(1)}, bf16[256,512]{1,0:T(8,128)(2,1)S(1)}, bf16[256,512]{1,0:T(8,128)(2,1)S(1)}) custom-call(s32[3]{0:T(128)S(1)} %pad_add_fusion.pos_ref, bf16[4,256,128]{2,1,0:T(8,128)(2,1)S(1)} %get-tuple-element.19.refs_0_, bf16[4,256,128]{2,1,0:T(8,128)(2,1)S(1)} %copy-done.6, ...), custom_call_target="tpu_custom_call" | custom-call | tf_op jit(solution)/shard_map/weights/pallas_call | solution.py:308
  126.8 4.0 %collective-permute-start.15 = (bf16[256,512]{1,0:T(8,128)(2,1)S(1)}, bf16[256,512]{1,0:T(8,128)(2,1)S(1)}, u32[]{:S(2)}, u32[]{:S(2)}) collective-permute-start(bf16[256,512]{1,0:T(8,128)(2,1)S(1)} %get-tuple-element.27), channel_id=1, source_target_pairs={{0,4},{2,6},{4,0},{6,2},{8,12},{10,14},{12,8},{14,10},{16,20},{18,... | collective-permute-start | bytes 786440 | tf_op jit(solution)/shard_map/ppermute | solution.py:233
  131.3 3.8 %collective-permute-done.14.refs_1_ = bf16[256,512]{1,0:T(8,128)(2,1)S(1)} collective-permute-done((bf16[256,512]{1,0:T(8,128)(2,1)S(1)}, bf16[256,512]{1,0:T(8,128)(2,1)S(1)}, u32[]{:S(2)}, u32[]{:S(2)}) %collective-permute-start.14) | collective-permute-done | bytes 262176 | tf_op jit(solution)/shard_map/ppermute | solution.py:233
  135.1 7.2 %collective-permute-done.15.refs_2_ = bf16[256,512]{1,0:T(8,128)(2,1)S(1)} collective-permute-done((bf16[256,512]{1,0:T(8,128)(2,1)S(1)}, bf16[256,512]{1,0:T(8,128)(2,1)S(1)}, u32[]{:S(2)}, u32[]{:S(2)}) %collective-permute-start.15) | collective-permute-done | bytes 262176 | tf_op jit(solution)/shard_map/ppermute | solution.py:233
  142.3 1.3 collective-permute-done.16.refs_3_
  145.1 1.3 collective-permute-start.18
  146.3 2.5 %collective-permute-start.19 = (bf16[64,512]{1,0:T(8,128)(2,1)S(1)}, bf16[64,512]{1,0:T(8,128)(2,1)S(1)}, u32[]{:S(2)}, u32[]{:S(2)}) collective-permute-start(bf16[64,512]{1,0:T(8,128)(2,1)S(1)} %get-tuple-element.32), channel_id=1, source_target_pairs={{0,24},{2,26},{4,28},{6,30},{8,16},{10,18},{12,20},{14,22},{16,8},... | collective-permute-start | bytes 196616 | tf_op jit(solution)/shard_map/ppermute | solution.py:233
  149.6 3.5 %collective-permute-done.18.refs_2_ = bf16[64,512]{1,0:T(8,128)(2,1)S(1)} collective-permute-done((bf16[64,512]{1,0:T(8,128)(2,1)S(1)}, bf16[64,512]{1,0:T(8,128)(2,1)S(1)}, u32[]{:S(2)}, u32[]{:S(2)}) %collective-permute-start.18) | collective-permute-done | bytes 65568 | tf_op jit(solution)/shard_map/ppermute | solution.py:233
  153.1 1.4 finish.1
  (80 shorter events, 11.1 us)
Async XLA Ops:
  0.6 14.7 %copy-start.3 = (bf16[2,1,128,1024]{3,2,1,0:T(8,128)(2,1)S(1)}, bf16[2,1,128,1024]{3,2,1,0:T(8,128)(2,1)}, u32[]{:S(2)}) copy-start(bf16[2,1,128,1024]{3,2,1,0:T(8,128)(2,1)} %d_ref.1) | copy-start | bytes 1572868
  0.6 14.7 %copy-start.13 = (bf16[2,1,128,512]{3,2,1,0:T(8,128)(2,1)S(1)}, bf16[2,1,128,512]{3,2,1,0:T(8,128)(2,1)}, u32[]{:S(2)}) copy-start(bf16[2,1,128,512]{3,2,1,0:T(8,128)(2,1)} %v_ref.1) | copy-start | bytes 786436
  0.7 14.7 %copy-start.4 = (bf16[512,1024]{1,0:T(8,128)(2,1)S(1)}, bf16[512,1024]{1,0:T(8,128)(2,1)}, u32[]{:S(2)}) copy-start(bf16[512,1024]{1,0:T(8,128)(2,1)} %w_ref.1) | copy-start | bytes 3145732
  3.7 38.5 %copy-start.16 = (s32[16,8]{0,1:T(8,128)S(1)}, s32[16,8]{0,1:T(8,128)}, u32[]{:S(2)}) copy-start(s32[16,8]{0,1:T(8,128)} %param.16) | copy-start | bytes 1540
  3.7 34.8 %all-to-all-start = ((bf16[16,128,128]{2,1,0:T(8,128)(2,1)}), bf16[16,128,128]{2,1,0:T(8,128)(2,1)S(1)}, u32[]{:S(2)}, u32[]{:S(2)}) async-start(bf16[16,128,128]{2,1,0:T(8,128)(2,1)} %pack_qk.1), calls=%async_computation | async-start | bytes 1048576 | tf_op jit(solution)/shard_map/all_to_all | solution.py:254
  13.3 80.0 %copy-start.1 = (bf16[256,1024]{1,0:T(8,128)(2,1)}, bf16[256,1024]{1,0:T(8,128)(2,1)S(1)}, u32[]{:S(2)}) copy-start(bf16[256,1024]{1,0:T(8,128)(2,1)S(1)} %pad_maximum_fusion.1.refs_4_) | copy-start | bytes 1572868
  13.3 29.1 %collective-permute-start.7 = (bf16[256,1024]{1,0:T(8,128)(2,1)S(1)}, bf16[256,1024]{1,0:T(8,128)(2,1)S(1)}, u32[]{:S(2)}, u32[]{:S(2)}) collective-permute-start(bf16[256,1024]{1,0:T(8,128)(2,1)S(1)} %pad_maximum_fusion.1.refs_4_), channel_id=1, source_target_pairs={{0,8},{2,10},{4,12},{6,14},{8,16},{10,18},{12,20},{14,22},{16,24},... | collective-permute-start | bytes 1572872 | tf_op jit(solution)/shard_map/ppermute | solution.py:233
  38.5 28.3 %all-to-all-start.1 = ((bf16[16,128,128]{2,1,0:T(8,128)(2,1)}), bf16[16,128,128]{2,1,0:T(8,128)(2,1)S(1)}, u32[]{:S(2)}, u32[]{:S(2)}) async-start(bf16[16,128,128]{2,1,0:T(8,128)(2,1)} %pack_vd.1), calls=%async_computation.1 | async-start | bytes 1048576 | tf_op jit(solution)/shard_map/all_to_all | solution.py:263
  42.4 50.8 %copy-start.11 = (bf16[256,1024]{1,0:T(8,128)(2,1)}, bf16[256,1024]{1,0:T(8,128)(2,1)S(1)}, u32[]{:S(2)}) copy-start(bf16[256,1024]{1,0:T(8,128)(2,1)S(1)} %collective-permute-done.7.refs_5_) | copy-start | bytes 1572868
  42.4 44.6 %collective-permute-start.8 = (bf16[256,1024]{1,0:T(8,128)(2,1)S(1)}, bf16[256,1024]{1,0:T(8,128)(2,1)}, u32[]{:S(2)}, u32[]{:S(2)}) collective-permute-start(bf16[256,1024]{1,0:T(8,128)(2,1)S(1)} %collective-permute-done.7.refs_5_), channel_id=1, source_target_pairs={{0,8},{2,10},{4,12},{6,14},{8,16},{10,18},{12,20},{14,22},{16,24},... | collective-permute-start | bytes 1572872 | tf_op jit(solution)/shard_map/ppermute | solution.py:233
  83.4 6.4 %collective-permute-start = (bf16[4,256,128]{2,1,0:T(8,128)(2,1)S(1)}, bf16[4,256,128]{2,1,0:T(8,128)(2,1)S(1)}, u32[]{:S(2)}, u32[]{:S(2)}) collective-permute-start(bf16[4,256,128]{2,1,0:T(8,128)(2,1)S(1)} %get-tuple-element.20), channel_id=1, source_target_pairs={{0,2},{2,0},{4,6},{6,4},{8,10},{10,8},{12,14},{14,12},{16,18},{18,... | collective-permute-start | bytes 786440 | tf_op jit(solution)/shard_map/ppermute | solution.py:233
  84.1 9.2 %collective-permute-start.1 = (bf16[4,256,128]{2,1,0:T(8,128)(2,1)S(1)}, bf16[4,256,128]{2,1,0:T(8,128)(2,1)S(1)}, u32[]{:S(2)}, u32[]{:S(2)}) collective-permute-start(bf16[4,256,128]{2,1,0:T(8,128)(2,1)S(1)} %get-tuple-element.21), channel_id=1, source_target_pairs={{0,4},{2,6},{4,0},{6,2},{8,12},{10,14},{12,8},{14,10},{16,20},{18,... | collective-permute-start | bytes 786440 | tf_op jit(solution)/shard_map/ppermute | solution.py:233
  85.0 8.3 %collective-permute-start.2 = (bf16[4,256,128]{2,1,0:T(8,128)(2,1)S(1)}, bf16[4,256,128]{2,1,0:T(8,128)(2,1)S(1)}, u32[]{:S(2)}, u32[]{:S(2)}) collective-permute-start(bf16[4,256,128]{2,1,0:T(8,128)(2,1)S(1)} %get-tuple-element.22), channel_id=1, source_target_pairs={{0,6},{2,4},{4,2},{6,0},{8,14},{10,12},{12,10},{14,8},{16,22},{18,... | collective-permute-start | bytes 786440 | tf_op jit(solution)/shard_map/ppermute | solution.py:233
  87.0 22.6 %collective-permute-start.9 = (bf16[256,1024]{1,0:T(8,128)(2,1)}, bf16[256,1024]{1,0:T(8,128)(2,1)}, u32[]{:S(2)}, u32[]{:S(2)}) collective-permute-start(bf16[256,1024]{1,0:T(8,128)(2,1)} %collective-permute-done.8.refs_6_), channel_id=1, source_target_pairs={{0,8},{2,10},{4,12},{6,14},{8,16},{10,18},{12,20},{14,22},{16,24},... | collective-permute-start | bytes 1572872 | tf_op jit(solution)/shard_map/ppermute | solution.py:233
  96.5 24.9 %copy-start = (bf16[3,1024,512]{2,1,0:T(8,128)(2,1)S(1)}, bf16[3,1024,512]{2,1,0:T(8,128)(2,1)}, u32[]{:S(2)}) copy-start(bf16[3,1024,512]{2,1,0:T(8,128)(2,1)} %refs_4_.1) | copy-start | bytes 9437188
  100.8 22.3 %copy-start.6 = (bf16[4,256,128]{2,1,0:T(8,128)(2,1)S(1)}, bf16[4,256,128]{2,1,0:T(8,128)(2,1)}, u32[]{:S(2)}) copy-start(bf16[4,256,128]{2,1,0:T(8,128)(2,1)} %copy-done.5) | copy-start | bytes 786436
  100.9 22.3 %copy-start.8 = (bf16[4,256,128]{2,1,0:T(8,128)(2,1)S(1)}, bf16[4,256,128]{2,1,0:T(8,128)(2,1)}, u32[]{:S(2)}) copy-start(bf16[4,256,128]{2,1,0:T(8,128)(2,1)} %copy-done.7) | copy-start | bytes 786436
  100.9 22.3 %copy-start.10 = (bf16[4,256,128]{2,1,0:T(8,128)(2,1)S(1)}, bf16[4,256,128]{2,1,0:T(8,128)(2,1)}, u32[]{:S(2)}) copy-start(bf16[4,256,128]{2,1,0:T(8,128)(2,1)} %copy-done.9) | copy-start | bytes 786436
  101.0 8.7 %collective-permute-start.3 = (bf16[4,192,128]{2,1,0:T(8,128)(2,1)S(1)}, bf16[4,192,128]{2,1,0:T(8,128)(2,1)S(1)}, u32[]{:S(2)}, u32[]{:S(2)}) collective-permute-start(bf16[4,192,128]{2,1,0:T(8,128)(2,1)S(1)} %get-tuple-element.46), channel_id=1, source_target_pairs={{0,8},{2,10},{4,12},{6,14},{8,0},{10,2},{12,4},{14,6},{16,24},{18,... | collective-permute-start | bytes 589832 | tf_op jit(solution)/shard_map/ppermute | solution.py:233
  105.0 8.9 %collective-permute-start.4 = (bf16[4,192,128]{2,1,0:T(8,128)(2,1)S(1)}, bf16[4,192,128]{2,1,0:T(8,128)(2,1)S(1)}, u32[]{:S(2)}, u32[]{:S(2)}) collective-permute-start(bf16[4,192,128]{2,1,0:T(8,128)(2,1)S(1)} %get-tuple-element.45), channel_id=1, source_target_pairs={{0,16},{2,18},{4,20},{6,22},{8,24},{10,26},{12,28},{14,30},{16,0},... | collective-permute-start | bytes 589832 | tf_op jit(solution)/shard_map/ppermute | solution.py:233
  105.0 18.1 %collective-permute-start.10 = (bf16[256,1024]{1,0:T(8,128)(2,1)S(1)}, bf16[256,1024]{1,0:T(8,128)(2,1)S(1)}, u32[]{:S(2)}, u32[]{:S(2)}) collective-permute-start(bf16[256,1024]{1,0:T(8,128)(2,1)S(1)} %copy-done.2), channel_id=1, source_target_pairs={{0,1},{1,0},{2,3},{3,2},{4,5},{5,4},{6,7},{7,6},{8,9},{9,8},{10,11... | collective-permute-start | bytes 1572872 | tf_op jit(solution)/shard_map/ppermute | solution.py:244
  105.0 18.1 %collective-permute-start.11 = (bf16[256,1024]{1,0:T(8,128)(2,1)S(1)}, bf16[256,1024]{1,0:T(8,128)(2,1)S(1)}, u32[]{:S(2)}, u32[]{:S(2)}) collective-permute-start(bf16[256,1024]{1,0:T(8,128)(2,1)S(1)} %copy-done.12), channel_id=1, source_target_pairs={{0,1},{1,0},{2,3},{3,2},{4,5},{5,4},{6,7},{7,6},{8,9},{9,8},{10,11... | collective-permute-start | bytes 1572872 | tf_op jit(solution)/shard_map/ppermute | solution.py:244
  109.6 13.5 %collective-permute-start.12 = (bf16[256,1024]{1,0:T(8,128)(2,1)}, bf16[256,1024]{1,0:T(8,128)(2,1)S(1)}, u32[]{:S(2)}, u32[]{:S(2)}) collective-permute-start(bf16[256,1024]{1,0:T(8,128)(2,1)} %collective-permute-done.8.refs_6_), channel_id=1, source_target_pairs={{0,1},{1,0},{2,3},{3,2},{4,5},{5,4},{6,7},{7,6},{8,9},{9,8},{10,11... | collective-permute-start | bytes 1572872 | tf_op jit(solution)/shard_map/ppermute | solution.py:244
  109.6 13.5 %collective-permute-start.13 = (bf16[256,1024]{1,0:T(8,128)(2,1)}, bf16[256,1024]{1,0:T(8,128)(2,1)S(1)}, u32[]{:S(2)}, u32[]{:S(2)}) collective-permute-start(bf16[256,1024]{1,0:T(8,128)(2,1)} %collective-permute-done.9.refs_7_), channel_id=1, source_target_pairs={{0,1},{1,0},{2,3},{3,2},{4,5},{5,4},{6,7},{7,6},{8,9},{9,8},{10,11... | collective-permute-start | bytes 1572872 | tf_op jit(solution)/shard_map/ppermute | solution.py:244
  113.9 7.5 %collective-permute-start.5 = (bf16[4,192,128]{2,1,0:T(8,128)(2,1)S(1)}, bf16[4,192,128]{2,1,0:T(8,128)(2,1)S(1)}, u32[]{:S(2)}, u32[]{:S(2)}) collective-permute-start(bf16[4,192,128]{2,1,0:T(8,128)(2,1)S(1)} %get-tuple-element.44), channel_id=1, source_target_pairs={{0,24},{2,26},{4,28},{6,30},{8,16},{10,18},{12,20},{14,22},{16,8},... | collective-permute-start | bytes 589832 | tf_op jit(solution)/shard_map/ppermute | solution.py:233
  123.0 25.8 %collective-permute-start.6 = (f32[256,512]{1,0:T(8,128)S(1)}, f32[256,512]{1,0:T(8,128)S(1)}, u32[]{:S(2)}, u32[]{:S(2)}) collective-permute-start(f32[256,512]{1,0:T(8,128)S(1)} %get-tuple-element.24), channel_id=1, source_target_pairs={{0,1},{1,0},{2,3},{3,2},{4,5},{5,4},{6,7},{7,6},{8,9},{9,8},{10,11... | collective-permute-start | bytes 1572872 | tf_op jit(solution)/shard_map/ppermute | solution.py:244
  126.0 9.2 %collective-permute-start.14 = (bf16[256,512]{1,0:T(8,128)(2,1)S(1)}, bf16[256,512]{1,0:T(8,128)(2,1)S(1)}, u32[]{:S(2)}, u32[]{:S(2)}) collective-permute-start(bf16[256,512]{1,0:T(8,128)(2,1)S(1)} %get-tuple-element.26), channel_id=1, source_target_pairs={{0,2},{2,0},{4,6},{6,4},{8,10},{10,8},{12,14},{14,12},{16,18},{18,... | collective-permute-start | bytes 786440 | tf_op jit(solution)/shard_map/ppermute | solution.py:233
  126.8 15.5 %collective-permute-start.15 = (bf16[256,512]{1,0:T(8,128)(2,1)S(1)}, bf16[256,512]{1,0:T(8,128)(2,1)S(1)}, u32[]{:S(2)}, u32[]{:S(2)}) collective-permute-start(bf16[256,512]{1,0:T(8,128)(2,1)S(1)} %get-tuple-element.27), channel_id=1, source_target_pairs={{0,4},{2,6},{4,0},{6,2},{8,12},{10,14},{12,8},{14,10},{16,20},{18,... | collective-permute-start | bytes 786440 | tf_op jit(solution)/shard_map/ppermute | solution.py:233
  130.8 12.8 %collective-permute-start.16 = (bf16[256,512]{1,0:T(8,128)(2,1)S(1)}, bf16[256,512]{1,0:T(8,128)(2,1)S(1)}, u32[]{:S(2)}, u32[]{:S(2)}) collective-permute-start(bf16[256,512]{1,0:T(8,128)(2,1)S(1)} %get-tuple-element.28), channel_id=1, source_target_pairs={{0,6},{2,4},{4,2},{6,0},{8,14},{10,12},{12,10},{14,8},{16,22},{18,... | collective-permute-start | bytes 786440 | tf_op jit(solution)/shard_map/ppermute | solution.py:233
  144.3 5.2 %collective-permute-start.17 = (bf16[64,512]{1,0:T(8,128)(2,1)S(1)}, bf16[64,512]{1,0:T(8,128)(2,1)S(1)}, u32[]{:S(2)}, u32[]{:S(2)}) collective-permute-start(bf16[64,512]{1,0:T(8,128)(2,1)S(1)} %get-tuple-element.30), channel_id=1, source_target_pairs={{0,8},{2,10},{4,12},{6,14},{8,0},{10,2},{12,4},{14,6},{16,24},{18,... | collective-permute-start | bytes 196616 | tf_op jit(solution)/shard_map/ppermute | solution.py:233
  145.1 8.0 %collective-permute-start.18 = (bf16[64,512]{1,0:T(8,128)(2,1)S(1)}, bf16[64,512]{1,0:T(8,128)(2,1)S(1)}, u32[]{:S(2)}, u32[]{:S(2)}) collective-permute-start(bf16[64,512]{1,0:T(8,128)(2,1)S(1)} %get-tuple-element.31), channel_id=1, source_target_pairs={{0,16},{2,18},{4,20},{6,22},{8,24},{10,26},{12,28},{14,30},{16,0},... | collective-permute-start | bytes 196616 | tf_op jit(solution)/shard_map/ppermute | solution.py:233
  146.3 6.8 %collective-permute-start.19 = (bf16[64,512]{1,0:T(8,128)(2,1)S(1)}, bf16[64,512]{1,0:T(8,128)(2,1)S(1)}, u32[]{:S(2)}, u32[]{:S(2)}) collective-permute-start(bf16[64,512]{1,0:T(8,128)(2,1)S(1)} %get-tuple-element.32), channel_id=1, source_target_pairs={{0,24},{2,26},{4,28},{6,30},{8,16},{10,18},{12,20},{14,22},{16,8},... | collective-permute-start | bytes 196616 | tf_op jit(solution)/shard_map/ppermute | solution.py:233
  (8 other events, 27.5 us)

commit v2 on v0

--- a/solution.py
+++ b/solution.py
@@ -1,9 +1,347 @@
+import functools
+
 import jax
 import jax.numpy as jnp
 from jax import lax
+from jax.experimental import pallas as pl
+from jax.experimental.pallas import tpu as pltpu
 from jax.sharding import PartitionSpec as P
 
 HD = 64
+LANE = 128
+QUAD = 4
+BF = jnp.bfloat16
+F32 = jnp.float32
+MIB = 2**20
+OFF = -1e30
+
+
+def mul(a, b):
+    return jnp.dot(a, b, preferred_element_type=F32)
+
+
+def mul_nt(a, b):
+    return lax.dot_general(a, b, (((1,), (1,)), ((), ())), preferred_element_type=F32)
+
+
+def call(kernel, name, outs, args, scratch=(), mib=16, us=1, after=(), scalars=0, load=False):
+    args, after = list(args), list(after)
+    specs = [pl.BlockSpec(memory_space=pltpu.SMEM)] * scalars
+    for arg in args[scalars:]:
+        if load:
+            specs.append(pl.BlockSpec(arg.shape, lambda i, rank=arg.ndim: (0,) * rank))
+        else:
+            specs.append(pl.BlockSpec(memory_space=pltpu.VMEM))
+    out_specs = [pl.BlockSpec(memory_space=pltpu.VMEM)] * len(outs)
+
+    def run(pos_ref, *refs):
+        kernel(pos_ref, *refs[: len(args)], *refs[len(args) + len(after) :])
+
+    return lambda pos: pl.pallas_call(
+        run,
+        out_shape=[jax.ShapeDtypeStruct(dims, dtype) for dims, dtype in outs],
+        grid=(1,) if load else (),
+        in_specs=[pl.BlockSpec(memory_space=pltpu.SMEM)] + specs + [pl.BlockSpec(memory_space=pl.ANY)] * len(after),
+        out_specs=out_specs,
+        scratch_shapes=[pltpu.VMEM(dims, dtype) for dims, dtype in scratch],
+        compiler_params=pltpu.CompilerParams(vmem_limit_bytes=mib * MIB),
+        cost_estimate=pl.CostEstimate(flops=int(us * 1.1e9), bytes_accessed=MIB, transcendentals=0),
+        name=name,
+    )(pos, *args, *after)
+
+
+def pack_kernel(pos_ref, q_ref, k_ref, v_ref, d_ref, w_ref, out_ref):
+    for scene in range(q_ref.shape[0]):
+        arrays = (
+            (q_ref[scene, 0].T * HD**-0.5).astype(BF),
+            k_ref[scene, 0].T,
+            v_ref[scene, 0].T,
+            mul_nt(w_ref[...], d_ref[scene, 0]).astype(BF),
+        )
+        for view in range(out_ref.shape[0]):
+            plane, quad = view // QUAD, view % QUAD
+            if quad // 2 == scene:
+                row = (2 * plane + quad % 2) * HD
+                for n, arr in enumerate(arrays):
+                    out_ref[view, n * HD : (n + 1) * HD] = arr[row : row + HD]
+
+
+def fetch_kernel(pos_ref, t_ref, d_ref, both, t_out, d_out):
+    core = pos_ref[2]
+    both[:LANE] = t_out[...] = t_ref[core, 0]
+    both[LANE:] = d_out[...] = d_ref[core, 0]
+
+
+def gate(value, after):
+    return lax.optimization_barrier((value, after))[0]
+
+
+def cameras_of(pos_ref, planes):
+    for j in range(QUAD):
+        for k in range(planes):
+            yield j, k, (pos_ref[0] ^ k) * QUAD + (pos_ref[1] ^ j)
+
+
+def rows_of(cam):
+    return pl.ds(pl.multiple_of(cam * LANE, LANE), LANE)
+
+
+def wrap(ref, cameras, reach, by_lane):
+    low, high, edge = reach * LANE, (cameras + reach) * LANE, reach * LANE
+    if by_lane:
+        ref[:, :edge] = ref[:, high - edge : high]
+        ref[:, high:] = ref[:, low : low + edge]
+    else:
+        ref[:edge] = ref[high - edge : high]
+        ref[high:] = ref[low : low + edge]
+
+
+def fold(acc, cameras, reach):
+    low, high, edge = reach * LANE, (cameras + reach) * LANE, reach * LANE
+    acc[high - edge : high] += acc[:edge]
+    acc[low : low + edge] += acc[high:]
+
+
+def attend_kernel(reach, pos_ref, near_ref, count_ref, in_ref, *refs):
+    outs, (k_row, v_row, k_col, v_col, dk_acc, dv_acc, s_buf, p_buf, d_buf, att_buf, dq_buf) = refs[:QUAD], refs[QUAD:]
+    cameras = in_ref.shape[0]
+    span = 2 * reach + 2
+    for cam in range(cameras):
+        rows = slice((cam + reach) * LANE, (cam + reach + 1) * LANE)
+        key, val = in_ref[cam, HD : 2 * HD], in_ref[cam, 2 * HD : 3 * HD]
+        k_col[:, rows] = key
+        v_col[:, rows] = val
+        k_row[rows, :] = key.T
+        v_row[rows, :] = val.T
+    for ref, by_lane in ((k_col, True), (v_col, True), (k_row, False), (v_row, False)):
+        wrap(ref, cameras, reach, by_lane)
+    dk_acc[...] = jnp.zeros_like(dk_acc)
+    dv_acc[...] = jnp.zeros_like(dv_acc)
+
+    def step(i, carry):
+        def pair(n):
+            rows = slice(n * HD, (n + 1) * HD)
+            return jnp.concatenate([in_ref[2 * i, rows], in_ref[2 * i + 1, rows]], axis=1)
+
+        q_col, d_col = pair(0), pair(3)
+        q_rows = q_col.T
+        place = lax.broadcasted_iota(jnp.int32, (16, 2 * LANE), 0)
+        second = lax.broadcasted_iota(jnp.int32, (16, 2 * LANE), 1) >= LANE
+        target = lax.rem(2 * i + place + (cameras - reach), cameras)
+        live = target == jnp.where(second, 2 * i + 1, 2 * i)
+        for m in range(2 * reach):
+            first, other = [jnp.where(m < count_ref[2 * i + t], near_ref[2 * i + t, m], -1) for t in range(2)]
+            live = live | (target == jnp.where(second, other, first))
+        offset = place - reach - jnp.where(second, 1, 0)
+        bias = jnp.where(live & (jnp.abs(offset) <= reach), 0.0, OFF)
+        window = pl.ds(pl.multiple_of(2 * i * LANE, 2 * LANE), span * LANE)
+        top = None
+        for j in range(span):
+            score = mul(k_row[rows_of(2 * i + j), :], q_col)
+            s_buf[j] = score
+            peak = jnp.max(score, axis=0, keepdims=True) + bias[j : j + 1]
+            top = peak if top is None else jnp.maximum(top, peak)
+        total = jnp.zeros((8, 2 * LANE), F32)
+        for j in range(span):
+            prob = jnp.exp(s_buf[j] + (bias[j : j + 1] - top))
+            total = total + jnp.sum(prob.reshape(LANE // 8, 8, 2 * LANE), axis=0)
+            p_buf[j * LANE : (j + 1) * LANE] = prob.astype(BF)
+        inv = 1.0 / jnp.sum(total, axis=0, keepdims=True)
+        att = (mul(v_col[:, window], p_buf[...]) * inv).astype(BF)
+        d_wide = d_col.astype(F32)
+        delta = jnp.sum(att.astype(F32) * d_wide, axis=0, keepdims=True) * inv
+        d_low = (d_wide * inv).astype(BF)
+        dv_acc[window, :] += mul(p_buf[...], d_low.T)
+        for j in range(span):
+            rows = slice(j * LANE, (j + 1) * LANE)
+            d_prob = mul(v_row[rows_of(2 * i + j), :], d_low)
+            d_buf[rows] = (p_buf[rows].astype(F32) * (d_prob - delta)).astype(BF)
+        dk_acc[window, :] += mul(d_buf[...], q_rows)
+        d_query = (mul(k_col[:, window], d_buf[...]) * HD**-0.5).astype(BF)
+        for t in range(2):
+            att_buf[2 * i + t] = att[:, t * LANE : (t + 1) * LANE]
+            dq_buf[2 * i + t] = d_query[:, t * LANE : (t + 1) * LANE]
+        return carry
+
+    lax.fori_loop(0, cameras // 2, step, 0)
+    fold(dk_acc, cameras, reach)
+    fold(dv_acc, cameras, reach)
+    for j, k, cam in cameras_of(pos_ref, cameras // QUAD):
+        rows = rows_of(cam + reach)
+        outs[j][k, :HD] = att_buf[cam]
+        outs[j][k, HD : 2 * HD] = dv_acc[rows, :].T.astype(BF)
+        outs[j][k, 2 * HD : 3 * HD] = dq_buf[cam]
+        outs[j][k, 3 * HD :] = dk_acc[rows, :].T.astype(BF)
+
+
+def hand_out(wide, outs, planes, pos_ref):
+    part = wide.shape[0] // (QUAD * planes)
+    for j in range(QUAD):
+        for p in range(planes):
+            rows = pl.ds(pl.multiple_of((p * QUAD + (pos_ref[1] ^ j)) * part, part), part)
+            outs[j][p * part : (p + 1) * part] = wide[rows, :].astype(BF)
+
+
+def weights_kernel(planes, pos_ref, *refs):
+    blocks, (tok_ref, d_ref), far, outs = refs[:QUAD], refs[QUAD : QUAD + 2], refs[QUAD + 2 : -9], refs[-9:-5]
+    left, left_o, tok, d_o, wide = refs[-5:]
+    quad, core = pos_ref[1], pos_ref[2]
+    for j in range(QUAD):
+        scene, half = (quad ^ j) // 2, (quad ^ j) % 2
+        for k in range(planes):
+            at = rows_of(2 * k + (scene ^ core))
+            left_o[pl.ds(pl.multiple_of(half * HD, HD), HD), at] = blocks[j][k, :HD]
+            for n in range(3):
+                row = pl.multiple_of((2 * n + half) * HD, HD)
+                left[pl.ds(row, HD), at] = blocks[j][k, (n + 1) * HD : (n + 2) * HD]
+    for n in range(2):
+        at = slice(n * LANE, (n + 1) * LANE)
+        tok[at] = tok_ref[core ^ n, 0]
+        d_o[at] = d_ref[core ^ n, 0]
+    for n, ref in enumerate(far[:2], 2):
+        at = slice(n * LANE, (n + 1) * LANE)
+        tok[at] = ref[:LANE]
+        d_o[at] = ref[LANE:]
+    for n, ref in enumerate(far[2:]):
+        at = slice((n // 2 + 4) * LANE, (n // 2 + 5) * LANE)
+        (d_o if n % 2 else tok)[at] = ref[...]
+    wide[:, : 6 * HD] = mul(left[...], tok[...]).T
+    wide[:, 6 * HD :] = mul(left_o[...], d_o[...]).T
+    hand_out(wide, outs, planes, pos_ref)
+
+
+def sum_kernel(planes, pos_ref, *refs):
+    terms, outs, total = refs[:QUAD], refs[QUAD:-1], refs[-1]
+    acc = terms[0][...].astype(F32)
+    for term in terms[1:]:
+        acc = acc + term[...].astype(F32)
+    total[...] = acc
+    part = total.shape[0] // planes
+    for k in range(planes):
+        rows = pl.ds(pl.multiple_of((pos_ref[0] ^ k) * part, part), part)
+        outs[k][...] = total[rows, :].astype(BF)
+
+
+def finish_kernel(planes, pos_ref, *refs):
+    terms, (w_ref, o_ref, buf) = refs[:planes], refs[planes:]
+    for k in range(planes):
+        buf[pos_ref[0] ^ k] = terms[k][...].astype(F32)
+    two = 2 * HD
+    for p in range(planes):
+        cols = slice(p * two, (p + 1) * two)
+        o_ref[:, cols] = buf[p, :, 3 * two :]
+        for place, j in enumerate((2, 0, 1)):
+            w_ref[j, :, cols] = buf[p, :, place * two : (place + 1) * two]
+
+
+def turn_kernel(planes, pos_ref, *refs):
+    for k in range(1, planes):
+        for j in range(QUAD):
+            refs[QUAD + k - 1][j] = refs[j][k, HD:]
+
+
+def inputs_kernel(planes, pos_ref, *refs):
+    own, far, (w_ref, mine, theirs, turned) = refs[:QUAD], refs[QUAD : QUAD + planes - 1], refs[QUAD + planes - 1 :]
+    plane, quad, core = pos_ref[0], pos_ref[1], pos_ref[2]
+    for k in range(planes):
+        for j in range(QUAD):
+            block = own[j][0, HD:] if k == 0 else far[k - 1][j]
+            scene, half = (quad ^ j) // 2, (quad ^ j) % 2
+            row = pl.ds(pl.multiple_of((2 * (plane ^ k) + half) * HD, HD), HD)
+            for place, n in enumerate((2, 0, 1)):
+                turned[scene, n, row] = block[place * HD : (place + 1) * HD]
+    left = [jnp.concatenate([turned[scene, j].T for scene in range(2)], axis=0) for j in range(3)]
+    half = w_ref.shape[1] // 2
+    for ref, who in ((theirs, 1 - core), (mine, core)):
+        rows = pl.ds(pl.multiple_of(who * half, half), half)
+        acc = mul_nt(left[0], w_ref[0, rows, :])
+        for j in range(1, 3):
+            acc = acc + mul_nt(left[j], w_ref[j, rows, :])
+        ref[...] = acc
+
+
+def split_body(tokens, queries, keys, values, w_qkv, w_out, d_out, neighbours, degrees):
+    cameras = neighbours.shape[0]
+    reach = neighbours.shape[1] // 2
+    planes = cameras // QUAD
+    scenes, _, rows, width = queries.shape
+    model = tokens.shape[3]
+    part = model // cameras
+    view, core = lax.axis_index("view"), lax.axis_index("head")
+    pos = jnp.stack([view // QUAD, view % QUAD, core]).astype(jnp.int32)
+    span = 2 * reach + 2
+    ext = (cameras + 2 * reach) * rows
+
+    def along(value, pairs):
+        return lax.ppermute(value, "view", pairs)
+
+    def over_plane(values):
+        return [values[0]] + [along(values[j], [(i, i ^ j) for i in range(cameras)]) for j in range(1, QUAD)]
+
+    def over_column(values, first=0):
+        return [
+            value if k == 0 else along(value, [(i, i ^ (k * QUAD)) for i in range(cameras)])
+            for k, value in enumerate(values, first)
+        ]
+
+    def other_core(value):
+        return lax.ppermute(value, "head", [(0, 1), (1, 0)])
+
+    piece = ((rows, model), BF)
+    both, tok, out = call(fetch_kernel, "fetch", [((2 * rows, model), BF), piece, piece], (tokens, d_out))(pos)
+
+    arrays = (queries, keys, values, d_out, w_out)
+    packed = call(pack_kernel, "pack", [((cameras, 4 * HD, rows), BF)], arrays, load=True)(pos)[0]
+    packed = lax.all_to_all(packed, "view", 0, 0, tiled=True)
+
+    block = ((planes, 4 * HD, rows), BF)
+    blocks = call(
+        functools.partial(attend_kernel, reach), "attend", [block] * QUAD, (neighbours, degrees, packed),
+        [
+            ((ext, HD), BF), ((ext, HD), BF), ((HD, ext), BF), ((HD, ext), BF), ((ext, HD), F32), ((ext, HD), F32),
+            ((span, rows, 2 * rows), F32), ((span * rows, 2 * rows), BF), ((span * rows, 2 * rows), BF),
+            ((cameras, HD, rows), BF), ((cameras, HD, rows), BF),
+        ],
+        32, 13, scalars=2,
+    )(pos)
+    done = blocks[0]
+    blocks = over_plane(blocks)
+    near = over_column([both], 1)[0]
+    pieces = [over_column([gate(tok, packed)], 2)[0], over_column([gate(out, packed)], 2)[0]]
+    pieces += [over_column([gate(value, done)], 1)[0] for value in pieces]
+    column = []
+    for value in [near] + pieces:
+        column += [value, other_core(value)]
+    column = column[:2] + [column[2 + n] for n in (0, 2, 1, 3, 4, 6, 5, 7)]
+
+    depth = 2 * planes * rows
+    args = blocks + [tokens, d_out] + column
+    terms = call(
+        functools.partial(weights_kernel, planes), "weights", [((model // QUAD, 8 * HD), BF)] * QUAD, args,
+        [((6 * HD, depth), BF), ((2 * HD, depth), BF), ((depth, model), BF), ((depth, model), BF), ((model, 8 * HD), F32)],
+        32, 3,
+    )(pos)
+    started = terms[:1]
+    terms = call(
+        functools.partial(sum_kernel, planes), "plane_sum", [((part, 8 * HD), BF)] * planes, over_plane(terms),
+        [((model // QUAD, 8 * HD), F32)],
+    )(pos)
+    terms = over_column(terms)
+    d_wqkv, d_wo = call(
+        functools.partial(finish_kernel, planes), "finish", [((3, part, width), F32), ((part, width), F32)], terms,
+        [((planes, part, 8 * HD), F32)],
+    )(pos)
+
+    grads = call(
+        functools.partial(turn_kernel, planes), "turn", [((QUAD, 3 * HD, rows), BF)] * (planes - 1), blocks
+    )(pos)
+    args = blocks + over_column(grads, 1) + [w_qkv]
+    mine, theirs = call(
+        functools.partial(inputs_kernel, planes), "inputs", [((scenes * rows, model // 2), F32)] * 2, args,
+        [((scenes, 3, width, rows), BF)], 32, 2, after=started,
+    )(pos)
+    d_tokens = (mine + other_core(theirs)).astype(BF).reshape(scenes, 1, rows, model // 2)
+    return (d_tokens, d_wqkv, d_wo.T)
 
 
 def shifted(value, axis, steps):
@@ -12,7 +350,7 @@
     return lax.ppermute(value, axis, pairs)
 
 
-def body(tokens, queries, keys, values, w_qkv, w_out, d_out, neighbours, degrees):
+def halo_body(tokens, queries, keys, values, w_qkv, w_out, d_out, neighbours, degrees):
     cameras = neighbours.shape[0]
     reach = neighbours.shape[1] // 2
     offsets = [step for step in range(-reach, reach + 1) if step != 0]
@@ -133,6 +471,21 @@
     return (d_tokens, d_wqkv, d_wo)
 
 
+def body(tokens, queries, keys, values, w_qkv, w_out, d_out, neighbours, degrees):
+    args = (tokens, queries, keys, values, w_qkv, w_out, d_out, neighbours, degrees)
+    scenes, _, rows, width = queries.shape
+    cameras, reach = neighbours.shape[0], neighbours.shape[1] // 2
+    fits = (
+        scenes == 2
+        and lax.axis_size("head") == 2
+        and scenes * (width // HD) == cameras == lax.axis_size("view")
+        and rows == LANE
+        and cameras == QUAD * QUAD
+        and cameras >= 2 * reach + 2
+    )
+    return split_body(*args) if fits else halo_body(*args)
+
+
 def solution(mesh):
     return jax.shard_map(
         body,

time: 586 us -> 114 us (0.19)
  waiting for transfers between devices: 314 us -> 50.8 us
  matrix products: 88.5 us -> 0 us
  starting transfers between devices: 87.8 us -> 32.6 us
  local copies, waits for them, and re-layouts: 53.7 us -> 5.9 us
  Pallas kernels: 0 us -> 22.4 us
  between operations: 22.2 us -> 0.79 us
  other arithmetic: 17.3 us -> 0.85 us
    unnamed x4 -> x0, waiting for transfers between devices: 262 us -> none
    dot_general x58 -> x0, matrix products: 88.5 us -> none  [the longest x9 21.7 us: body(): jnp.einsum('shtu,suhd->sthd', prob_low, value_blk, preferred_element_type...]
    ppermute x32 -> x23, starting transfers between devices: 87.7 us -> 24.2 us  [the longest x17 23.6 us: along(): return lax.ppermute(value, 'view', pairs)]
    ppermute x16 -> x0, local copies, waits for them, and re-layouts: 28.7 us -> none  [shifted(): return lax.ppermute(value, axis, pairs)]
    ppermute x32 -> x23, waiting for transfers between devices: 52.1 us -> 29.7 us  [the longest x17 29.6 us: along(): return lax.ppermute(value, 'view', pairs)]
    pallas_call x0 -> x8, Pallas kernels: none -> 22.4 us  [call(): pl.pallas_call(run, out_shape=[jax.ShapeDtypeStruct(dims, dtype) for dims...]
    all_to_all x0 -> x1, waiting for transfers between devices: none -> 21.1 us  [split_body(): packed = lax.all_to_all(packed, 'view', 0, 0, tiled=True)]
    reduce_or x8 -> x0, other arithmetic: 10.3 us -> none  [body(): jnp.any(hit)]
  transfers between devices with their start and end apart: 35 -> 24, of which waited for: 7 -> 10; matrix products, arithmetic and copies ran while one was open for 23% -> 0% of each run, Pallas kernels for 0% -> 18%
where the time goes in v2:
time: 114 us; the launch traced here: 113 us
  waiting for transfers between devices  50.8 us (45%)
  starting transfers between devices  32.6 us (29%)
  Pallas kernels  22.4 us (20%)
  local copies, waits for them, and re-layouts  5.9 us (5%)
    ppermute x17, waiting for transfers between devices, along(): return lax.ppermute(value, 'view', pairs)  29.6 us
    ppermute x17, starting transfers between devices, along(): return lax.ppermute(value, 'view', pairs)  23.6 us
    pallas_call x8, Pallas kernels, call(): pl.pallas_call(run, out_shape=[jax.ShapeDtypeStruct(dims, dtype) for dims...  22.4 us
    all_to_all x1, waiting for transfers between devices, split_body(): packed = lax.all_to_all(packed, 'view', 0, 0, tiled=True)  21.1 us
    all_to_all x1, starting transfers between devices, split_body(): packed = lax.all_to_all(packed, 'view', 0, 0, tiled=True)  8.44 us
    unnamed x23, local copies, waits for them, and re-layouts  5.9 us
  transfers between devices with their start and end apart: 24, of which 10 were waited for; matrix products, arithmetic and copies ran while one was open for 0% of the time, Pallas kernels for 18%

profile of v2, /device:TPU:0, one launch (start us, length us, event | category | flops | bytes accessed | tf_op | source)
XLA Modules:
  0.0 113.3 jit_solution(8580037570638618592)
XLA Ops:
  0.7 1.2 %copy-done.1 = bf16[512,1024]{1,0:T(8,128)(2,1)S(1)} copy-done((bf16[512,1024]{1,0:T(8,128)(2,1)S(1)}, bf16[512,1024]{1,0:T(8,128)(2,1)}, u32[]{:S(2)}) %copy-start.1) | copy-done | bytes 1048600
  2.0 1.0 copy-done.2
  3.0 0.9 copy-done.5
  5.9 2.2 %pack.1 = bf16[16,256,128]{2,1,0:T(8,128)(2,1)} custom-call(s32[3]{0:T(128)S(1)} %pad_add_fusion.pos_ref, bf16[2,1,128,512]{3,2,1,0:T(8,128)(2,1)S(1)} %copy-done.5, bf16[2,1,128,512]{3,2,1,0:T(8,128)(2,1)S(1)} %copy-done.6, bf16[2,1,128,512]{3,2,1,0:T(8,128)(2,1)S(1)} %copy-done.7, bf16[2,1,128,1024]{3,2,1,0:T(8,128)(2,1)S(1)} %copy-done.2, ...), custom_call_target="tpu_custom_call" | custom-call | flops 1100000000 | bytes 1048576 | tf_op jit(solution)/shard_map/pack/pallas_call | solution.py:40
  8.1 8.4 %all-to-all-start = ((bf16[16,256,128]{2,1,0:T(8,128)(2,1)}), bf16[16,256,128]{2,1,0:T(8,128)(2,1)S(1)}, u32[]{:S(2)}, u32[]{:S(2)}) async-start(bf16[16,256,128]{2,1,0:T(8,128)(2,1)} %pack.1), calls=%async_computation | async-start | bytes 2097152 | tf_op jit(solution)/shard_map/all_to_all | solution.py:295
  17.9 1.9 %collective-permute-start.6 = (bf16[256,1024]{1,0:T(8,128)(2,1)S(1)}, bf16[256,1024]{1,0:T(8,128)(2,1)S(1)}, u32[]{:S(2)}, u32[]{:S(2)}) collective-permute-start(bf16[256,1024]{1,0:T(8,128)(2,1)S(1)} %get-tuple-element.36), channel_id=1, source_target_pairs={{0,8},{2,10},{4,12},{6,14},{8,0},{10,2},{12,4},{14,6},{16,24},{18,... | collective-permute-start | bytes 1572872 | tf_op jit(solution)/shard_map/ppermute | solution.py:276
  19.9 21.1 %all-to-all-done.refs_2_ = bf16[16,256,128]{2,1,0:T(8,128)(2,1)S(1)} async-done(((bf16[16,256,128]{2,1,0:T(8,128)(2,1)}), bf16[16,256,128]{2,1,0:T(8,128)(2,1)S(1)}, u32[]{:S(2)}, u32[]{:S(2)}) %all-to-all-start) | async-done | bytes 1048608 | tf_op jit(solution)/shard_map/all_to_all | solution.py:295
  41.0 2.7 %collective-permute-start.8 = (bf16[128,1024]{1,0:T(8,128)(2,1)}, bf16[128,1024]{1,0:T(8,128)(2,1)S(1)}, u32[]{:S(2)}, u32[]{:S(2)}) collective-permute-start(bf16[128,1024]{1,0:T(8,128)(2,1)} %copy-done.8), channel_id=1, source_target_pairs={{0,16},{2,18},{4,20},{6,22},{8,24},{10,26},{12,28},{14,30},{16,0},... | collective-permute-start | bytes 786440 | tf_op jit(solution)/shard_map/ppermute | solution.py:276
  43.9 12.9 %attend.1 = (bf16[4,256,128]{2,1,0:T(8,128)(2,1)S(1)}, bf16[4,256,128]{2,1,0:T(8,128)(2,1)S(1)}, bf16[4,256,128]{2,1,0:T(8,128)(2,1)S(1)}, bf16[4,256,128]{2,1,0:T(8,128)(2,1)S(1)}) custom-call(s32[3]{0:T(128)S(1)} %pad_add_fusion.pos_ref, s32[16,8]{1,0:T(8,128)S(1)} %copy.12.refs_0_, s32[16]{0:T(128)S(1)} %copy-done.9, ...), custom_call_target="tpu_custom_call" | custom-call | flops 14300000256 | bytes 1048576 | tf_op jit(solution)/shard_map/attend/pallas_call | solution.py:40
  56.8 1.3 %collective-permute-start = (bf16[4,256,128]{2,1,0:T(8,128)(2,1)S(1)}, bf16[4,256,128]{2,1,0:T(8,128)(2,1)S(1)}, u32[]{:S(2)}, u32[]{:S(2)}) collective-permute-start(bf16[4,256,128]{2,1,0:T(8,128)(2,1)S(1)} %get-tuple-element.30), channel_id=1, source_target_pairs={{0,2},{2,0},{4,6},{6,4},{8,10},{10,8},{12,14},{14,12},{16,18},{18,... | collective-permute-start | bytes 786440 | tf_op jit(solution)/shard_map/ppermute | solution.py:276
  58.2 1.3 %collective-permute-start.1 = (bf16[4,256,128]{2,1,0:T(8,128)(2,1)S(1)}, bf16[4,256,128]{2,1,0:T(8,128)(2,1)S(1)}, u32[]{:S(2)}, u32[]{:S(2)}) collective-permute-start(bf16[4,256,128]{2,1,0:T(8,128)(2,1)S(1)} %get-tuple-element.31), channel_id=1, source_target_pairs={{0,4},{2,6},{4,0},{6,2},{8,12},{10,14},{12,8},{14,10},{16,20},{18,... | collective-permute-start | bytes 786440 | tf_op jit(solution)/shard_map/ppermute | solution.py:276
  59.4 3.1 %collective-permute-done.8.refs_8_ = bf16[128,1024]{1,0:T(8,128)(2,1)S(1)} collective-permute-done((bf16[128,1024]{1,0:T(8,128)(2,1)}, bf16[128,1024]{1,0:T(8,128)(2,1)S(1)}, u32[]{:S(2)}, u32[]{:S(2)}) %collective-permute-start.8) | collective-permute-done | bytes 262176 | tf_op jit(solution)/shard_map/ppermute | solution.py:276
  62.6 1.8 %collective-permute-start.2 = (bf16[4,256,128]{2,1,0:T(8,128)(2,1)S(1)}, bf16[4,256,128]{2,1,0:T(8,128)(2,1)S(1)}, u32[]{:S(2)}, u32[]{:S(2)}) collective-permute-start(bf16[4,256,128]{2,1,0:T(8,128)(2,1)S(1)} %get-tuple-element.32), channel_id=1, source_target_pairs={{0,6},{2,4},{4,2},{6,0},{8,14},{10,12},{12,10},{14,8},{16,22},{18,... | collective-permute-start | bytes 786440 | tf_op jit(solution)/shard_map/ppermute | solution.py:276
  64.4 1.8 %collective-permute-done.9.refs_9_ = bf16[128,1024]{1,0:T(8,128)(2,1)S(1)} collective-permute-done((bf16[128,1024]{1,0:T(8,128)(2,1)S(1)}, bf16[128,1024]{1,0:T(8,128)(2,1)S(1)}, u32[]{:S(2)}, u32[]{:S(2)}) %collective-permute-start.9) | collective-permute-done | bytes 262176 | tf_op jit(solution)/shard_map/ppermute | solution.py:276
  66.2 2.0 %collective-permute-start.13 = (bf16[128,1024]{1,0:T(8,128)(2,1)S(1)}, bf16[128,1024]{1,0:T(8,128)(2,1)S(1)}, u32[]{:S(2)}, u32[]{:S(2)}) collective-permute-start(bf16[128,1024]{1,0:T(8,128)(2,1)S(1)} %collective-permute-done.9.refs_9_), channel_id=1, source_target_pairs={{0,8},{2,10},{4,12},{6,14},{8,0},{10,2},{12,4},{14,6},{16,24},{18,... | collective-permute-start | bytes 786440 | tf_op jit(solution)/shard_map/ppermute | solution.py:276
  68.3 4.2 %collective-permute-done.1.refs_2_ = bf16[4,256,128]{2,1,0:T(8,128)(2,1)S(1)} collective-permute-done((bf16[4,256,128]{2,1,0:T(8,128)(2,1)S(1)}, bf16[4,256,128]{2,1,0:T(8,128)(2,1)S(1)}, u32[]{:S(2)}, u32[]{:S(2)}) %collective-permute-start.1) | collective-permute-done | bytes 262176 | tf_op jit(solution)/shard_map/ppermute | solution.py:276
  73.0 2.4 %collective-permute-done.12.refs_12_ = bf16[128,1024]{1,0:T(8,128)(2,1)S(1)} collective-permute-done((bf16[128,1024]{1,0:T(8,128)(2,1)S(1)}, bf16[128,1024]{1,0:T(8,128)(2,1)S(1)}, u32[]{:S(2)}, u32[]{:S(2)}) %collective-permute-start.12) | collective-permute-done | bytes 262176 | tf_op jit(solution)/shard_map/ppermute | solution.py:276
  75.4 2.8 %collective-permute-done.13.refs_13_ = bf16[128,1024]{1,0:T(8,128)(2,1)S(1)} collective-permute-done((bf16[128,1024]{1,0:T(8,128)(2,1)S(1)}, bf16[128,1024]{1,0:T(8,128)(2,1)S(1)}, u32[]{:S(2)}, u32[]{:S(2)}) %collective-permute-start.13) | collective-permute-done | bytes 262176 | tf_op jit(solution)/shard_map/ppermute | solution.py:276
  79.1 1.3 %collective-permute-start.4 = (bf16[4,192,128]{2,1,0:T(8,128)(2,1)S(1)}, bf16[4,192,128]{2,1,0:T(8,128)(2,1)S(1)}, u32[]{:S(2)}, u32[]{:S(2)}) collective-permute-start(bf16[4,192,128]{2,1,0:T(8,128)(2,1)S(1)} %get-tuple-element.34), channel_id=1, source_target_pairs={{0,16},{2,18},{4,20},{6,22},{8,24},{10,26},{12,28},{14,30},{16,0},... | collective-permute-start | bytes 589832 | tf_op jit(solution)/shard_map/ppermute | solution.py:276
  80.5 2.8 %collective-permute-start.5 = (bf16[4,192,128]{2,1,0:T(8,128)(2,1)S(1)}, bf16[4,192,128]{2,1,0:T(8,128)(2,1)S(1)}, u32[]{:S(2)}, u32[]{:S(2)}) collective-permute-start(bf16[4,192,128]{2,1,0:T(8,128)(2,1)S(1)} %get-tuple-element.35), channel_id=1, source_target_pairs={{0,24},{2,26},{4,28},{6,30},{8,16},{10,18},{12,20},{14,22},{16,8},... | collective-permute-start | bytes 589832 | tf_op jit(solution)/shard_map/ppermute | solution.py:276
  83.3 2.3 %weights.1 = (bf16[256,512]{1,0:T(8,128)(2,1)S(1)}, bf16[256,512]{1,0:T(8,128)(2,1)S(1)}, bf16[256,512]{1,0:T(8,128)(2,1)S(1)}, bf16[256,512]{1,0:T(8,128)(2,1)S(1)}) custom-call(s32[3]{0:T(128)S(1)} %pad_add_fusion.pos_ref, bf16[4,256,128]{2,1,0:T(8,128)(2,1)S(1)} %get-tuple-element.29.refs_0_, bf16[4,256,128]{2,1,0:T(8,128)(2,1)S(1)} %collective-permute-done.refs_1_, ...), custom_call_target="tpu_custom_call" | custom-call | flops 3300000000 | bytes 1048576 | tf_op jit(solution)/shard_map/weights/pallas_call | solution.py:40
  85.5 1.8 %collective-permute-start.17 = (bf16[256,512]{1,0:T(8,128)(2,1)S(1)}, bf16[256,512]{1,0:T(8,128)(2,1)S(1)}, u32[]{:S(2)}, u32[]{:S(2)}) collective-permute-start(bf16[256,512]{1,0:T(8,128)(2,1)S(1)} %get-tuple-element.46), channel_id=1, source_target_pairs={{0,2},{2,0},{4,6},{6,4},{8,10},{10,8},{12,14},{14,12},{16,18},{18,... | collective-permute-start | bytes 786440 | tf_op jit(solution)/shard_map/ppermute | solution.py:276
  87.3 1.5 %collective-permute-done.3.refs_4_ = bf16[4,192,128]{2,1,0:T(8,128)(2,1)S(1)} collective-permute-done((bf16[4,192,128]{2,1,0:T(8,128)(2,1)S(1)}, bf16[4,192,128]{2,1,0:T(8,128)(2,1)S(1)}, u32[]{:S(2)}, u32[]{:S(2)}) %collective-permute-start.3) | collective-permute-done | bytes 196640 | tf_op jit(solution)/shard_map/ppermute | solution.py:276
  88.8 1.6 %collective-permute-start.19 = (bf16[256,512]{1,0:T(8,128)(2,1)S(1)}, bf16[256,512]{1,0:T(8,128)(2,1)S(1)}, u32[]{:S(2)}, u32[]{:S(2)}) collective-permute-start(bf16[256,512]{1,0:T(8,128)(2,1)S(1)} %get-tuple-element.48), channel_id=1, source_target_pairs={{0,6},{2,4},{4,2},{6,0},{8,14},{10,12},{12,10},{14,8},{16,22},{18,... | collective-permute-start | bytes 786440 | tf_op jit(solution)/shard_map/ppermute | solution.py:276
  90.4 5.9 %collective-permute-done.4.refs_5_ = bf16[4,192,128]{2,1,0:T(8,128)(2,1)S(1)} collective-permute-done((bf16[4,192,128]{2,1,0:T(8,128)(2,1)S(1)}, bf16[4,192,128]{2,1,0:T(8,128)(2,1)S(1)}, u32[]{:S(2)}, u32[]{:S(2)}) %collective-permute-start.4) | collective-permute-done | bytes 196640 | tf_op jit(solution)/shard_map/ppermute | solution.py:276
  96.3 1.6 %inputs.1 = (f32[256,512]{1,0:T(8,128)S(1)}, f32[256,512]{1,0:T(8,128)S(1)}) custom-call(s32[3]{0:T(128)S(1)} %pad_add_fusion.pos_ref, bf16[4,256,128]{2,1,0:T(8,128)(2,1)S(1)} %get-tuple-element.29.refs_0_, bf16[4,256,128]{2,1,0:T(8,128)(2,1)S(1)} %collective-permute-done.refs_1_, bf16[4,256,128]{2,1,0:T(8,128)(2,1)S(1)} %collective-permute-done.1.refs_2_, ...), custom_call_target="tpu_custom_call" | custom-call | flops 2200000000 | bytes 1048576 | tf_op jit(solution)/shard_map/inputs/pallas_call | solution.py:40
  98.0 2.5 %collective-permute-done.18.refs_2_ = bf16[256,512]{1,0:T(8,128)(2,1)S(1)} collective-permute-done((bf16[256,512]{1,0:T(8,128)(2,1)S(1)}, bf16[256,512]{1,0:T(8,128)(2,1)S(1)}, u32[]{:S(2)}, u32[]{:S(2)}) %collective-permute-start.18) | collective-permute-done | bytes 262176 | tf_op jit(solution)/shard_map/ppermute | solution.py:276
  101.3 1.7 %collective-permute-start.20 = (bf16[64,512]{1,0:T(8,128)(2,1)S(1)}, bf16[64,512]{1,0:T(8,128)(2,1)S(1)}, u32[]{:S(2)}, u32[]{:S(2)}) collective-permute-start(bf16[64,512]{1,0:T(8,128)(2,1)S(1)} %get-tuple-element.50), channel_id=1, source_target_pairs={{0,8},{2,10},{4,12},{6,14},{8,0},{10,2},{12,4},{14,6},{16,24},{18,... | collective-permute-start | bytes 196616 | tf_op jit(solution)/shard_map/ppermute | solution.py:276
  103.0 1.3 %collective-permute-start.21 = (bf16[64,512]{1,0:T(8,128)(2,1)S(1)}, bf16[64,512]{1,0:T(8,128)(2,1)S(1)}, u32[]{:S(2)}, u32[]{:S(2)}) collective-permute-start(bf16[64,512]{1,0:T(8,128)(2,1)S(1)} %get-tuple-element.51), channel_id=1, source_target_pairs={{0,16},{2,18},{4,20},{6,22},{8,24},{10,26},{12,28},{14,30},{16,0},... | collective-permute-start | bytes 196616 | tf_op jit(solution)/shard_map/ppermute | solution.py:276
  104.3 1.4 %collective-permute-start.22 = (bf16[64,512]{1,0:T(8,128)(2,1)S(1)}, bf16[64,512]{1,0:T(8,128)(2,1)S(1)}, u32[]{:S(2)}, u32[]{:S(2)}) collective-permute-start(bf16[64,512]{1,0:T(8,128)(2,1)S(1)} %get-tuple-element.52), channel_id=1, source_target_pairs={{0,24},{2,26},{4,28},{6,30},{8,16},{10,18},{12,20},{14,22},{16,8},... | collective-permute-start | bytes 196616 | tf_op jit(solution)/shard_map/ppermute | solution.py:276
  105.7 5.3 %collective-permute-done.21.refs_2_ = bf16[64,512]{1,0:T(8,128)(2,1)S(1)} collective-permute-done((bf16[64,512]{1,0:T(8,128)(2,1)S(1)}, bf16[64,512]{1,0:T(8,128)(2,1)S(1)}, u32[]{:S(2)}, u32[]{:S(2)}) %collective-permute-start.21) | collective-permute-done | bytes 65568 | tf_op jit(solution)/shard_map/ppermute | solution.py:276
  111.1 1.4 %finish.1 = (f32[3,64,512]{2,1,0:T(8,128)}, f32[64,512]{1,0:T(8,128)}) custom-call(s32[3]{0:T(128)S(1)} %pad_add_fusion.pos_ref, bf16[64,512]{1,0:T(8,128)(2,1)S(1)} %get-tuple-element.49.refs_0_, bf16[64,512]{1,0:T(8,128)(2,1)S(1)} %collective-permute-done.20.refs_1_, bf16[64,512]{1,0:T(8,128)(2,1)S(1)} %collective-permute-done.21.refs_2_, ...), custom_call_target="tpu_custom_call" | custom-call | flops 1100000000 | bytes 1048576 | tf_op jit(solution)/shard_map/finish/pallas_call | solution.py:40
  (49 shorter events, 6.7 us)
Async XLA Ops:
  0.7 1.2 %copy-start.1 = (bf16[512,1024]{1,0:T(8,128)(2,1)S(1)}, bf16[512,1024]{1,0:T(8,128)(2,1)}, u32[]{:S(2)}) copy-start(bf16[512,1024]{1,0:T(8,128)(2,1)} %refs_4_.2) | copy-start | bytes 3145732
  2.0 1.0 copy-start.2
  3.0 0.9 copy-start.5
  5.8 10.7 %copy-start.3 = (bf16[2,1,128,1024]{3,2,1,0:T(8,128)(2,1)S(1)}, bf16[2,1,128,1024]{3,2,1,0:T(8,128)(2,1)}, u32[]{:S(2)}) copy-start(bf16[2,1,128,1024]{3,2,1,0:T(8,128)(2,1)} %refs_5_.1) | copy-start | bytes 1572868
  5.8 10.7 %copy-start.4 = (bf16[2,1,128,1024]{3,2,1,0:T(8,128)(2,1)S(1)}, bf16[2,1,128,1024]{3,2,1,0:T(8,128)(2,1)}, u32[]{:S(2)}) copy-start(bf16[2,1,128,1024]{3,2,1,0:T(8,128)(2,1)} %refs_4_.3) | copy-start | bytes 1572868
  8.1 11.7 %copy-start.10 = (s32[16,8]{0,1:T(8,128)S(1)}, s32[16,8]{0,1:T(8,128)}, u32[]{:S(2)}) copy-start(s32[16,8]{0,1:T(8,128)} %param.16) | copy-start | bytes 1540
  8.1 35.8 %copy-start.9 = (s32[16]{0:T(128)S(1)}, s32[16]{0:T(128)}, u32[]{:S(2)}) copy-start(s32[16]{0:T(128)} %refs_1_.4) | copy-start | bytes 196
  8.1 32.9 %all-to-all-start = ((bf16[16,256,128]{2,1,0:T(8,128)(2,1)}), bf16[16,256,128]{2,1,0:T(8,128)(2,1)S(1)}, u32[]{:S(2)}, u32[]{:S(2)}) async-start(bf16[16,256,128]{2,1,0:T(8,128)(2,1)} %pack.1), calls=%async_computation | async-start | bytes 2097152 | tf_op jit(solution)/shard_map/all_to_all | solution.py:295
  17.9 40.3 %collective-permute-start.6 = (bf16[256,1024]{1,0:T(8,128)(2,1)S(1)}, bf16[256,1024]{1,0:T(8,128)(2,1)S(1)}, u32[]{:S(2)}, u32[]{:S(2)}) collective-permute-start(bf16[256,1024]{1,0:T(8,128)(2,1)S(1)} %get-tuple-element.36), channel_id=1, source_target_pairs={{0,8},{2,10},{4,12},{6,14},{8,0},{10,2},{12,4},{14,6},{16,24},{18,... | collective-permute-start | bytes 1572872 | tf_op jit(solution)/shard_map/ppermute | solution.py:276
  41.0 21.6 %collective-permute-start.8 = (bf16[128,1024]{1,0:T(8,128)(2,1)}, bf16[128,1024]{1,0:T(8,128)(2,1)S(1)}, u32[]{:S(2)}, u32[]{:S(2)}) collective-permute-start(bf16[128,1024]{1,0:T(8,128)(2,1)} %copy-done.8), channel_id=1, source_target_pairs={{0,16},{2,18},{4,20},{6,22},{8,24},{10,26},{12,28},{14,30},{16,0},... | collective-permute-start | bytes 786440 | tf_op jit(solution)/shard_map/ppermute | solution.py:276
  43.7 22.5 %collective-permute-start.9 = (bf16[128,1024]{1,0:T(8,128)(2,1)S(1)}, bf16[128,1024]{1,0:T(8,128)(2,1)S(1)}, u32[]{:S(2)}, u32[]{:S(2)}) collective-permute-start(bf16[128,1024]{1,0:T(8,128)(2,1)S(1)} %get-tuple-element.40), channel_id=1, source_target_pairs={{0,16},{2,18},{4,20},{6,22},{8,24},{10,26},{12,28},{14,30},{16,0},... | collective-permute-start | bytes 786440 | tf_op jit(solution)/shard_map/ppermute | solution.py:276
  56.8 9.4 %collective-permute-start = (bf16[4,256,128]{2,1,0:T(8,128)(2,1)S(1)}, bf16[4,256,128]{2,1,0:T(8,128)(2,1)S(1)}, u32[]{:S(2)}, u32[]{:S(2)}) collective-permute-start(bf16[4,256,128]{2,1,0:T(8,128)(2,1)S(1)} %get-tuple-element.30), channel_id=1, source_target_pairs={{0,2},{2,0},{4,6},{6,4},{8,10},{10,8},{12,14},{14,12},{16,18},{18,... | collective-permute-start | bytes 786440 | tf_op jit(solution)/shard_map/ppermute | solution.py:276
  58.2 20.6 %collective-permute-start.7 = (bf16[256,1024]{1,0:T(8,128)(2,1)S(1)}, bf16[256,1024]{1,0:T(8,128)(2,1)S(1)}, u32[]{:S(2)}, u32[]{:S(2)}) collective-permute-start(bf16[256,1024]{1,0:T(8,128)(2,1)S(1)} %collective-permute-done.6.refs_6_), channel_id=1, source_target_pairs={{0,1},{1,0},{2,3},{3,2},{4,5},{5,4},{6,7},{7,6},{8,9},{9,8},{10,11... | collective-permute-start | bytes 1572872 | tf_op jit(solution)/shard_map/ppermute | solution.py:288
  58.2 14.3 %collective-permute-start.1 = (bf16[4,256,128]{2,1,0:T(8,128)(2,1)S(1)}, bf16[4,256,128]{2,1,0:T(8,128)(2,1)S(1)}, u32[]{:S(2)}, u32[]{:S(2)}) collective-permute-start(bf16[4,256,128]{2,1,0:T(8,128)(2,1)S(1)} %get-tuple-element.31), channel_id=1, source_target_pairs={{0,4},{2,6},{4,0},{6,2},{8,12},{10,14},{12,8},{14,10},{16,20},{18,... | collective-permute-start | bytes 786440 | tf_op jit(solution)/shard_map/ppermute | solution.py:276
  62.6 9.9 %collective-permute-start.2 = (bf16[4,256,128]{2,1,0:T(8,128)(2,1)S(1)}, bf16[4,256,128]{2,1,0:T(8,128)(2,1)S(1)}, u32[]{:S(2)}, u32[]{:S(2)}) collective-permute-start(bf16[4,256,128]{2,1,0:T(8,128)(2,1)S(1)} %get-tuple-element.32), channel_id=1, source_target_pairs={{0,6},{2,4},{4,2},{6,0},{8,14},{10,12},{12,10},{14,8},{16,22},{18,... | collective-permute-start | bytes 786440 | tf_op jit(solution)/shard_map/ppermute | solution.py:276
  66.2 9.2 %collective-permute-start.12 = (bf16[128,1024]{1,0:T(8,128)(2,1)S(1)}, bf16[128,1024]{1,0:T(8,128)(2,1)S(1)}, u32[]{:S(2)}, u32[]{:S(2)}) collective-permute-start(bf16[128,1024]{1,0:T(8,128)(2,1)S(1)} %collective-permute-done.8.refs_8_), channel_id=1, source_target_pairs={{0,8},{2,10},{4,12},{6,14},{8,0},{10,2},{12,4},{14,6},{16,24},{18,... | collective-permute-start | bytes 786440 | tf_op jit(solution)/shard_map/ppermute | solution.py:276
  66.2 12.0 %collective-permute-start.13 = (bf16[128,1024]{1,0:T(8,128)(2,1)S(1)}, bf16[128,1024]{1,0:T(8,128)(2,1)S(1)}, u32[]{:S(2)}, u32[]{:S(2)}) collective-permute-start(bf16[128,1024]{1,0:T(8,128)(2,1)S(1)} %collective-permute-done.9.refs_9_), channel_id=1, source_target_pairs={{0,8},{2,10},{4,12},{6,14},{8,0},{10,2},{12,4},{14,6},{16,24},{18,... | collective-permute-start | bytes 786440 | tf_op jit(solution)/shard_map/ppermute | solution.py:276
  72.5 6.6 %collective-permute-start.10 = (bf16[128,1024]{1,0:T(8,128)(2,1)S(1)}, bf16[128,1024]{1,0:T(8,128)(2,1)S(1)}, u32[]{:S(2)}, u32[]{:S(2)}) collective-permute-start(bf16[128,1024]{1,0:T(8,128)(2,1)S(1)} %collective-permute-done.8.refs_8_), channel_id=1, source_target_pairs={{0,1},{1,0},{2,3},{3,2},{4,5},{5,4},{6,7},{7,6},{8,9},{9,8},{10,11... | collective-permute-start | bytes 786440 | tf_op jit(solution)/shard_map/ppermute | solution.py:288
  72.5 8.0 %collective-permute-start.11 = (bf16[128,1024]{1,0:T(8,128)(2,1)S(1)}, bf16[128,1024]{1,0:T(8,128)(2,1)S(1)}, u32[]{:S(2)}, u32[]{:S(2)}) collective-permute-start(bf16[128,1024]{1,0:T(8,128)(2,1)S(1)} %collective-permute-done.9.refs_9_), channel_id=1, source_target_pairs={{0,1},{1,0},{2,3},{3,2},{4,5},{5,4},{6,7},{7,6},{8,9},{9,8},{10,11... | collective-permute-start | bytes 786440 | tf_op jit(solution)/shard_map/ppermute | solution.py:288
  75.4 7.9 %collective-permute-start.14 = (bf16[128,1024]{1,0:T(8,128)(2,1)S(1)}, bf16[128,1024]{1,0:T(8,128)(2,1)S(1)}, u32[]{:S(2)}, u32[]{:S(2)}) collective-permute-start(bf16[128,1024]{1,0:T(8,128)(2,1)S(1)} %collective-permute-done.12.refs_12_), channel_id=1, source_target_pairs={{0,1},{1,0},{2,3},{3,2},{4,5},{5,4},{6,7},{7,6},{8,9},{9,8},{10,11... | collective-permute-start | bytes 786440 | tf_op jit(solution)/shard_map/ppermute | solution.py:288
  78.2 5.1 %collective-permute-start.15 = (bf16[128,1024]{1,0:T(8,128)(2,1)S(1)}, bf16[128,1024]{1,0:T(8,128)(2,1)S(1)}, u32[]{:S(2)}, u32[]{:S(2)}) collective-permute-start(bf16[128,1024]{1,0:T(8,128)(2,1)S(1)} %collective-permute-done.13.refs_13_), channel_id=1, source_target_pairs={{0,1},{1,0},{2,3},{3,2},{4,5},{5,4},{6,7},{7,6},{8,9},{9,8},{10,11... | collective-permute-start | bytes 786440 | tf_op jit(solution)/shard_map/ppermute | solution.py:288
  78.8 10.0 %collective-permute-start.3 = (bf16[4,192,128]{2,1,0:T(8,128)(2,1)S(1)}, bf16[4,192,128]{2,1,0:T(8,128)(2,1)S(1)}, u32[]{:S(2)}, u32[]{:S(2)}) collective-permute-start(bf16[4,192,128]{2,1,0:T(8,128)(2,1)S(1)} %get-tuple-element.33), channel_id=1, source_target_pairs={{0,8},{2,10},{4,12},{6,14},{8,0},{10,2},{12,4},{14,6},{16,24},{18,... | collective-permute-start | bytes 589832 | tf_op jit(solution)/shard_map/ppermute | solution.py:276
  79.1 17.1 %collective-permute-start.4 = (bf16[4,192,128]{2,1,0:T(8,128)(2,1)S(1)}, bf16[4,192,128]{2,1,0:T(8,128)(2,1)S(1)}, u32[]{:S(2)}, u32[]{:S(2)}) collective-permute-start(bf16[4,192,128]{2,1,0:T(8,128)(2,1)S(1)} %get-tuple-element.34), channel_id=1, source_target_pairs={{0,16},{2,18},{4,20},{6,22},{8,24},{10,26},{12,28},{14,30},{16,0},... | collective-permute-start | bytes 589832 | tf_op jit(solution)/shard_map/ppermute | solution.py:276
  80.5 15.8 %copy-start = (bf16[3,1024,512]{2,1,0:T(8,128)(2,1)S(1)}, bf16[3,1024,512]{2,1,0:T(8,128)(2,1)}, u32[]{:S(2)}) copy-start(bf16[3,1024,512]{2,1,0:T(8,128)(2,1)} %refs_7_.1) | copy-start | bytes 9437188
  80.5 15.8 %collective-permute-start.5 = (bf16[4,192,128]{2,1,0:T(8,128)(2,1)S(1)}, bf16[4,192,128]{2,1,0:T(8,128)(2,1)S(1)}, u32[]{:S(2)}, u32[]{:S(2)}) collective-permute-start(bf16[4,192,128]{2,1,0:T(8,128)(2,1)S(1)} %get-tuple-element.35), channel_id=1, source_target_pairs={{0,24},{2,26},{4,28},{6,30},{8,16},{10,18},{12,20},{14,22},{16,8},... | collective-permute-start | bytes 589832 | tf_op jit(solution)/shard_map/ppermute | solution.py:276
  85.5 12.4 %collective-permute-start.17 = (bf16[256,512]{1,0:T(8,128)(2,1)S(1)}, bf16[256,512]{1,0:T(8,128)(2,1)S(1)}, u32[]{:S(2)}, u32[]{:S(2)}) collective-permute-start(bf16[256,512]{1,0:T(8,128)(2,1)S(1)} %get-tuple-element.46), channel_id=1, source_target_pairs={{0,2},{2,0},{4,6},{6,4},{8,10},{10,8},{12,14},{14,12},{16,18},{18,... | collective-permute-start | bytes 786440 | tf_op jit(solution)/shard_map/ppermute | solution.py:276
  87.3 13.2 %collective-permute-start.18 = (bf16[256,512]{1,0:T(8,128)(2,1)S(1)}, bf16[256,512]{1,0:T(8,128)(2,1)S(1)}, u32[]{:S(2)}, u32[]{:S(2)}) collective-permute-start(bf16[256,512]{1,0:T(8,128)(2,1)S(1)} %get-tuple-element.47), channel_id=1, source_target_pairs={{0,4},{2,6},{4,0},{6,2},{8,12},{10,14},{12,8},{14,10},{16,20},{18,... | collective-permute-start | bytes 786440 | tf_op jit(solution)/shard_map/ppermute | solution.py:276
  88.8 11.7 %collective-permute-start.19 = (bf16[256,512]{1,0:T(8,128)(2,1)S(1)}, bf16[256,512]{1,0:T(8,128)(2,1)S(1)}, u32[]{:S(2)}, u32[]{:S(2)}) collective-permute-start(bf16[256,512]{1,0:T(8,128)(2,1)S(1)} %get-tuple-element.48), channel_id=1, source_target_pairs={{0,6},{2,4},{4,2},{6,0},{8,14},{10,12},{12,10},{14,8},{16,22},{18,... | collective-permute-start | bytes 786440 | tf_op jit(solution)/shard_map/ppermute | solution.py:276
  97.9 14.7 %collective-permute-start.16 = (f32[256,512]{1,0:T(8,128)S(1)}, f32[256,512]{1,0:T(8,128)S(1)}, u32[]{:S(2)}, u32[]{:S(2)}) collective-permute-start(f32[256,512]{1,0:T(8,128)S(1)} %get-tuple-element.45), channel_id=1, source_target_pairs={{0,1},{1,0},{2,3},{3,2},{4,5},{5,4},{6,7},{7,6},{8,9},{9,8},{10,11... | collective-permute-start | bytes 1572872 | tf_op jit(solution)/shard_map/ppermute | solution.py:288
  101.3 4.5 %collective-permute-start.20 = (bf16[64,512]{1,0:T(8,128)(2,1)S(1)}, bf16[64,512]{1,0:T(8,128)(2,1)S(1)}, u32[]{:S(2)}, u32[]{:S(2)}) collective-permute-start(bf16[64,512]{1,0:T(8,128)(2,1)S(1)} %get-tuple-element.50), channel_id=1, source_target_pairs={{0,8},{2,10},{4,12},{6,14},{8,0},{10,2},{12,4},{14,6},{16,24},{18,... | collective-permute-start | bytes 196616 | tf_op jit(solution)/shard_map/ppermute | solution.py:276
  103.0 8.1 %collective-permute-start.21 = (bf16[64,512]{1,0:T(8,128)(2,1)S(1)}, bf16[64,512]{1,0:T(8,128)(2,1)S(1)}, u32[]{:S(2)}, u32[]{:S(2)}) collective-permute-start(bf16[64,512]{1,0:T(8,128)(2,1)S(1)} %get-tuple-element.51), channel_id=1, source_target_pairs={{0,16},{2,18},{4,20},{6,22},{8,24},{10,26},{12,28},{14,30},{16,0},... | collective-permute-start | bytes 196616 | tf_op jit(solution)/shard_map/ppermute | solution.py:276
  104.3 6.8 %collective-permute-start.22 = (bf16[64,512]{1,0:T(8,128)(2,1)S(1)}, bf16[64,512]{1,0:T(8,128)(2,1)S(1)}, u32[]{:S(2)}, u32[]{:S(2)}) collective-permute-start(bf16[64,512]{1,0:T(8,128)(2,1)S(1)} %get-tuple-element.52), channel_id=1, source_target_pairs={{0,24},{2,26},{4,28},{6,30},{8,16},{10,18},{12,20},{14,22},{16,8},... | collective-permute-start | bytes 196616 | tf_op jit(solution)/shard_map/ppermute | solution.py:276
  (3 other events, 2.6 us)

commit v3 on v2

--- a/solution.py
+++ b/solution.py
@@ -24,14 +24,11 @@
     return lax.dot_general(a, b, (((1,), (1,)), ((), ())), preferred_element_type=F32)
 
 
-def call(kernel, name, outs, args, scratch=(), mib=16, us=1, after=(), scalars=0, load=False):
+def call(kernel, name, outs, args, scratch=(), mib=16, us=1, after=(), scalars=0, inputs=None, sems=0):
     args, after = list(args), list(after)
     specs = [pl.BlockSpec(memory_space=pltpu.SMEM)] * scalars
     for arg in args[scalars:]:
-        if load:
-            specs.append(pl.BlockSpec(arg.shape, lambda i, rank=arg.ndim: (0,) * rank))
-        else:
-            specs.append(pl.BlockSpec(memory_space=pltpu.VMEM))
+        specs.append(pl.BlockSpec(memory_space=inputs or pltpu.VMEM))
     out_specs = [pl.BlockSpec(memory_space=pltpu.VMEM)] * len(outs)
 
     def run(pos_ref, *refs):
@@ -40,46 +37,65 @@
     return lambda pos: pl.pallas_call(
         run,
         out_shape=[jax.ShapeDtypeStruct(dims, dtype) for dims, dtype in outs],
-        grid=(1,) if load else (),
         in_specs=[pl.BlockSpec(memory_space=pltpu.SMEM)] + specs + [pl.BlockSpec(memory_space=pl.ANY)] * len(after),
         out_specs=out_specs,
-        scratch_shapes=[pltpu.VMEM(dims, dtype) for dims, dtype in scratch],
+        scratch_shapes=[pltpu.VMEM(dims, dtype) for dims, dtype in scratch] + [pltpu.SemaphoreType.DMA(())] * sems,
         compiler_params=pltpu.CompilerParams(vmem_limit_bytes=mib * MIB),
         cost_estimate=pl.CostEstimate(flops=int(us * 1.1e9), bytes_accessed=MIB, transcendentals=0),
         name=name,
     )(pos, *args, *after)
 
 
-def pack_kernel(pos_ref, q_ref, k_ref, v_ref, d_ref, w_ref, out_ref):
-    for scene in range(q_ref.shape[0]):
-        arrays = (
-            (q_ref[scene, 0].T * HD**-0.5).astype(BF),
-            k_ref[scene, 0].T,
-            v_ref[scene, 0].T,
-            mul_nt(w_ref[...], d_ref[scene, 0]).astype(BF),
-        )
+def pack_kernel(pos_ref, *refs):
+    far, out_ref, near, sems = refs[:5], refs[5], refs[6:11], refs[11:]
+    copies = [pltpu.make_async_copy(*trio) for trio in zip(far, near, sems)]
+    for copy in copies:
+        copy.start()
+    q_ref, k_ref, v_ref, d_ref, w_ref = near
+    scenes = range(q_ref.shape[0])
+
+    def put(n, scene, arr):
         for view in range(out_ref.shape[0]):
             plane, quad = view // QUAD, view % QUAD
             if quad // 2 == scene:
                 row = (2 * plane + quad % 2) * HD
-                for n, arr in enumerate(arrays):
-                    out_ref[view, n * HD : (n + 1) * HD] = arr[row : row + HD]
-
-
-def fetch_kernel(pos_ref, t_ref, d_ref, both, t_out, d_out):
-    core = pos_ref[2]
-    both[:LANE] = t_out[...] = t_ref[core, 0]
-    both[LANE:] = d_out[...] = d_ref[core, 0]
+                out_ref[view, n * HD : (n + 1) * HD] = arr[row : row + HD]
+
+    copies[0].wait()
+    for scene in scenes:
+        put(0, scene, (q_ref[scene, 0].T * HD**-0.5).astype(BF))
+    copies[1].wait()
+    for scene in scenes:
+        put(1, scene, k_ref[scene, 0].T)
+    copies[2].wait()
+    for scene in scenes:
+        put(2, scene, v_ref[scene, 0].T)
+    copies[3].wait()
+    copies[4].wait()
+    for scene in scenes:
+        put(3, scene, mul_nt(w_ref[...], d_ref[scene, 0]).astype(BF))
+
+
+def fetch_kernel(pos_ref, t_ref, d_ref, both, t_out, d_out, *sems):
+    copies = [
+        pltpu.make_async_copy(ref.at[pos_ref[2], 0], out, sem)
+        for ref, out, sem in zip((t_ref, d_ref), (t_out, d_out), sems)
+    ]
+    for n, (copy, out) in enumerate(zip(copies, (t_out, d_out))):
+        copy.start()
+    for n, (copy, out) in enumerate(zip(copies, (t_out, d_out))):
+        copy.wait()
+        both[n * LANE : (n + 1) * LANE] = out[...]
 
 
 def gate(value, after):
     return lax.optimization_barrier((value, after))[0]
 
 
-def cameras_of(pos_ref, planes):
-    for j in range(QUAD):
-        for k in range(planes):
-            yield j, k, (pos_ref[0] ^ k) * QUAD + (pos_ref[1] ^ j)
+def places(refs, mine):
+    if len(refs) == 1:
+        return [(refs[0].at[n], n) for n in range(refs[0].shape[0])]
+    return [(ref, mine ^ n) for n, ref in enumerate(refs)]
 
 
 def rows_of(cam):
@@ -103,7 +119,7 @@
 
 
 def attend_kernel(reach, pos_ref, near_ref, count_ref, in_ref, *refs):
-    outs, (k_row, v_row, k_col, v_col, dk_acc, dv_acc, s_buf, p_buf, d_buf, att_buf, dq_buf) = refs[:QUAD], refs[QUAD:]
+    outs, (k_row, v_row, k_col, v_col, dk_acc, dv_acc, s_buf, p_buf, d_buf, att_buf, dq_buf) = refs[:4], refs[4:]
     cameras = in_ref.shape[0]
     span = 2 * reach + 2
     for cam in range(cameras):
@@ -166,34 +182,29 @@
     lax.fori_loop(0, cameras // 2, step, 0)
     fold(dk_acc, cameras, reach)
     fold(dv_acc, cameras, reach)
-    for j, k, cam in cameras_of(pos_ref, cameras // QUAD):
-        rows = rows_of(cam + reach)
-        outs[j][k, :HD] = att_buf[cam]
-        outs[j][k, HD : 2 * HD] = dv_acc[rows, :].T.astype(BF)
-        outs[j][k, 2 * HD : 3 * HD] = dq_buf[cam]
-        outs[j][k, 3 * HD :] = dk_acc[rows, :].T.astype(BF)
-
-
-def hand_out(wide, outs, planes, pos_ref):
-    part = wide.shape[0] // (QUAD * planes)
-    for j in range(QUAD):
-        for p in range(planes):
-            rows = pl.ds(pl.multiple_of((p * QUAD + (pos_ref[1] ^ j)) * part, part), part)
-            outs[j][p * part : (p + 1) * part] = wide[rows, :].astype(BF)
+    for ref, quad in places(outs, pos_ref[1]):
+        for plane in range(cameras // QUAD):
+            cam = plane * QUAD + quad
+            rows = rows_of(cam + reach)
+            ref[plane, :HD] = att_buf[cam]
+            ref[plane, HD : 2 * HD] = dv_acc[rows, :].T.astype(BF)
+            ref[plane, 2 * HD : 3 * HD] = dq_buf[cam]
+            ref[plane, 3 * HD :] = dk_acc[rows, :].T.astype(BF)
 
 
 def weights_kernel(planes, pos_ref, *refs):
-    blocks, (tok_ref, d_ref), far, outs = refs[:QUAD], refs[QUAD : QUAD + 2], refs[QUAD + 2 : -9], refs[-9:-5]
+    blocks, (tok_ref, d_ref), far, outs = refs[:4], refs[4:6], refs[6:16], refs[16:-5]
     left, left_o, tok, d_o, wide = refs[-5:]
-    quad, core = pos_ref[1], pos_ref[2]
-    for j in range(QUAD):
-        scene, half = (quad ^ j) // 2, (quad ^ j) % 2
+    plane, core = pos_ref[0], pos_ref[2]
+    for ref, quad in places(blocks, pos_ref[1]):
+        scene, half = quad // 2, quad % 2
         for k in range(planes):
             at = rows_of(2 * k + (scene ^ core))
-            left_o[pl.ds(pl.multiple_of(half * HD, HD), HD), at] = blocks[j][k, :HD]
+            block = ref.at[plane ^ k]
+            left_o[pl.ds(pl.multiple_of(half * HD, HD), HD), at] = block[:HD]
             for n in range(3):
                 row = pl.multiple_of((2 * n + half) * HD, HD)
-                left[pl.ds(row, HD), at] = blocks[j][k, (n + 1) * HD : (n + 2) * HD]
+                left[pl.ds(row, HD), at] = block[(n + 1) * HD : (n + 2) * HD]
     for n in range(2):
         at = slice(n * LANE, (n + 1) * LANE)
         tok[at] = tok_ref[core ^ n, 0]
@@ -203,29 +214,33 @@
         tok[at] = ref[:LANE]
         d_o[at] = ref[LANE:]
     for n, ref in enumerate(far[2:]):
-        at = slice((n // 2 + 4) * LANE, (n // 2 + 5) * LANE)
-        (d_o if n % 2 else tok)[at] = ref[...]
+        at = slice((n % 4 + 4) * LANE, (n % 4 + 5) * LANE)
+        (d_o if n // 4 else tok)[at] = ref[...]
     wide[:, : 6 * HD] = mul(left[...], tok[...]).T
     wide[:, 6 * HD :] = mul(left_o[...], d_o[...]).T
-    hand_out(wide, outs, planes, pos_ref)
+    part = wide.shape[0] // (QUAD * planes)
+    for ref, quad in places(outs, pos_ref[1]):
+        for p in range(planes):
+            rows = pl.ds(pl.multiple_of((p * QUAD + quad) * part, part), part)
+            ref[p * part : (p + 1) * part] = wide[rows, :].astype(BF)
 
 
 def sum_kernel(planes, pos_ref, *refs):
-    terms, outs, total = refs[:QUAD], refs[QUAD:-1], refs[-1]
-    acc = terms[0][...].astype(F32)
-    for term in terms[1:]:
-        acc = acc + term[...].astype(F32)
+    terms, outs, total = refs[:4], refs[4:-1], refs[-1]
+    acc = None
+    for ref, _ in places(terms, 0):
+        acc = ref[...].astype(F32) if acc is None else acc + ref[...].astype(F32)
     total[...] = acc
     part = total.shape[0] // planes
-    for k in range(planes):
-        rows = pl.ds(pl.multiple_of((pos_ref[0] ^ k) * part, part), part)
-        outs[k][...] = total[rows, :].astype(BF)
+    for ref, plane in places(outs, pos_ref[0]):
+        rows = pl.ds(pl.multiple_of(plane * part, part), part)
+        ref[...] = total[rows, :].astype(BF)
 
 
 def finish_kernel(planes, pos_ref, *refs):
-    terms, (w_ref, o_ref, buf) = refs[:planes], refs[planes:]
-    for k in range(planes):
-        buf[pos_ref[0] ^ k] = terms[k][...].astype(F32)
+    terms, (w_ref, o_ref, buf) = refs[:4], refs[4:]
+    for ref, plane in places(terms, pos_ref[0]):
+        buf[plane] = ref[...].astype(F32)
     two = 2 * HD
     for p in range(planes):
         cols = slice(p * two, (p + 1) * two)
@@ -235,21 +250,34 @@
 
 
 def turn_kernel(planes, pos_ref, *refs):
-    for k in range(1, planes):
-        for j in range(QUAD):
-            refs[QUAD + k - 1][j] = refs[j][k, HD:]
+    blocks, outs = refs[:4], refs[4:]
+    for ref, quad in places(blocks, pos_ref[1]):
+        for n in range(planes):
+            if len(outs) == 1:
+                outs[0][n, quad] = ref[n, HD:]
+            elif n:
+                outs[n - 1][quad] = ref[pos_ref[0] ^ n, HD:]
 
 
 def inputs_kernel(planes, pos_ref, *refs):
-    own, far, (w_ref, mine, theirs, turned) = refs[:QUAD], refs[QUAD : QUAD + planes - 1], refs[QUAD + planes - 1 :]
-    plane, quad, core = pos_ref[0], pos_ref[1], pos_ref[2]
-    for k in range(planes):
-        for j in range(QUAD):
-            block = own[j][0, HD:] if k == 0 else far[k - 1][j]
-            scene, half = (quad ^ j) // 2, (quad ^ j) % 2
-            row = pl.ds(pl.multiple_of((2 * (plane ^ k) + half) * HD, HD), HD)
-            for place, n in enumerate((2, 0, 1)):
-                turned[scene, n, row] = block[place * HD : (place + 1) * HD]
+    blocks, far, (w_ref, mine, theirs, turned) = refs[:4], refs[4:7], refs[7:]
+    plane, core = pos_ref[0], pos_ref[2]
+
+    def put(block, home, quad):
+        row = pl.ds(pl.multiple_of((2 * home + quad % 2) * HD, HD), HD)
+        for place, n in enumerate((2, 0, 1)):
+            turned[quad // 2, n, row] = block[place * HD : (place + 1) * HD]
+
+    if len(far) == 1:
+        for home in range(planes):
+            for quad in range(QUAD):
+                put(far[0][home, quad], home, quad)
+    else:
+        for ref, quad in places(blocks, pos_ref[1]):
+            put(ref[plane, HD:], plane, quad)
+        for k, ref in enumerate(far, 1):
+            for quad in range(QUAD):
+                put(ref[quad], plane ^ k, quad)
     left = [jnp.concatenate([turned[scene, j].T for scene in range(2)], axis=0) for j in range(3)]
     half = w_ref.shape[1] // 2
     for ref, who in ((theirs, 1 - core), (mine, core)):
@@ -276,9 +304,15 @@
         return lax.ppermute(value, "view", pairs)
 
     def over_plane(values):
+        if len(values) == 1:
+            groups = [[p * QUAD + j for j in range(QUAD)] for p in range(planes)]
+            return [lax.all_to_all(values[0], "view", 0, 0, axis_index_groups=groups, tiled=True)]
         return [values[0]] + [along(values[j], [(i, i ^ j) for i in range(cameras)]) for j in range(1, QUAD)]
 
     def over_column(values, first=0):
+        if len(values) == 1 and values[0].shape[0] == planes:
+            groups = [[p * QUAD + j for p in range(planes)] for j in range(QUAD)]
+            return [lax.all_to_all(values[0], "view", 0, 0, axis_index_groups=groups, tiled=True)]
         return [
             value if k == 0 else along(value, [(i, i ^ (k * QUAD)) for i in range(cameras)])
             for k, value in enumerate(values, first)
@@ -287,54 +321,51 @@
     def other_core(value):
         return lax.ppermute(value, "head", [(0, 1), (1, 0)])
 
-    piece = ((rows, model), BF)
-    both, tok, out = call(fetch_kernel, "fetch", [((2 * rows, model), BF), piece, piece], (tokens, d_out))(pos)
-
     arrays = (queries, keys, values, d_out, w_out)
-    packed = call(pack_kernel, "pack", [((cameras, 4 * HD, rows), BF)], arrays, load=True)(pos)[0]
+    packed = call(
+        pack_kernel, "pack", [((cameras, 4 * HD, rows), BF)], arrays, [(arr.shape, BF) for arr in arrays],
+        56, inputs=pl.ANY, sems=len(arrays),
+    )(pos)[0]
     packed = lax.all_to_all(packed, "view", 0, 0, tiled=True)
 
-    block = ((planes, 4 * HD, rows), BF)
+    own = call(fetch_kernel, "fetch", [((2 * rows, model), BF), ((rows, model), BF), ((rows, model), BF)], (tokens, d_out), (), 40, inputs=pl.ANY, sems=2)(pos)
+    near = over_column([own[0]], 1)[0]
+    column = [near, other_core(near)]
+
     blocks = call(
-        functools.partial(attend_kernel, reach), "attend", [block] * QUAD, (neighbours, degrees, packed),
+        functools.partial(attend_kernel, reach), "attend", [((planes, 4 * HD, rows), BF)] * QUAD, (neighbours, degrees, packed),
         [
             ((ext, HD), BF), ((ext, HD), BF), ((HD, ext), BF), ((HD, ext), BF), ((ext, HD), F32), ((ext, HD), F32),
             ((span, rows, 2 * rows), F32), ((span * rows, 2 * rows), BF), ((span * rows, 2 * rows), BF),
             ((cameras, HD, rows), BF), ((cameras, HD, rows), BF),
         ],
-        32, 13, scalars=2,
+        32, 5, scalars=2, after=[],
     )(pos)
     done = blocks[0]
     blocks = over_plane(blocks)
-    near = over_column([both], 1)[0]
-    pieces = [over_column([gate(tok, packed)], 2)[0], over_column([gate(out, packed)], 2)[0]]
-    pieces += [over_column([gate(value, done)], 1)[0] for value in pieces]
-    column = []
-    for value in [near] + pieces:
-        column += [value, other_core(value)]
-    column = column[:2] + [column[2 + n] for n in (0, 2, 1, 3, 4, 6, 5, 7)]
+    first = over_column([gate(own[1], packed)], 2)[0]
+    second = over_column([gate(own[2], packed)], 2)[0]
+    for far in (first, second):
+        column += [far, other_core(far)]
+        far = over_column([gate(far, done)], 1)[0]
+        column += [far, other_core(far)]
 
     depth = 2 * planes * rows
-    args = blocks + [tokens, d_out] + column
     terms = call(
-        functools.partial(weights_kernel, planes), "weights", [((model // QUAD, 8 * HD), BF)] * QUAD, args,
+        functools.partial(weights_kernel, planes), "weights", [((model // QUAD, 8 * HD), BF)] * QUAD, blocks + [tokens, d_out] + column,
         [((6 * HD, depth), BF), ((2 * HD, depth), BF), ((depth, model), BF), ((depth, model), BF), ((model, 8 * HD), F32)],
         32, 3,
     )(pos)
     started = terms[:1]
     terms = call(
-        functools.partial(sum_kernel, planes), "plane_sum", [((part, 8 * HD), BF)] * planes, over_plane(terms),
-        [((model // QUAD, 8 * HD), F32)],
+        functools.partial(sum_kernel, planes), "plane_sum", [((part, 8 * HD), BF)] * planes, over_plane(terms), [((model // QUAD, 8 * HD), F32)],
     )(pos)
-    terms = over_column(terms)
     d_wqkv, d_wo = call(
-        functools.partial(finish_kernel, planes), "finish", [((3, part, width), F32), ((part, width), F32)], terms,
-        [((planes, part, 8 * HD), F32)],
+        functools.partial(finish_kernel, planes), "finish", [((3, part, width), F32), ((part, width), F32)],
+        over_column(terms), [((planes, part, 8 * HD), F32)],
     )(pos)
 
-    grads = call(
-        functools.partial(turn_kernel, planes), "turn", [((QUAD, 3 * HD, rows), BF)] * (planes - 1), blocks
-    )(pos)
+    grads = call(functools.partial(turn_kernel, planes), "turn", [((QUAD, 3 * HD, rows), BF)] * (planes - 1), blocks, after=())(pos)
     args = blocks + over_column(grads, 1) + [w_qkv]
     mine, theirs = call(
         functools.partial(inputs_kernel, planes), "inputs", [((scenes * rows, model // 2), F32)] * 2, args,

time: 114 us -> 111 us (0.974)
  local copies, waits for them, and re-layouts: 5.9 us -> 0.8 us
  Pallas kernels: 22.4 us -> 24.4 us
    unnamed x23 -> x15, local copies, waits for them, and re-layouts: 5.9 us -> 0.8 us
    pallas_call x8, Pallas kernels: 22.4 us -> 24.4 us  [call(): pl.pallas_call(run, out_shape=[jax.ShapeDtypeStruct(dims, dtype) for dims...]
where the time goes in v3:
time: 111 us
  waiting for transfers between devices  50.7 us (46%)
  starting transfers between devices  32.5 us (29%)
  Pallas kernels  24.4 us (22%)
  other arithmetic  1.44 us (1%)
    ppermute x17, waiting for transfers between devices, along(): return lax.ppermute(value, 'view', pairs)  29.6 us
    pallas_call x8, Pallas kernels, call(): pl.pallas_call(run, out_shape=[jax.ShapeDtypeStruct(dims, dtype) for dims...  24.4 us
    ppermute x17, starting transfers between devices, along(): return lax.ppermute(value, 'view', pairs)  23.6 us
    all_to_all x1, waiting for transfers between devices, split_body(): packed = lax.all_to_all(packed, 'view', 0, 0, tiled=True)  21.1 us
    all_to_all x1, starting transfers between devices, split_body(): packed = lax.all_to_all(packed, 'view', 0, 0, tiled=True)  8.33 us
  transfers between devices with their start and end apart: 24, of which 10 were waited for; matrix products, arithmetic and copies ran while one was open for 0% of the time, Pallas kernels for 18%

profile of v3, /device:TPU:0, one launch (start us, length us, event | category | flops | bytes accessed | tf_op | source)
XLA Modules:
  0.0 110.6 jit_solution(16694138084744839048)
XLA Ops:
  1.3 4.1 %pack.1 = bf16[16,256,128]{2,1,0:T(8,128)(2,1)} custom-call(s32[3]{0:T(128)} %pad_add_fusion.pos_ref, bf16[2,1,128,512]{3,2,1,0:T(8,128)(2,1)} %refs_0_.3, bf16[2,1,128,512]{3,2,1,0:T(8,128)(2,1)} %refs_1_.3, bf16[2,1,128,512]{3,2,1,0:T(8,128)(2,1)} %refs_2_.1, bf16[2,1,128,1024]{3,2,1,0:T(8,128)(2,1)} %refs_5_.1, bf16[512,1024]{1,0:T(8,128)(2,1)} %refs_4_.2), custom_call_target="tpu_custom_call" | custom-call | flops 1100000000 | bytes 1048576 | tf_op jit(solution)/shard_map/pack/pallas_call | solution.py:37
  5.5 8.3 %all-to-all-start = ((bf16[16,256,128]{2,1,0:T(8,128)(2,1)}), bf16[16,256,128]{2,1,0:T(8,128)(2,1)S(1)}, u32[]{:S(2)}, u32[]{:S(2)}) async-start(bf16[16,256,128]{2,1,0:T(8,128)(2,1)} %pack.1), calls=%async_computation | async-start | bytes 2097152 | tf_op jit(solution)/shard_map/all_to_all | solution.py:329
  14.5 0.7 copy-done.4
  15.2 1.9 %collective-permute-start.6 = (bf16[256,1024]{1,0:T(8,128)(2,1)S(1)}, bf16[256,1024]{1,0:T(8,128)(2,1)S(1)}, u32[]{:S(2)}, u32[]{:S(2)}) collective-permute-start(bf16[256,1024]{1,0:T(8,128)(2,1)S(1)} %get-tuple-element.36), channel_id=1, source_target_pairs={{0,8},{2,10},{4,12},{6,14},{8,0},{10,2},{12,4},{14,6},{16,24},{18,... | collective-permute-start | bytes 1572872 | tf_op jit(solution)/shard_map/ppermute | solution.py:304
  17.2 21.1 %all-to-all-done.refs_2_ = bf16[16,256,128]{2,1,0:T(8,128)(2,1)S(1)} async-done(((bf16[16,256,128]{2,1,0:T(8,128)(2,1)}), bf16[16,256,128]{2,1,0:T(8,128)(2,1)S(1)}, u32[]{:S(2)}, u32[]{:S(2)}) %all-to-all-start) | async-done | bytes 1048608 | tf_op jit(solution)/shard_map/all_to_all | solution.py:329
  38.3 2.7 %collective-permute-start.8 = (bf16[128,1024]{1,0:T(8,128)(2,1)}, bf16[128,1024]{1,0:T(8,128)(2,1)S(1)}, u32[]{:S(2)}, u32[]{:S(2)}) collective-permute-start(bf16[128,1024]{1,0:T(8,128)(2,1)} %copy-done.4), channel_id=1, source_target_pairs={{0,16},{2,18},{4,20},{6,22},{8,24},{10,26},{12,28},{14,30},{16,0},... | collective-permute-start | bytes 786440 | tf_op jit(solution)/shard_map/ppermute | solution.py:304
  41.2 12.9 %attend.1 = (bf16[4,256,128]{2,1,0:T(8,128)(2,1)S(1)}, bf16[4,256,128]{2,1,0:T(8,128)(2,1)S(1)}, bf16[4,256,128]{2,1,0:T(8,128)(2,1)S(1)}, bf16[4,256,128]{2,1,0:T(8,128)(2,1)S(1)}) custom-call(s32[3]{0:T(128)S(1)} %copy-done, s32[16,8]{1,0:T(8,128)S(1)} %copy.12.refs_0_, s32[16]{0:T(128)S(1)} %copy-done.5, bf16[16,256,128]{2,1,0:T(8,128)(2,1)S(1)} %all-to-all-done.refs_2_), custom_call_target="tpu_custom_call" | custom-call | flops 5500000256 | bytes 1048576 | tf_op jit(solution)/shard_map/attend/pallas_call | solution.py:37
  54.1 1.3 %collective-permute-start = (bf16[4,256,128]{2,1,0:T(8,128)(2,1)S(1)}, bf16[4,256,128]{2,1,0:T(8,128)(2,1)S(1)}, u32[]{:S(2)}, u32[]{:S(2)}) collective-permute-start(bf16[4,256,128]{2,1,0:T(8,128)(2,1)S(1)} %get-tuple-element.30), channel_id=1, source_target_pairs={{0,2},{2,0},{4,6},{6,4},{8,10},{10,8},{12,14},{14,12},{16,18},{18,... | collective-permute-start | bytes 786440 | tf_op jit(solution)/shard_map/ppermute | solution.py:304
  55.5 1.3 %collective-permute-start.1 = (bf16[4,256,128]{2,1,0:T(8,128)(2,1)S(1)}, bf16[4,256,128]{2,1,0:T(8,128)(2,1)S(1)}, u32[]{:S(2)}, u32[]{:S(2)}) collective-permute-start(bf16[4,256,128]{2,1,0:T(8,128)(2,1)S(1)} %get-tuple-element.31), channel_id=1, source_target_pairs={{0,4},{2,6},{4,0},{6,2},{8,12},{10,14},{12,8},{14,10},{16,20},{18,... | collective-permute-start | bytes 786440 | tf_op jit(solution)/shard_map/ppermute | solution.py:304
  56.7 3.1 %collective-permute-done.8.refs_8_ = bf16[128,1024]{1,0:T(8,128)(2,1)S(1)} collective-permute-done((bf16[128,1024]{1,0:T(8,128)(2,1)}, bf16[128,1024]{1,0:T(8,128)(2,1)S(1)}, u32[]{:S(2)}, u32[]{:S(2)}) %collective-permute-start.8) | collective-permute-done | bytes 262176 | tf_op jit(solution)/shard_map/ppermute | solution.py:304
  59.9 1.8 %collective-permute-start.2 = (bf16[4,256,128]{2,1,0:T(8,128)(2,1)S(1)}, bf16[4,256,128]{2,1,0:T(8,128)(2,1)S(1)}, u32[]{:S(2)}, u32[]{:S(2)}) collective-permute-start(bf16[4,256,128]{2,1,0:T(8,128)(2,1)S(1)} %get-tuple-element.32), channel_id=1, source_target_pairs={{0,6},{2,4},{4,2},{6,0},{8,14},{10,12},{12,10},{14,8},{16,22},{18,... | collective-permute-start | bytes 786440 | tf_op jit(solution)/shard_map/ppermute | solution.py:304
  61.7 1.8 %collective-permute-done.12.refs_12_ = bf16[128,1024]{1,0:T(8,128)(2,1)S(1)} collective-permute-done((bf16[128,1024]{1,0:T(8,128)(2,1)S(1)}, bf16[128,1024]{1,0:T(8,128)(2,1)S(1)}, u32[]{:S(2)}, u32[]{:S(2)}) %collective-permute-start.12) | collective-permute-done | bytes 262176 | tf_op jit(solution)/shard_map/ppermute | solution.py:304
  63.5 2.0 %collective-permute-start.14 = (bf16[128,1024]{1,0:T(8,128)(2,1)S(1)}, bf16[128,1024]{1,0:T(8,128)(2,1)S(1)}, u32[]{:S(2)}, u32[]{:S(2)}) collective-permute-start(bf16[128,1024]{1,0:T(8,128)(2,1)S(1)} %collective-permute-done.12.refs_12_), channel_id=1, source_target_pairs={{0,8},{2,10},{4,12},{6,14},{8,0},{10,2},{12,4},{14,6},{16,24},{18,... | collective-permute-start | bytes 786440 | tf_op jit(solution)/shard_map/ppermute | solution.py:304
  65.5 4.3 %collective-permute-done.1.refs_2_ = bf16[4,256,128]{2,1,0:T(8,128)(2,1)S(1)} collective-permute-done((bf16[4,256,128]{2,1,0:T(8,128)(2,1)S(1)}, bf16[4,256,128]{2,1,0:T(8,128)(2,1)S(1)}, u32[]{:S(2)}, u32[]{:S(2)}) %collective-permute-start.1) | collective-permute-done | bytes 262176 | tf_op jit(solution)/shard_map/ppermute | solution.py:304
  70.3 2.3 %collective-permute-done.10.refs_10_ = bf16[128,1024]{1,0:T(8,128)(2,1)S(1)} collective-permute-done((bf16[128,1024]{1,0:T(8,128)(2,1)S(1)}, bf16[128,1024]{1,0:T(8,128)(2,1)S(1)}, u32[]{:S(2)}, u32[]{:S(2)}) %collective-permute-start.10) | collective-permute-done | bytes 262176 | tf_op jit(solution)/shard_map/ppermute | solution.py:304
  72.7 2.8 %collective-permute-done.14.refs_14_ = bf16[128,1024]{1,0:T(8,128)(2,1)S(1)} collective-permute-done((bf16[128,1024]{1,0:T(8,128)(2,1)S(1)}, bf16[128,1024]{1,0:T(8,128)(2,1)S(1)}, u32[]{:S(2)}, u32[]{:S(2)}) %collective-permute-start.14) | collective-permute-done | bytes 262176 | tf_op jit(solution)/shard_map/ppermute | solution.py:304
  76.4 1.3 %collective-permute-start.4 = (bf16[4,192,128]{2,1,0:T(8,128)(2,1)S(1)}, bf16[4,192,128]{2,1,0:T(8,128)(2,1)S(1)}, u32[]{:S(2)}, u32[]{:S(2)}) collective-permute-start(bf16[4,192,128]{2,1,0:T(8,128)(2,1)S(1)} %get-tuple-element.34), channel_id=1, source_target_pairs={{0,16},{2,18},{4,20},{6,22},{8,24},{10,26},{12,28},{14,30},{16,0},... | collective-permute-start | bytes 589832 | tf_op jit(solution)/shard_map/ppermute | solution.py:304
  77.8 2.8 %collective-permute-start.5 = (bf16[4,192,128]{2,1,0:T(8,128)(2,1)S(1)}, bf16[4,192,128]{2,1,0:T(8,128)(2,1)S(1)}, u32[]{:S(2)}, u32[]{:S(2)}) collective-permute-start(bf16[4,192,128]{2,1,0:T(8,128)(2,1)S(1)} %get-tuple-element.35), channel_id=1, source_target_pairs={{0,24},{2,26},{4,28},{6,30},{8,16},{10,18},{12,20},{14,22},{16,8},... | collective-permute-start | bytes 589832 | tf_op jit(solution)/shard_map/ppermute | solution.py:304
  80.5 2.3 %weights.1 = (bf16[256,512]{1,0:T(8,128)(2,1)S(1)}, bf16[256,512]{1,0:T(8,128)(2,1)S(1)}, bf16[256,512]{1,0:T(8,128)(2,1)S(1)}, bf16[256,512]{1,0:T(8,128)(2,1)S(1)}) custom-call(s32[3]{0:T(128)S(1)} %copy-done, bf16[4,256,128]{2,1,0:T(8,128)(2,1)S(1)} %get-tuple-element.29.refs_0_, bf16[4,256,128]{2,1,0:T(8,128)(2,1)S(1)} %collective-permute-done.refs_1_, ...), custom_call_target="tpu_custom_call" | custom-call | flops 3300000000 | bytes 1048576 | tf_op jit(solution)/shard_map/weights/pallas_call | solution.py:37
  82.8 1.8 %collective-permute-start.17 = (bf16[256,512]{1,0:T(8,128)(2,1)S(1)}, bf16[256,512]{1,0:T(8,128)(2,1)S(1)}, u32[]{:S(2)}, u32[]{:S(2)}) collective-permute-start(bf16[256,512]{1,0:T(8,128)(2,1)S(1)} %get-tuple-element.46), channel_id=1, source_target_pairs={{0,2},{2,0},{4,6},{6,4},{8,10},{10,8},{12,14},{14,12},{16,18},{18,... | collective-permute-start | bytes 786440 | tf_op jit(solution)/shard_map/ppermute | solution.py:304
  84.6 1.5 %collective-permute-done.3.refs_4_ = bf16[4,192,128]{2,1,0:T(8,128)(2,1)S(1)} collective-permute-done((bf16[4,192,128]{2,1,0:T(8,128)(2,1)S(1)}, bf16[4,192,128]{2,1,0:T(8,128)(2,1)S(1)}, u32[]{:S(2)}, u32[]{:S(2)}) %collective-permute-start.3) | collective-permute-done | bytes 196640 | tf_op jit(solution)/shard_map/ppermute | solution.py:304
  86.1 1.6 %collective-permute-start.19 = (bf16[256,512]{1,0:T(8,128)(2,1)S(1)}, bf16[256,512]{1,0:T(8,128)(2,1)S(1)}, u32[]{:S(2)}, u32[]{:S(2)}) collective-permute-start(bf16[256,512]{1,0:T(8,128)(2,1)S(1)} %get-tuple-element.48), channel_id=1, source_target_pairs={{0,6},{2,4},{4,2},{6,0},{8,14},{10,12},{12,10},{14,8},{16,22},{18,... | collective-permute-start | bytes 786440 | tf_op jit(solution)/shard_map/ppermute | solution.py:304
  87.6 5.9 %collective-permute-done.4.refs_5_ = bf16[4,192,128]{2,1,0:T(8,128)(2,1)S(1)} collective-permute-done((bf16[4,192,128]{2,1,0:T(8,128)(2,1)S(1)}, bf16[4,192,128]{2,1,0:T(8,128)(2,1)S(1)}, u32[]{:S(2)}, u32[]{:S(2)}) %collective-permute-start.4) | collective-permute-done | bytes 196640 | tf_op jit(solution)/shard_map/ppermute | solution.py:304
  93.5 1.6 %inputs.1 = (f32[256,512]{1,0:T(8,128)S(1)}, f32[256,512]{1,0:T(8,128)S(1)}) custom-call(s32[3]{0:T(128)S(1)} %copy-done, bf16[4,256,128]{2,1,0:T(8,128)(2,1)S(1)} %get-tuple-element.29.refs_0_, bf16[4,256,128]{2,1,0:T(8,128)(2,1)S(1)} %collective-permute-done.refs_1_, bf16[4,256,128]{2,1,0:T(8,128)(2,1)S(1)} %collective-permute-done.1.refs_2_, ...), custom_call_target="tpu_custom_call" | custom-call | flops 2200000000 | bytes 1048576 | tf_op jit(solution)/shard_map/inputs/pallas_call | solution.py:37
  95.2 2.5 %collective-permute-done.18.refs_2_ = bf16[256,512]{1,0:T(8,128)(2,1)S(1)} collective-permute-done((bf16[256,512]{1,0:T(8,128)(2,1)S(1)}, bf16[256,512]{1,0:T(8,128)(2,1)S(1)}, u32[]{:S(2)}, u32[]{:S(2)}) %collective-permute-start.18) | collective-permute-done | bytes 262176 | tf_op jit(solution)/shard_map/ppermute | solution.py:304
  97.8 0.8 plane_sum.1
  98.6 1.7 %collective-permute-start.20 = (bf16[64,512]{1,0:T(8,128)(2,1)S(1)}, bf16[64,512]{1,0:T(8,128)(2,1)S(1)}, u32[]{:S(2)}, u32[]{:S(2)}) collective-permute-start(bf16[64,512]{1,0:T(8,128)(2,1)S(1)} %get-tuple-element.50), channel_id=1, source_target_pairs={{0,8},{2,10},{4,12},{6,14},{8,0},{10,2},{12,4},{14,6},{16,24},{18,... | collective-permute-start | bytes 196616 | tf_op jit(solution)/shard_map/ppermute | solution.py:304
  100.3 1.3 %collective-permute-start.21 = (bf16[64,512]{1,0:T(8,128)(2,1)S(1)}, bf16[64,512]{1,0:T(8,128)(2,1)S(1)}, u32[]{:S(2)}, u32[]{:S(2)}) collective-permute-start(bf16[64,512]{1,0:T(8,128)(2,1)S(1)} %get-tuple-element.51), channel_id=1, source_target_pairs={{0,16},{2,18},{4,20},{6,22},{8,24},{10,26},{12,28},{14,30},{16,0},... | collective-permute-start | bytes 196616 | tf_op jit(solution)/shard_map/ppermute | solution.py:304
  101.6 1.4 %collective-permute-start.22 = (bf16[64,512]{1,0:T(8,128)(2,1)S(1)}, bf16[64,512]{1,0:T(8,128)(2,1)S(1)}, u32[]{:S(2)}, u32[]{:S(2)}) collective-permute-start(bf16[64,512]{1,0:T(8,128)(2,1)S(1)} %get-tuple-element.52), channel_id=1, source_target_pairs={{0,24},{2,26},{4,28},{6,30},{8,16},{10,18},{12,20},{14,22},{16,8},... | collective-permute-start | bytes 196616 | tf_op jit(solution)/shard_map/ppermute | solution.py:304
  103.0 5.4 %collective-permute-done.21.refs_2_ = bf16[64,512]{1,0:T(8,128)(2,1)S(1)} collective-permute-done((bf16[64,512]{1,0:T(8,128)(2,1)S(1)}, bf16[64,512]{1,0:T(8,128)(2,1)S(1)}, u32[]{:S(2)}, u32[]{:S(2)}) %collective-permute-start.21) | collective-permute-done | bytes 65568 | tf_op jit(solution)/shard_map/ppermute | solution.py:304
  108.4 1.4 %finish.1 = (f32[3,64,512]{2,1,0:T(8,128)}, f32[64,512]{1,0:T(8,128)}) custom-call(s32[3]{0:T(128)S(1)} %copy-done, bf16[64,512]{1,0:T(8,128)(2,1)S(1)} %get-tuple-element.49.refs_0_, bf16[64,512]{1,0:T(8,128)(2,1)S(1)} %collective-permute-done.20.refs_1_, bf16[64,512]{1,0:T(8,128)(2,1)S(1)} %collective-permute-done.21.refs_2_, ...), custom_call_target="tpu_custom_call" | custom-call | flops 1100000000 | bytes 1048576 | tf_op jit(solution)/shard_map/finish/pallas_call | solution.py:37
  109.8 0.8 add_convert_fusion
  (41 shorter events, 3.2 us)
Async XLA Ops:
  0.6 13.2 %copy-start.2 = (bf16[2,1,128,1024]{3,2,1,0:T(8,128)(2,1)S(1)}, bf16[2,1,128,1024]{3,2,1,0:T(8,128)(2,1)}, u32[]{:S(2)}) copy-start(bf16[2,1,128,1024]{3,2,1,0:T(8,128)(2,1)} %refs_5_.1) | copy-start | bytes 1572868
  0.6 13.2 %copy-start.3 = (bf16[2,1,128,1024]{3,2,1,0:T(8,128)(2,1)S(1)}, bf16[2,1,128,1024]{3,2,1,0:T(8,128)(2,1)}, u32[]{:S(2)}) copy-start(bf16[2,1,128,1024]{3,2,1,0:T(8,128)(2,1)} %refs_4_.3) | copy-start | bytes 1572868
  1.3 12.5 %copy-start = (s32[3]{0:T(128)S(1)}, s32[3]{0:T(128)}, u32[]{:S(2)}) copy-start(s32[3]{0:T(128)} %pad_add_fusion.pos_ref) | copy-start | bytes 40
  5.5 11.7 %copy-start.6 = (s32[16,8]{0,1:T(8,128)S(1)}, s32[16,8]{0,1:T(8,128)}, u32[]{:S(2)}) copy-start(s32[16,8]{0,1:T(8,128)} %param.16) | copy-start | bytes 1540
  5.5 35.7 %copy-start.5 = (s32[16]{0:T(128)S(1)}, s32[16]{0:T(128)}, u32[]{:S(2)}) copy-start(s32[16]{0:T(128)} %refs_1_.4) | copy-start | bytes 196
  5.5 32.8 %all-to-all-start = ((bf16[16,256,128]{2,1,0:T(8,128)(2,1)}), bf16[16,256,128]{2,1,0:T(8,128)(2,1)S(1)}, u32[]{:S(2)}, u32[]{:S(2)}) async-start(bf16[16,256,128]{2,1,0:T(8,128)(2,1)} %pack.1), calls=%async_computation | async-start | bytes 2097152 | tf_op jit(solution)/shard_map/all_to_all | solution.py:329
  14.5 0.7 copy-start.4
  15.2 40.3 %collective-permute-start.6 = (bf16[256,1024]{1,0:T(8,128)(2,1)S(1)}, bf16[256,1024]{1,0:T(8,128)(2,1)S(1)}, u32[]{:S(2)}, u32[]{:S(2)}) collective-permute-start(bf16[256,1024]{1,0:T(8,128)(2,1)S(1)} %get-tuple-element.36), channel_id=1, source_target_pairs={{0,8},{2,10},{4,12},{6,14},{8,0},{10,2},{12,4},{14,6},{16,24},{18,... | collective-permute-start | bytes 1572872 | tf_op jit(solution)/shard_map/ppermute | solution.py:304
  38.3 21.6 %collective-permute-start.8 = (bf16[128,1024]{1,0:T(8,128)(2,1)}, bf16[128,1024]{1,0:T(8,128)(2,1)S(1)}, u32[]{:S(2)}, u32[]{:S(2)}) collective-permute-start(bf16[128,1024]{1,0:T(8,128)(2,1)} %copy-done.4), channel_id=1, source_target_pairs={{0,16},{2,18},{4,20},{6,22},{8,24},{10,26},{12,28},{14,30},{16,0},... | collective-permute-start | bytes 786440 | tf_op jit(solution)/shard_map/ppermute | solution.py:304
  41.0 22.5 %collective-permute-start.12 = (bf16[128,1024]{1,0:T(8,128)(2,1)S(1)}, bf16[128,1024]{1,0:T(8,128)(2,1)S(1)}, u32[]{:S(2)}, u32[]{:S(2)}) collective-permute-start(bf16[128,1024]{1,0:T(8,128)(2,1)S(1)} %get-tuple-element.41), channel_id=1, source_target_pairs={{0,16},{2,18},{4,20},{6,22},{8,24},{10,26},{12,28},{14,30},{16,0},... | collective-permute-start | bytes 786440 | tf_op jit(solution)/shard_map/ppermute | solution.py:304
  54.1 9.4 %collective-permute-start = (bf16[4,256,128]{2,1,0:T(8,128)(2,1)S(1)}, bf16[4,256,128]{2,1,0:T(8,128)(2,1)S(1)}, u32[]{:S(2)}, u32[]{:S(2)}) collective-permute-start(bf16[4,256,128]{2,1,0:T(8,128)(2,1)S(1)} %get-tuple-element.30), channel_id=1, source_target_pairs={{0,2},{2,0},{4,6},{6,4},{8,10},{10,8},{12,14},{14,12},{16,18},{18,... | collective-permute-start | bytes 786440 | tf_op jit(solution)/shard_map/ppermute | solution.py:304
  55.5 20.6 %collective-permute-start.7 = (bf16[256,1024]{1,0:T(8,128)(2,1)S(1)}, bf16[256,1024]{1,0:T(8,128)(2,1)S(1)}, u32[]{:S(2)}, u32[]{:S(2)}) collective-permute-start(bf16[256,1024]{1,0:T(8,128)(2,1)S(1)} %collective-permute-done.6.refs_6_), channel_id=1, source_target_pairs={{0,1},{1,0},{2,3},{3,2},{4,5},{5,4},{6,7},{7,6},{8,9},{9,8},{10,11... | collective-permute-start | bytes 1572872 | tf_op jit(solution)/shard_map/ppermute | solution.py:322
  55.5 14.3 %collective-permute-start.1 = (bf16[4,256,128]{2,1,0:T(8,128)(2,1)S(1)}, bf16[4,256,128]{2,1,0:T(8,128)(2,1)S(1)}, u32[]{:S(2)}, u32[]{:S(2)}) collective-permute-start(bf16[4,256,128]{2,1,0:T(8,128)(2,1)S(1)} %get-tuple-element.31), channel_id=1, source_target_pairs={{0,4},{2,6},{4,0},{6,2},{8,12},{10,14},{12,8},{14,10},{16,20},{18,... | collective-permute-start | bytes 786440 | tf_op jit(solution)/shard_map/ppermute | solution.py:304
  59.9 10.0 %collective-permute-start.2 = (bf16[4,256,128]{2,1,0:T(8,128)(2,1)S(1)}, bf16[4,256,128]{2,1,0:T(8,128)(2,1)S(1)}, u32[]{:S(2)}, u32[]{:S(2)}) collective-permute-start(bf16[4,256,128]{2,1,0:T(8,128)(2,1)S(1)} %get-tuple-element.32), channel_id=1, source_target_pairs={{0,6},{2,4},{4,2},{6,0},{8,14},{10,12},{12,10},{14,8},{16,22},{18,... | collective-permute-start | bytes 786440 | tf_op jit(solution)/shard_map/ppermute | solution.py:304
  63.5 9.2 %collective-permute-start.10 = (bf16[128,1024]{1,0:T(8,128)(2,1)S(1)}, bf16[128,1024]{1,0:T(8,128)(2,1)S(1)}, u32[]{:S(2)}, u32[]{:S(2)}) collective-permute-start(bf16[128,1024]{1,0:T(8,128)(2,1)S(1)} %collective-permute-done.8.refs_8_), channel_id=1, source_target_pairs={{0,8},{2,10},{4,12},{6,14},{8,0},{10,2},{12,4},{14,6},{16,24},{18,... | collective-permute-start | bytes 786440 | tf_op jit(solution)/shard_map/ppermute | solution.py:304
  63.5 12.0 %collective-permute-start.14 = (bf16[128,1024]{1,0:T(8,128)(2,1)S(1)}, bf16[128,1024]{1,0:T(8,128)(2,1)S(1)}, u32[]{:S(2)}, u32[]{:S(2)}) collective-permute-start(bf16[128,1024]{1,0:T(8,128)(2,1)S(1)} %collective-permute-done.12.refs_12_), channel_id=1, source_target_pairs={{0,8},{2,10},{4,12},{6,14},{8,0},{10,2},{12,4},{14,6},{16,24},{18,... | collective-permute-start | bytes 786440 | tf_op jit(solution)/shard_map/ppermute | solution.py:304
  69.8 6.6 %collective-permute-start.13 = (bf16[128,1024]{1,0:T(8,128)(2,1)S(1)}, bf16[128,1024]{1,0:T(8,128)(2,1)S(1)}, u32[]{:S(2)}, u32[]{:S(2)}) collective-permute-start(bf16[128,1024]{1,0:T(8,128)(2,1)S(1)} %collective-permute-done.12.refs_12_), channel_id=1, source_target_pairs={{0,1},{1,0},{2,3},{3,2},{4,5},{5,4},{6,7},{7,6},{8,9},{9,8},{10,11... | collective-permute-start | bytes 786440 | tf_op jit(solution)/shard_map/ppermute | solution.py:322
  69.8 8.0 %collective-permute-start.9 = (bf16[128,1024]{1,0:T(8,128)(2,1)S(1)}, bf16[128,1024]{1,0:T(8,128)(2,1)S(1)}, u32[]{:S(2)}, u32[]{:S(2)}) collective-permute-start(bf16[128,1024]{1,0:T(8,128)(2,1)S(1)} %collective-permute-done.8.refs_8_), channel_id=1, source_target_pairs={{0,1},{1,0},{2,3},{3,2},{4,5},{5,4},{6,7},{7,6},{8,9},{9,8},{10,11... | collective-permute-start | bytes 786440 | tf_op jit(solution)/shard_map/ppermute | solution.py:322
  72.7 7.9 %collective-permute-start.11 = (bf16[128,1024]{1,0:T(8,128)(2,1)S(1)}, bf16[128,1024]{1,0:T(8,128)(2,1)S(1)}, u32[]{:S(2)}, u32[]{:S(2)}) collective-permute-start(bf16[128,1024]{1,0:T(8,128)(2,1)S(1)} %collective-permute-done.10.refs_10_), channel_id=1, source_target_pairs={{0,1},{1,0},{2,3},{3,2},{4,5},{5,4},{6,7},{7,6},{8,9},{9,8},{10,11... | collective-permute-start | bytes 786440 | tf_op jit(solution)/shard_map/ppermute | solution.py:322
  75.5 5.1 %collective-permute-start.15 = (bf16[128,1024]{1,0:T(8,128)(2,1)S(1)}, bf16[128,1024]{1,0:T(8,128)(2,1)S(1)}, u32[]{:S(2)}, u32[]{:S(2)}) collective-permute-start(bf16[128,1024]{1,0:T(8,128)(2,1)S(1)} %collective-permute-done.14.refs_14_), channel_id=1, source_target_pairs={{0,1},{1,0},{2,3},{3,2},{4,5},{5,4},{6,7},{7,6},{8,9},{9,8},{10,11... | collective-permute-start | bytes 786440 | tf_op jit(solution)/shard_map/ppermute | solution.py:322
  76.1 10.0 %collective-permute-start.3 = (bf16[4,192,128]{2,1,0:T(8,128)(2,1)S(1)}, bf16[4,192,128]{2,1,0:T(8,128)(2,1)S(1)}, u32[]{:S(2)}, u32[]{:S(2)}) collective-permute-start(bf16[4,192,128]{2,1,0:T(8,128)(2,1)S(1)} %get-tuple-element.33), channel_id=1, source_target_pairs={{0,8},{2,10},{4,12},{6,14},{8,0},{10,2},{12,4},{14,6},{16,24},{18,... | collective-permute-start | bytes 589832 | tf_op jit(solution)/shard_map/ppermute | solution.py:304
  76.4 17.1 %collective-permute-start.4 = (bf16[4,192,128]{2,1,0:T(8,128)(2,1)S(1)}, bf16[4,192,128]{2,1,0:T(8,128)(2,1)S(1)}, u32[]{:S(2)}, u32[]{:S(2)}) collective-permute-start(bf16[4,192,128]{2,1,0:T(8,128)(2,1)S(1)} %get-tuple-element.34), channel_id=1, source_target_pairs={{0,16},{2,18},{4,20},{6,22},{8,24},{10,26},{12,28},{14,30},{16,0},... | collective-permute-start | bytes 589832 | tf_op jit(solution)/shard_map/ppermute | solution.py:304
  77.8 15.8 %copy-start.1 = (bf16[3,1024,512]{2,1,0:T(8,128)(2,1)S(1)}, bf16[3,1024,512]{2,1,0:T(8,128)(2,1)}, u32[]{:S(2)}) copy-start(bf16[3,1024,512]{2,1,0:T(8,128)(2,1)} %refs_7_.1) | copy-start | bytes 9437188
  77.8 15.8 %collective-permute-start.5 = (bf16[4,192,128]{2,1,0:T(8,128)(2,1)S(1)}, bf16[4,192,128]{2,1,0:T(8,128)(2,1)S(1)}, u32[]{:S(2)}, u32[]{:S(2)}) collective-permute-start(bf16[4,192,128]{2,1,0:T(8,128)(2,1)S(1)} %get-tuple-element.35), channel_id=1, source_target_pairs={{0,24},{2,26},{4,28},{6,30},{8,16},{10,18},{12,20},{14,22},{16,8},... | collective-permute-start | bytes 589832 | tf_op jit(solution)/shard_map/ppermute | solution.py:304
  82.8 12.4 %collective-permute-start.17 = (bf16[256,512]{1,0:T(8,128)(2,1)S(1)}, bf16[256,512]{1,0:T(8,128)(2,1)S(1)}, u32[]{:S(2)}, u32[]{:S(2)}) collective-permute-start(bf16[256,512]{1,0:T(8,128)(2,1)S(1)} %get-tuple-element.46), channel_id=1, source_target_pairs={{0,2},{2,0},{4,6},{6,4},{8,10},{10,8},{12,14},{14,12},{16,18},{18,... | collective-permute-start | bytes 786440 | tf_op jit(solution)/shard_map/ppermute | solution.py:304
  84.6 13.2 %collective-permute-start.18 = (bf16[256,512]{1,0:T(8,128)(2,1)S(1)}, bf16[256,512]{1,0:T(8,128)(2,1)S(1)}, u32[]{:S(2)}, u32[]{:S(2)}) collective-permute-start(bf16[256,512]{1,0:T(8,128)(2,1)S(1)} %get-tuple-element.47), channel_id=1, source_target_pairs={{0,4},{2,6},{4,0},{6,2},{8,12},{10,14},{12,8},{14,10},{16,20},{18,... | collective-permute-start | bytes 786440 | tf_op jit(solution)/shard_map/ppermute | solution.py:304
  86.1 11.7 %collective-permute-start.19 = (bf16[256,512]{1,0:T(8,128)(2,1)S(1)}, bf16[256,512]{1,0:T(8,128)(2,1)S(1)}, u32[]{:S(2)}, u32[]{:S(2)}) collective-permute-start(bf16[256,512]{1,0:T(8,128)(2,1)S(1)} %get-tuple-element.48), channel_id=1, source_target_pairs={{0,6},{2,4},{4,2},{6,0},{8,14},{10,12},{12,10},{14,8},{16,22},{18,... | collective-permute-start | bytes 786440 | tf_op jit(solution)/shard_map/ppermute | solution.py:304
  95.2 14.7 %collective-permute-start.16 = (f32[256,512]{1,0:T(8,128)S(1)}, f32[256,512]{1,0:T(8,128)S(1)}, u32[]{:S(2)}, u32[]{:S(2)}) collective-permute-start(f32[256,512]{1,0:T(8,128)S(1)} %get-tuple-element.45), channel_id=1, source_target_pairs={{0,1},{1,0},{2,3},{3,2},{4,5},{5,4},{6,7},{7,6},{8,9},{9,8},{10,11... | collective-permute-start | bytes 1572872 | tf_op jit(solution)/shard_map/ppermute | solution.py:322
  98.6 4.5 %collective-permute-start.20 = (bf16[64,512]{1,0:T(8,128)(2,1)S(1)}, bf16[64,512]{1,0:T(8,128)(2,1)S(1)}, u32[]{:S(2)}, u32[]{:S(2)}) collective-permute-start(bf16[64,512]{1,0:T(8,128)(2,1)S(1)} %get-tuple-element.50), channel_id=1, source_target_pairs={{0,8},{2,10},{4,12},{6,14},{8,0},{10,2},{12,4},{14,6},{16,24},{18,... | collective-permute-start | bytes 196616 | tf_op jit(solution)/shard_map/ppermute | solution.py:304
  100.3 8.1 %collective-permute-start.21 = (bf16[64,512]{1,0:T(8,128)(2,1)S(1)}, bf16[64,512]{1,0:T(8,128)(2,1)S(1)}, u32[]{:S(2)}, u32[]{:S(2)}) collective-permute-start(bf16[64,512]{1,0:T(8,128)(2,1)S(1)} %get-tuple-element.51), channel_id=1, source_target_pairs={{0,16},{2,18},{4,20},{6,22},{8,24},{10,26},{12,28},{14,30},{16,0},... | collective-permute-start | bytes 196616 | tf_op jit(solution)/shard_map/ppermute | solution.py:304
  101.6 6.8 %collective-permute-start.22 = (bf16[64,512]{1,0:T(8,128)(2,1)S(1)}, bf16[64,512]{1,0:T(8,128)(2,1)S(1)}, u32[]{:S(2)}, u32[]{:S(2)}) collective-permute-start(bf16[64,512]{1,0:T(8,128)(2,1)S(1)} %get-tuple-element.52), channel_id=1, source_target_pairs={{0,24},{2,26},{4,28},{6,30},{8,16},{10,18},{12,20},{14,22},{16,8},... | collective-permute-start | bytes 196616 | tf_op jit(solution)/shard_map/ppermute | solution.py:304

commit v4 on v3

--- a/solution.py
+++ b/solution.py
@@ -46,7 +46,7 @@
     )(pos, *args, *after)
 
 
-def pack_kernel(pos_ref, *refs):
+def pack_kernel(_, *refs):
     far, out_ref, near, sems = refs[:5], refs[5], refs[6:11], refs[11:]
     copies = [pltpu.make_async_copy(*trio) for trio in zip(far, near, sems)]
     for copy in copies:
@@ -72,8 +72,9 @@
         put(2, scene, v_ref[scene, 0].T)
     copies[3].wait()
     copies[4].wait()
+    d_head = mul_nt(w_ref[...], d_ref[...].reshape(len(scenes) * LANE, -1)).astype(BF)
     for scene in scenes:
-        put(3, scene, mul_nt(w_ref[...], d_ref[scene, 0]).astype(BF))
+        put(3, scene, d_head[:, scene * LANE : (scene + 1) * LANE])
 
 
 def fetch_kernel(pos_ref, t_ref, d_ref, both, t_out, d_out, *sems):
@@ -216,37 +217,34 @@
     for n, ref in enumerate(far[2:]):
         at = slice((n % 4 + 4) * LANE, (n % 4 + 5) * LANE)
         (d_o if n // 4 else tok)[at] = ref[...]
-    wide[:, : 6 * HD] = mul(left[...], tok[...]).T
-    wide[:, 6 * HD :] = mul(left_o[...], d_o[...]).T
+    wide[:, : 6 * HD] = mul(left[...], tok[...]).astype(BF).T
+    wide[:, 6 * HD :] = mul(left_o[...], d_o[...]).astype(BF).T
     part = wide.shape[0] // (QUAD * planes)
     for ref, quad in places(outs, pos_ref[1]):
         for p in range(planes):
             rows = pl.ds(pl.multiple_of((p * QUAD + quad) * part, part), part)
-            ref[p * part : (p + 1) * part] = wide[rows, :].astype(BF)
+            ref[p * part : (p + 1) * part] = wide[rows, :]
 
 
 def sum_kernel(planes, pos_ref, *refs):
-    terms, outs, total = refs[:4], refs[4:-1], refs[-1]
-    acc = None
-    for ref, _ in places(terms, 0):
-        acc = ref[...].astype(F32) if acc is None else acc + ref[...].astype(F32)
-    total[...] = acc
-    part = total.shape[0] // planes
+    terms, outs = refs[:QUAD], refs[QUAD:]
+    part = terms[0].shape[0] // planes
     for ref, plane in places(outs, pos_ref[0]):
         rows = pl.ds(pl.multiple_of(plane * part, part), part)
-        ref[...] = total[rows, :].astype(BF)
+        acc = terms[0][rows, :].astype(F32)
+        for term in terms[1:]:
+            acc = acc + term[rows, :].astype(F32)
+        ref[...] = acc.astype(BF)
 
 
 def finish_kernel(planes, pos_ref, *refs):
-    terms, (w_ref, o_ref, buf) = refs[:4], refs[4:]
+    terms, (w_ref, o_ref) = refs[:planes], refs[planes:]
+    two = 2 * HD
     for ref, plane in places(terms, pos_ref[0]):
-        buf[plane] = ref[...].astype(F32)
-    two = 2 * HD
-    for p in range(planes):
-        cols = slice(p * two, (p + 1) * two)
-        o_ref[:, cols] = buf[p, :, 3 * two :]
+        cols = pl.ds(pl.multiple_of(plane * two, two), two)
+        o_ref[:, cols] = ref[:, 3 * two :].astype(F32)
         for place, j in enumerate((2, 0, 1)):
-            w_ref[j, :, cols] = buf[p, :, place * two : (place + 1) * two]
+            w_ref[j, :, cols] = ref[:, place * two : (place + 1) * two].astype(F32)
 
 
 def turn_kernel(planes, pos_ref, *refs):
@@ -325,7 +323,7 @@
     packed = call(
         pack_kernel, "pack", [((cameras, 4 * HD, rows), BF)], arrays, [(arr.shape, BF) for arr in arrays],
         56, inputs=pl.ANY, sems=len(arrays),
-    )(pos)[0]
+    )(jnp.zeros(1, jnp.int32))[0]
     packed = lax.all_to_all(packed, "view", 0, 0, tiled=True)
 
     own = call(fetch_kernel, "fetch", [((2 * rows, model), BF), ((rows, model), BF), ((rows, model), BF)], (tokens, d_out), (), 40, inputs=pl.ANY, sems=2)(pos)
@@ -353,16 +351,16 @@
     depth = 2 * planes * rows
     terms = call(
         functools.partial(weights_kernel, planes), "weights", [((model // QUAD, 8 * HD), BF)] * QUAD, blocks + [tokens, d_out] + column,
-        [((6 * HD, depth), BF), ((2 * HD, depth), BF), ((depth, model), BF), ((depth, model), BF), ((model, 8 * HD), F32)],
+        [((6 * HD, depth), BF), ((2 * HD, depth), BF), ((depth, model), BF), ((depth, model), BF), ((model, 8 * HD), BF)],
         32, 3,
     )(pos)
     started = terms[:1]
     terms = call(
-        functools.partial(sum_kernel, planes), "plane_sum", [((part, 8 * HD), BF)] * planes, over_plane(terms), [((model // QUAD, 8 * HD), F32)],
+        functools.partial(sum_kernel, planes), "plane_sum", [((part, 8 * HD), BF)] * planes, over_plane(terms),
     )(pos)
     d_wqkv, d_wo = call(
         functools.partial(finish_kernel, planes), "finish", [((3, part, width), F32), ((part, width), F32)],
-        over_column(terms), [((planes, part, 8 * HD), F32)],
+        over_column(terms),
     )(pos)
 
     grads = call(functools.partial(turn_kernel, planes), "turn", [((QUAD, 3 * HD, rows), BF)] * (planes - 1), blocks, after=())(pos)

time: 111 us -> 109 us (0.982)
  Pallas kernels: 24.4 us -> 23.2 us
    pallas_call x8, Pallas kernels: 24.4 us -> 23.2 us  [call(): pl.pallas_call(run, out_shape=[jax.ShapeDtypeStruct(dims, dtype) for dims...]
  transfers between devices with their start and end apart: 24 -> 24, of which waited for: 10 -> 11; matrix products, arithmetic and copies ran while one was open for 0% -> 0% of each run, Pallas kernels for 18% -> 18%
where the time goes in v4:
time: 109 us
  waiting for transfers between devices  50.7 us (47%)
  starting transfers between devices  32.5 us (30%)
  Pallas kernels  23.2 us (21%)
    ppermute x17, waiting for transfers between devices, along(): return lax.ppermute(value, 'view', pairs)  29.7 us
    ppermute x17, starting transfers between devices, along(): return lax.ppermute(value, 'view', pairs)  23.5 us
    pallas_call x8, Pallas kernels, call(): pl.pallas_call(run, out_shape=[jax.ShapeDtypeStruct(dims, dtype) for dims...  23.2 us
    all_to_all x1, waiting for transfers between devices, split_body(): packed = lax.all_to_all(packed, 'view', 0, 0, tiled=True)  21 us
    all_to_all x1, starting transfers between devices, split_body(): packed = lax.all_to_all(packed, 'view', 0, 0, tiled=True)  8.32 us
  transfers between devices with their start and end apart: 24, of which 11 were waited for; matrix products, arithmetic and copies ran while one was open for 0% of the time, Pallas kernels for 18%

profile of v4, /device:TPU:0, one launch (start us, length us, event | category | flops | bytes accessed | tf_op | source)
XLA Modules:
  0.0 108.8 jit_solution(4971359954954892044)
XLA Ops:
  0.7 3.2 %pack.1 = bf16[16,256,128]{2,1,0:T(8,128)(2,1)} custom-call(s32[1]{0:T(128)} %constant.35.clone.1.pos_ref, bf16[2,1,128,512]{3,2,1,0:T(8,128)(2,1)} %refs_0_.3, bf16[2,1,128,512]{3,2,1,0:T(8,128)(2,1)} %refs_1_.3, bf16[2,1,128,512]{3,2,1,0:T(8,128)(2,1)} %refs_2_.1, bf16[2,1,128,1024]{3,2,1,0:T(8,128)(2,1)} %refs_5_.1, bf16[512,1024]{1,0:T(8,128)(2,1)} %refs_4_.2), custom_call_target="tpu_custom_call" | custom-call | flops 1100000000 | bytes 1048576 | tf_op jit(solution)/shard_map/pack/pallas_call | solution.py:37
  3.9 8.3 %all-to-all-start = ((bf16[16,256,128]{2,1,0:T(8,128)(2,1)}), bf16[16,256,128]{2,1,0:T(8,128)(2,1)S(1)}, u32[]{:S(2)}, u32[]{:S(2)}) async-start(bf16[16,256,128]{2,1,0:T(8,128)(2,1)} %pack.1), calls=%async_computation | async-start | bytes 2097152 | tf_op jit(solution)/shard_map/all_to_all | solution.py:327
  13.0 0.7 copy-done.3
  13.7 1.9 %collective-permute-start.6 = (bf16[256,1024]{1,0:T(8,128)(2,1)S(1)}, bf16[256,1024]{1,0:T(8,128)(2,1)S(1)}, u32[]{:S(2)}, u32[]{:S(2)}) collective-permute-start(bf16[256,1024]{1,0:T(8,128)(2,1)S(1)} %get-tuple-element.36), channel_id=1, source_target_pairs={{0,8},{2,10},{4,12},{6,14},{8,0},{10,2},{12,4},{14,6},{16,24},{18,... | collective-permute-start | bytes 1572872 | tf_op jit(solution)/shard_map/ppermute | solution.py:302
  15.6 21.0 %all-to-all-done.refs_2_ = bf16[16,256,128]{2,1,0:T(8,128)(2,1)S(1)} async-done(((bf16[16,256,128]{2,1,0:T(8,128)(2,1)}), bf16[16,256,128]{2,1,0:T(8,128)(2,1)S(1)}, u32[]{:S(2)}, u32[]{:S(2)}) %all-to-all-start) | async-done | bytes 1048608 | tf_op jit(solution)/shard_map/all_to_all | solution.py:327
  36.7 2.7 %collective-permute-start.8 = (bf16[128,1024]{1,0:T(8,128)(2,1)}, bf16[128,1024]{1,0:T(8,128)(2,1)S(1)}, u32[]{:S(2)}, u32[]{:S(2)}) collective-permute-start(bf16[128,1024]{1,0:T(8,128)(2,1)} %copy-done.3), channel_id=1, source_target_pairs={{0,16},{2,18},{4,20},{6,22},{8,24},{10,26},{12,28},{14,30},{16,0},... | collective-permute-start | bytes 786440 | tf_op jit(solution)/shard_map/ppermute | solution.py:302
  39.6 12.9 %attend.1 = (bf16[4,256,128]{2,1,0:T(8,128)(2,1)S(1)}, bf16[4,256,128]{2,1,0:T(8,128)(2,1)S(1)}, bf16[4,256,128]{2,1,0:T(8,128)(2,1)S(1)}, bf16[4,256,128]{2,1,0:T(8,128)(2,1)S(1)}) custom-call(s32[3]{0:T(128)S(1)} %pad_add_fusion.pos_ref, s32[16,8]{1,0:T(8,128)S(1)} %copy.12.refs_0_, s32[16]{0:T(128)S(1)} %copy-done.4, ...), custom_call_target="tpu_custom_call" | custom-call | flops 5500000256 | bytes 1048576 | tf_op jit(solution)/shard_map/attend/pallas_call | solution.py:37
  52.5 1.3 %collective-permute-start = (bf16[4,256,128]{2,1,0:T(8,128)(2,1)S(1)}, bf16[4,256,128]{2,1,0:T(8,128)(2,1)S(1)}, u32[]{:S(2)}, u32[]{:S(2)}) collective-permute-start(bf16[4,256,128]{2,1,0:T(8,128)(2,1)S(1)} %get-tuple-element.30), channel_id=1, source_target_pairs={{0,2},{2,0},{4,6},{6,4},{8,10},{10,8},{12,14},{14,12},{16,18},{18,... | collective-permute-start | bytes 786440 | tf_op jit(solution)/shard_map/ppermute | solution.py:302
  53.9 1.3 %collective-permute-start.1 = (bf16[4,256,128]{2,1,0:T(8,128)(2,1)S(1)}, bf16[4,256,128]{2,1,0:T(8,128)(2,1)S(1)}, u32[]{:S(2)}, u32[]{:S(2)}) collective-permute-start(bf16[4,256,128]{2,1,0:T(8,128)(2,1)S(1)} %get-tuple-element.31), channel_id=1, source_target_pairs={{0,4},{2,6},{4,0},{6,2},{8,12},{10,14},{12,8},{14,10},{16,20},{18,... | collective-permute-start | bytes 786440 | tf_op jit(solution)/shard_map/ppermute | solution.py:302
  55.1 3.1 %collective-permute-done.8.refs_8_ = bf16[128,1024]{1,0:T(8,128)(2,1)S(1)} collective-permute-done((bf16[128,1024]{1,0:T(8,128)(2,1)}, bf16[128,1024]{1,0:T(8,128)(2,1)S(1)}, u32[]{:S(2)}, u32[]{:S(2)}) %collective-permute-start.8) | collective-permute-done | bytes 262176 | tf_op jit(solution)/shard_map/ppermute | solution.py:302
  58.2 1.8 %collective-permute-start.2 = (bf16[4,256,128]{2,1,0:T(8,128)(2,1)S(1)}, bf16[4,256,128]{2,1,0:T(8,128)(2,1)S(1)}, u32[]{:S(2)}, u32[]{:S(2)}) collective-permute-start(bf16[4,256,128]{2,1,0:T(8,128)(2,1)S(1)} %get-tuple-element.32), channel_id=1, source_target_pairs={{0,6},{2,4},{4,2},{6,0},{8,14},{10,12},{12,10},{14,8},{16,22},{18,... | collective-permute-start | bytes 786440 | tf_op jit(solution)/shard_map/ppermute | solution.py:302
  60.1 1.8 %collective-permute-done.12.refs_12_ = bf16[128,1024]{1,0:T(8,128)(2,1)S(1)} collective-permute-done((bf16[128,1024]{1,0:T(8,128)(2,1)S(1)}, bf16[128,1024]{1,0:T(8,128)(2,1)S(1)}, u32[]{:S(2)}, u32[]{:S(2)}) %collective-permute-start.12) | collective-permute-done | bytes 262176 | tf_op jit(solution)/shard_map/ppermute | solution.py:302
  61.9 2.0 %collective-permute-start.14 = (bf16[128,1024]{1,0:T(8,128)(2,1)S(1)}, bf16[128,1024]{1,0:T(8,128)(2,1)S(1)}, u32[]{:S(2)}, u32[]{:S(2)}) collective-permute-start(bf16[128,1024]{1,0:T(8,128)(2,1)S(1)} %collective-permute-done.12.refs_12_), channel_id=1, source_target_pairs={{0,8},{2,10},{4,12},{6,14},{8,0},{10,2},{12,4},{14,6},{16,24},{18,... | collective-permute-start | bytes 786440 | tf_op jit(solution)/shard_map/ppermute | solution.py:302
  63.9 4.3 %collective-permute-done.1.refs_2_ = bf16[4,256,128]{2,1,0:T(8,128)(2,1)S(1)} collective-permute-done((bf16[4,256,128]{2,1,0:T(8,128)(2,1)S(1)}, bf16[4,256,128]{2,1,0:T(8,128)(2,1)S(1)}, u32[]{:S(2)}, u32[]{:S(2)}) %collective-permute-start.1) | collective-permute-done | bytes 262176 | tf_op jit(solution)/shard_map/ppermute | solution.py:302
  68.7 2.3 %collective-permute-done.10.refs_10_ = bf16[128,1024]{1,0:T(8,128)(2,1)S(1)} collective-permute-done((bf16[128,1024]{1,0:T(8,128)(2,1)S(1)}, bf16[128,1024]{1,0:T(8,128)(2,1)S(1)}, u32[]{:S(2)}, u32[]{:S(2)}) %collective-permute-start.10) | collective-permute-done | bytes 262176 | tf_op jit(solution)/shard_map/ppermute | solution.py:302
  71.0 2.8 %collective-permute-done.14.refs_14_ = bf16[128,1024]{1,0:T(8,128)(2,1)S(1)} collective-permute-done((bf16[128,1024]{1,0:T(8,128)(2,1)S(1)}, bf16[128,1024]{1,0:T(8,128)(2,1)S(1)}, u32[]{:S(2)}, u32[]{:S(2)}) %collective-permute-start.14) | collective-permute-done | bytes 262176 | tf_op jit(solution)/shard_map/ppermute | solution.py:302
  74.8 1.3 %collective-permute-start.4 = (bf16[4,192,128]{2,1,0:T(8,128)(2,1)S(1)}, bf16[4,192,128]{2,1,0:T(8,128)(2,1)S(1)}, u32[]{:S(2)}, u32[]{:S(2)}) collective-permute-start(bf16[4,192,128]{2,1,0:T(8,128)(2,1)S(1)} %get-tuple-element.34), channel_id=1, source_target_pairs={{0,16},{2,18},{4,20},{6,22},{8,24},{10,26},{12,28},{14,30},{16,0},... | collective-permute-start | bytes 589832 | tf_op jit(solution)/shard_map/ppermute | solution.py:302
  76.2 2.8 %collective-permute-start.5 = (bf16[4,192,128]{2,1,0:T(8,128)(2,1)S(1)}, bf16[4,192,128]{2,1,0:T(8,128)(2,1)S(1)}, u32[]{:S(2)}, u32[]{:S(2)}) collective-permute-start(bf16[4,192,128]{2,1,0:T(8,128)(2,1)S(1)} %get-tuple-element.35), channel_id=1, source_target_pairs={{0,24},{2,26},{4,28},{6,30},{8,16},{10,18},{12,20},{14,22},{16,8},... | collective-permute-start | bytes 589832 | tf_op jit(solution)/shard_map/ppermute | solution.py:302
  78.9 2.2 %weights.1 = (bf16[256,512]{1,0:T(8,128)(2,1)S(1)}, bf16[256,512]{1,0:T(8,128)(2,1)S(1)}, bf16[256,512]{1,0:T(8,128)(2,1)S(1)}, bf16[256,512]{1,0:T(8,128)(2,1)S(1)}) custom-call(s32[3]{0:T(128)S(1)} %pad_add_fusion.pos_ref, bf16[4,256,128]{2,1,0:T(8,128)(2,1)S(1)} %get-tuple-element.29.refs_0_, bf16[4,256,128]{2,1,0:T(8,128)(2,1)S(1)} %collective-permute-done.refs_1_, ...), custom_call_target="tpu_custom_call" | custom-call | flops 3300000000 | bytes 1048576 | tf_op jit(solution)/shard_map/weights/pallas_call | solution.py:37
  81.1 1.8 %collective-permute-start.17 = (bf16[256,512]{1,0:T(8,128)(2,1)S(1)}, bf16[256,512]{1,0:T(8,128)(2,1)S(1)}, u32[]{:S(2)}, u32[]{:S(2)}) collective-permute-start(bf16[256,512]{1,0:T(8,128)(2,1)S(1)} %get-tuple-element.46), channel_id=1, source_target_pairs={{0,2},{2,0},{4,6},{6,4},{8,10},{10,8},{12,14},{14,12},{16,18},{18,... | collective-permute-start | bytes 786440 | tf_op jit(solution)/shard_map/ppermute | solution.py:302
  82.9 1.5 %collective-permute-done.3.refs_4_ = bf16[4,192,128]{2,1,0:T(8,128)(2,1)S(1)} collective-permute-done((bf16[4,192,128]{2,1,0:T(8,128)(2,1)S(1)}, bf16[4,192,128]{2,1,0:T(8,128)(2,1)S(1)}, u32[]{:S(2)}, u32[]{:S(2)}) %collective-permute-start.3) | collective-permute-done | bytes 196640 | tf_op jit(solution)/shard_map/ppermute | solution.py:302
  84.4 1.6 %collective-permute-start.19 = (bf16[256,512]{1,0:T(8,128)(2,1)S(1)}, bf16[256,512]{1,0:T(8,128)(2,1)S(1)}, u32[]{:S(2)}, u32[]{:S(2)}) collective-permute-start(bf16[256,512]{1,0:T(8,128)(2,1)S(1)} %get-tuple-element.48), channel_id=1, source_target_pairs={{0,6},{2,4},{4,2},{6,0},{8,14},{10,12},{12,10},{14,8},{16,22},{18,... | collective-permute-start | bytes 786440 | tf_op jit(solution)/shard_map/ppermute | solution.py:302
  86.0 5.9 %collective-permute-done.4.refs_5_ = bf16[4,192,128]{2,1,0:T(8,128)(2,1)S(1)} collective-permute-done((bf16[4,192,128]{2,1,0:T(8,128)(2,1)S(1)}, bf16[4,192,128]{2,1,0:T(8,128)(2,1)S(1)}, u32[]{:S(2)}, u32[]{:S(2)}) %collective-permute-start.4) | collective-permute-done | bytes 196640 | tf_op jit(solution)/shard_map/ppermute | solution.py:302
  91.9 1.6 %inputs.1 = (f32[256,512]{1,0:T(8,128)S(1)}, f32[256,512]{1,0:T(8,128)S(1)}) custom-call(s32[3]{0:T(128)S(1)} %pad_add_fusion.pos_ref, bf16[4,256,128]{2,1,0:T(8,128)(2,1)S(1)} %get-tuple-element.29.refs_0_, bf16[4,256,128]{2,1,0:T(8,128)(2,1)S(1)} %collective-permute-done.refs_1_, bf16[4,256,128]{2,1,0:T(8,128)(2,1)S(1)} %collective-permute-done.1.refs_2_, ...), custom_call_target="tpu_custom_call" | custom-call | flops 2200000000 | bytes 1048576 | tf_op jit(solution)/shard_map/inputs/pallas_call | solution.py:37
  93.6 2.5 %collective-permute-done.18.refs_2_ = bf16[256,512]{1,0:T(8,128)(2,1)S(1)} collective-permute-done((bf16[256,512]{1,0:T(8,128)(2,1)S(1)}, bf16[256,512]{1,0:T(8,128)(2,1)S(1)}, u32[]{:S(2)}, u32[]{:S(2)}) %collective-permute-start.18) | collective-permute-done | bytes 262176 | tf_op jit(solution)/shard_map/ppermute | solution.py:302
  96.1 0.7 plane_sum.1
  96.8 1.8 %collective-permute-start.20 = (bf16[64,512]{1,0:T(8,128)(2,1)S(1)}, bf16[64,512]{1,0:T(8,128)(2,1)S(1)}, u32[]{:S(2)}, u32[]{:S(2)}) collective-permute-start(bf16[64,512]{1,0:T(8,128)(2,1)S(1)} %get-tuple-element.50), channel_id=1, source_target_pairs={{0,8},{2,10},{4,12},{6,14},{8,0},{10,2},{12,4},{14,6},{16,24},{18,... | collective-permute-start | bytes 196616 | tf_op jit(solution)/shard_map/ppermute | solution.py:302
  98.6 1.3 %collective-permute-start.21 = (bf16[64,512]{1,0:T(8,128)(2,1)S(1)}, bf16[64,512]{1,0:T(8,128)(2,1)S(1)}, u32[]{:S(2)}, u32[]{:S(2)}) collective-permute-start(bf16[64,512]{1,0:T(8,128)(2,1)S(1)} %get-tuple-element.51), channel_id=1, source_target_pairs={{0,16},{2,18},{4,20},{6,22},{8,24},{10,26},{12,28},{14,30},{16,0},... | collective-permute-start | bytes 196616 | tf_op jit(solution)/shard_map/ppermute | solution.py:302
  99.8 1.4 %collective-permute-start.22 = (bf16[64,512]{1,0:T(8,128)(2,1)S(1)}, bf16[64,512]{1,0:T(8,128)(2,1)S(1)}, u32[]{:S(2)}, u32[]{:S(2)}) collective-permute-start(bf16[64,512]{1,0:T(8,128)(2,1)S(1)} %get-tuple-element.52), channel_id=1, source_target_pairs={{0,24},{2,26},{4,28},{6,30},{8,16},{10,18},{12,20},{14,22},{16,8},... | collective-permute-start | bytes 196616 | tf_op jit(solution)/shard_map/ppermute | solution.py:302
  101.3 5.4 %collective-permute-done.21.refs_2_ = bf16[64,512]{1,0:T(8,128)(2,1)S(1)} collective-permute-done((bf16[64,512]{1,0:T(8,128)(2,1)S(1)}, bf16[64,512]{1,0:T(8,128)(2,1)S(1)}, u32[]{:S(2)}, u32[]{:S(2)}) %collective-permute-start.21) | collective-permute-done | bytes 65568 | tf_op jit(solution)/shard_map/ppermute | solution.py:302
  106.7 1.4 %finish.1 = (f32[3,64,512]{2,1,0:T(8,128)}, f32[64,512]{1,0:T(8,128)}) custom-call(s32[3]{0:T(128)S(1)} %pad_add_fusion.pos_ref, bf16[64,512]{1,0:T(8,128)(2,1)S(1)} %get-tuple-element.49.refs_0_, bf16[64,512]{1,0:T(8,128)(2,1)S(1)} %collective-permute-done.20.refs_1_, bf16[64,512]{1,0:T(8,128)(2,1)S(1)} %collective-permute-done.21.refs_2_, ...), custom_call_target="tpu_custom_call" | custom-call | flops 1100000000 | bytes 1048576 | tf_op jit(solution)/shard_map/finish/pallas_call | solution.py:37
  108.1 0.8 add_convert_fusion
  (39 shorter events, 2.7 us)
Async XLA Ops:
  0.6 11.7 %copy-start.1 = (bf16[2,1,128,1024]{3,2,1,0:T(8,128)(2,1)S(1)}, bf16[2,1,128,1024]{3,2,1,0:T(8,128)(2,1)}, u32[]{:S(2)}) copy-start(bf16[2,1,128,1024]{3,2,1,0:T(8,128)(2,1)} %refs_5_.1) | copy-start | bytes 1572868
  0.6 11.7 %copy-start.2 = (bf16[2,1,128,1024]{3,2,1,0:T(8,128)(2,1)S(1)}, bf16[2,1,128,1024]{3,2,1,0:T(8,128)(2,1)}, u32[]{:S(2)}) copy-start(bf16[2,1,128,1024]{3,2,1,0:T(8,128)(2,1)} %refs_4_.3) | copy-start | bytes 1572868
  3.9 11.7 %copy-start.5 = (s32[16,8]{0,1:T(8,128)S(1)}, s32[16,8]{0,1:T(8,128)}, u32[]{:S(2)}) copy-start(s32[16,8]{0,1:T(8,128)} %param.16) | copy-start | bytes 1540
  3.9 35.7 %copy-start.4 = (s32[16]{0:T(128)S(1)}, s32[16]{0:T(128)}, u32[]{:S(2)}) copy-start(s32[16]{0:T(128)} %refs_1_.4) | copy-start | bytes 196
  3.9 32.8 %all-to-all-start = ((bf16[16,256,128]{2,1,0:T(8,128)(2,1)}), bf16[16,256,128]{2,1,0:T(8,128)(2,1)S(1)}, u32[]{:S(2)}, u32[]{:S(2)}) async-start(bf16[16,256,128]{2,1,0:T(8,128)(2,1)} %pack.1), calls=%async_computation | async-start | bytes 2097152 | tf_op jit(solution)/shard_map/all_to_all | solution.py:327
  13.0 0.7 copy-start.3
  13.7 40.2 %collective-permute-start.6 = (bf16[256,1024]{1,0:T(8,128)(2,1)S(1)}, bf16[256,1024]{1,0:T(8,128)(2,1)S(1)}, u32[]{:S(2)}, u32[]{:S(2)}) collective-permute-start(bf16[256,1024]{1,0:T(8,128)(2,1)S(1)} %get-tuple-element.36), channel_id=1, source_target_pairs={{0,8},{2,10},{4,12},{6,14},{8,0},{10,2},{12,4},{14,6},{16,24},{18,... | collective-permute-start | bytes 1572872 | tf_op jit(solution)/shard_map/ppermute | solution.py:302
  36.7 21.6 %collective-permute-start.8 = (bf16[128,1024]{1,0:T(8,128)(2,1)}, bf16[128,1024]{1,0:T(8,128)(2,1)S(1)}, u32[]{:S(2)}, u32[]{:S(2)}) collective-permute-start(bf16[128,1024]{1,0:T(8,128)(2,1)} %copy-done.3), channel_id=1, source_target_pairs={{0,16},{2,18},{4,20},{6,22},{8,24},{10,26},{12,28},{14,30},{16,0},... | collective-permute-start | bytes 786440 | tf_op jit(solution)/shard_map/ppermute | solution.py:302
  39.3 22.5 %collective-permute-start.12 = (bf16[128,1024]{1,0:T(8,128)(2,1)S(1)}, bf16[128,1024]{1,0:T(8,128)(2,1)S(1)}, u32[]{:S(2)}, u32[]{:S(2)}) collective-permute-start(bf16[128,1024]{1,0:T(8,128)(2,1)S(1)} %get-tuple-element.41), channel_id=1, source_target_pairs={{0,16},{2,18},{4,20},{6,22},{8,24},{10,26},{12,28},{14,30},{16,0},... | collective-permute-start | bytes 786440 | tf_op jit(solution)/shard_map/ppermute | solution.py:302
  52.5 9.4 %collective-permute-start = (bf16[4,256,128]{2,1,0:T(8,128)(2,1)S(1)}, bf16[4,256,128]{2,1,0:T(8,128)(2,1)S(1)}, u32[]{:S(2)}, u32[]{:S(2)}) collective-permute-start(bf16[4,256,128]{2,1,0:T(8,128)(2,1)S(1)} %get-tuple-element.30), channel_id=1, source_target_pairs={{0,2},{2,0},{4,6},{6,4},{8,10},{10,8},{12,14},{14,12},{16,18},{18,... | collective-permute-start | bytes 786440 | tf_op jit(solution)/shard_map/ppermute | solution.py:302
  53.8 20.6 %collective-permute-start.7 = (bf16[256,1024]{1,0:T(8,128)(2,1)S(1)}, bf16[256,1024]{1,0:T(8,128)(2,1)S(1)}, u32[]{:S(2)}, u32[]{:S(2)}) collective-permute-start(bf16[256,1024]{1,0:T(8,128)(2,1)S(1)} %collective-permute-done.6.refs_6_), channel_id=1, source_target_pairs={{0,1},{1,0},{2,3},{3,2},{4,5},{5,4},{6,7},{7,6},{8,9},{9,8},{10,11... | collective-permute-start | bytes 1572872 | tf_op jit(solution)/shard_map/ppermute | solution.py:320
  53.9 14.3 %collective-permute-start.1 = (bf16[4,256,128]{2,1,0:T(8,128)(2,1)S(1)}, bf16[4,256,128]{2,1,0:T(8,128)(2,1)S(1)}, u32[]{:S(2)}, u32[]{:S(2)}) collective-permute-start(bf16[4,256,128]{2,1,0:T(8,128)(2,1)S(1)} %get-tuple-element.31), channel_id=1, source_target_pairs={{0,4},{2,6},{4,0},{6,2},{8,12},{10,14},{12,8},{14,10},{16,20},{18,... | collective-permute-start | bytes 786440 | tf_op jit(solution)/shard_map/ppermute | solution.py:302
  58.2 9.9 %collective-permute-start.2 = (bf16[4,256,128]{2,1,0:T(8,128)(2,1)S(1)}, bf16[4,256,128]{2,1,0:T(8,128)(2,1)S(1)}, u32[]{:S(2)}, u32[]{:S(2)}) collective-permute-start(bf16[4,256,128]{2,1,0:T(8,128)(2,1)S(1)} %get-tuple-element.32), channel_id=1, source_target_pairs={{0,6},{2,4},{4,2},{6,0},{8,14},{10,12},{12,10},{14,8},{16,22},{18,... | collective-permute-start | bytes 786440 | tf_op jit(solution)/shard_map/ppermute | solution.py:302
  61.9 9.2 %collective-permute-start.10 = (bf16[128,1024]{1,0:T(8,128)(2,1)S(1)}, bf16[128,1024]{1,0:T(8,128)(2,1)S(1)}, u32[]{:S(2)}, u32[]{:S(2)}) collective-permute-start(bf16[128,1024]{1,0:T(8,128)(2,1)S(1)} %collective-permute-done.8.refs_8_), channel_id=1, source_target_pairs={{0,8},{2,10},{4,12},{6,14},{8,0},{10,2},{12,4},{14,6},{16,24},{18,... | collective-permute-start | bytes 786440 | tf_op jit(solution)/shard_map/ppermute | solution.py:302
  61.9 12.0 %collective-permute-start.14 = (bf16[128,1024]{1,0:T(8,128)(2,1)S(1)}, bf16[128,1024]{1,0:T(8,128)(2,1)S(1)}, u32[]{:S(2)}, u32[]{:S(2)}) collective-permute-start(bf16[128,1024]{1,0:T(8,128)(2,1)S(1)} %collective-permute-done.12.refs_12_), channel_id=1, source_target_pairs={{0,8},{2,10},{4,12},{6,14},{8,0},{10,2},{12,4},{14,6},{16,24},{18,... | collective-permute-start | bytes 786440 | tf_op jit(solution)/shard_map/ppermute | solution.py:302
  68.2 6.6 %collective-permute-start.13 = (bf16[128,1024]{1,0:T(8,128)(2,1)S(1)}, bf16[128,1024]{1,0:T(8,128)(2,1)S(1)}, u32[]{:S(2)}, u32[]{:S(2)}) collective-permute-start(bf16[128,1024]{1,0:T(8,128)(2,1)S(1)} %collective-permute-done.12.refs_12_), channel_id=1, source_target_pairs={{0,1},{1,0},{2,3},{3,2},{4,5},{5,4},{6,7},{7,6},{8,9},{9,8},{10,11... | collective-permute-start | bytes 786440 | tf_op jit(solution)/shard_map/ppermute | solution.py:320
  68.2 8.0 %collective-permute-start.9 = (bf16[128,1024]{1,0:T(8,128)(2,1)S(1)}, bf16[128,1024]{1,0:T(8,128)(2,1)S(1)}, u32[]{:S(2)}, u32[]{:S(2)}) collective-permute-start(bf16[128,1024]{1,0:T(8,128)(2,1)S(1)} %collective-permute-done.8.refs_8_), channel_id=1, source_target_pairs={{0,1},{1,0},{2,3},{3,2},{4,5},{5,4},{6,7},{7,6},{8,9},{9,8},{10,11... | collective-permute-start | bytes 786440 | tf_op jit(solution)/shard_map/ppermute | solution.py:320
  71.0 7.9 %collective-permute-start.11 = (bf16[128,1024]{1,0:T(8,128)(2,1)S(1)}, bf16[128,1024]{1,0:T(8,128)(2,1)S(1)}, u32[]{:S(2)}, u32[]{:S(2)}) collective-permute-start(bf16[128,1024]{1,0:T(8,128)(2,1)S(1)} %collective-permute-done.10.refs_10_), channel_id=1, source_target_pairs={{0,1},{1,0},{2,3},{3,2},{4,5},{5,4},{6,7},{7,6},{8,9},{9,8},{10,11... | collective-permute-start | bytes 786440 | tf_op jit(solution)/shard_map/ppermute | solution.py:320
  73.9 5.1 %collective-permute-start.15 = (bf16[128,1024]{1,0:T(8,128)(2,1)S(1)}, bf16[128,1024]{1,0:T(8,128)(2,1)S(1)}, u32[]{:S(2)}, u32[]{:S(2)}) collective-permute-start(bf16[128,1024]{1,0:T(8,128)(2,1)S(1)} %collective-permute-done.14.refs_14_), channel_id=1, source_target_pairs={{0,1},{1,0},{2,3},{3,2},{4,5},{5,4},{6,7},{7,6},{8,9},{9,8},{10,11... | collective-permute-start | bytes 786440 | tf_op jit(solution)/shard_map/ppermute | solution.py:320
  74.5 10.0 %collective-permute-start.3 = (bf16[4,192,128]{2,1,0:T(8,128)(2,1)S(1)}, bf16[4,192,128]{2,1,0:T(8,128)(2,1)S(1)}, u32[]{:S(2)}, u32[]{:S(2)}) collective-permute-start(bf16[4,192,128]{2,1,0:T(8,128)(2,1)S(1)} %get-tuple-element.33), channel_id=1, source_target_pairs={{0,8},{2,10},{4,12},{6,14},{8,0},{10,2},{12,4},{14,6},{16,24},{18,... | collective-permute-start | bytes 589832 | tf_op jit(solution)/shard_map/ppermute | solution.py:302
  74.8 17.1 %collective-permute-start.4 = (bf16[4,192,128]{2,1,0:T(8,128)(2,1)S(1)}, bf16[4,192,128]{2,1,0:T(8,128)(2,1)S(1)}, u32[]{:S(2)}, u32[]{:S(2)}) collective-permute-start(bf16[4,192,128]{2,1,0:T(8,128)(2,1)S(1)} %get-tuple-element.34), channel_id=1, source_target_pairs={{0,16},{2,18},{4,20},{6,22},{8,24},{10,26},{12,28},{14,30},{16,0},... | collective-permute-start | bytes 589832 | tf_op jit(solution)/shard_map/ppermute | solution.py:302
  76.2 15.8 %copy-start = (bf16[3,1024,512]{2,1,0:T(8,128)(2,1)S(1)}, bf16[3,1024,512]{2,1,0:T(8,128)(2,1)}, u32[]{:S(2)}) copy-start(bf16[3,1024,512]{2,1,0:T(8,128)(2,1)} %refs_7_.1) | copy-start | bytes 9437188
  76.2 15.8 %collective-permute-start.5 = (bf16[4,192,128]{2,1,0:T(8,128)(2,1)S(1)}, bf16[4,192,128]{2,1,0:T(8,128)(2,1)S(1)}, u32[]{:S(2)}, u32[]{:S(2)}) collective-permute-start(bf16[4,192,128]{2,1,0:T(8,128)(2,1)S(1)} %get-tuple-element.35), channel_id=1, source_target_pairs={{0,24},{2,26},{4,28},{6,30},{8,16},{10,18},{12,20},{14,22},{16,8},... | collective-permute-start | bytes 589832 | tf_op jit(solution)/shard_map/ppermute | solution.py:302
  81.1 12.5 %collective-permute-start.17 = (bf16[256,512]{1,0:T(8,128)(2,1)S(1)}, bf16[256,512]{1,0:T(8,128)(2,1)S(1)}, u32[]{:S(2)}, u32[]{:S(2)}) collective-permute-start(bf16[256,512]{1,0:T(8,128)(2,1)S(1)} %get-tuple-element.46), channel_id=1, source_target_pairs={{0,2},{2,0},{4,6},{6,4},{8,10},{10,8},{12,14},{14,12},{16,18},{18,... | collective-permute-start | bytes 786440 | tf_op jit(solution)/shard_map/ppermute | solution.py:302
  82.9 13.2 %collective-permute-start.18 = (bf16[256,512]{1,0:T(8,128)(2,1)S(1)}, bf16[256,512]{1,0:T(8,128)(2,1)S(1)}, u32[]{:S(2)}, u32[]{:S(2)}) collective-permute-start(bf16[256,512]{1,0:T(8,128)(2,1)S(1)} %get-tuple-element.47), channel_id=1, source_target_pairs={{0,4},{2,6},{4,0},{6,2},{8,12},{10,14},{12,8},{14,10},{16,20},{18,... | collective-permute-start | bytes 786440 | tf_op jit(solution)/shard_map/ppermute | solution.py:302
  84.4 11.7 %collective-permute-start.19 = (bf16[256,512]{1,0:T(8,128)(2,1)S(1)}, bf16[256,512]{1,0:T(8,128)(2,1)S(1)}, u32[]{:S(2)}, u32[]{:S(2)}) collective-permute-start(bf16[256,512]{1,0:T(8,128)(2,1)S(1)} %get-tuple-element.48), channel_id=1, source_target_pairs={{0,6},{2,4},{4,2},{6,0},{8,14},{10,12},{12,10},{14,8},{16,22},{18,... | collective-permute-start | bytes 786440 | tf_op jit(solution)/shard_map/ppermute | solution.py:302
  93.5 14.5 %collective-permute-start.16 = (f32[256,512]{1,0:T(8,128)S(1)}, f32[256,512]{1,0:T(8,128)S(1)}, u32[]{:S(2)}, u32[]{:S(2)}) collective-permute-start(f32[256,512]{1,0:T(8,128)S(1)} %get-tuple-element.45), channel_id=1, source_target_pairs={{0,1},{1,0},{2,3},{3,2},{4,5},{5,4},{6,7},{7,6},{8,9},{9,8},{10,11... | collective-permute-start | bytes 1572872 | tf_op jit(solution)/shard_map/ppermute | solution.py:320
  96.8 4.5 %collective-permute-start.20 = (bf16[64,512]{1,0:T(8,128)(2,1)S(1)}, bf16[64,512]{1,0:T(8,128)(2,1)S(1)}, u32[]{:S(2)}, u32[]{:S(2)}) collective-permute-start(bf16[64,512]{1,0:T(8,128)(2,1)S(1)} %get-tuple-element.50), channel_id=1, source_target_pairs={{0,8},{2,10},{4,12},{6,14},{8,0},{10,2},{12,4},{14,6},{16,24},{18,... | collective-permute-start | bytes 196616 | tf_op jit(solution)/shard_map/ppermute | solution.py:302
  98.6 8.1 %collective-permute-start.21 = (bf16[64,512]{1,0:T(8,128)(2,1)S(1)}, bf16[64,512]{1,0:T(8,128)(2,1)S(1)}, u32[]{:S(2)}, u32[]{:S(2)}) collective-permute-start(bf16[64,512]{1,0:T(8,128)(2,1)S(1)} %get-tuple-element.51), channel_id=1, source_target_pairs={{0,16},{2,18},{4,20},{6,22},{8,24},{10,26},{12,28},{14,30},{16,0},... | collective-permute-start | bytes 196616 | tf_op jit(solution)/shard_map/ppermute | solution.py:302
  99.8 6.8 %collective-permute-start.22 = (bf16[64,512]{1,0:T(8,128)(2,1)S(1)}, bf16[64,512]{1,0:T(8,128)(2,1)S(1)}, u32[]{:S(2)}, u32[]{:S(2)}) collective-permute-start(bf16[64,512]{1,0:T(8,128)(2,1)S(1)} %get-tuple-element.52), channel_id=1, source_target_pairs={{0,24},{2,26},{4,28},{6,30},{8,16},{10,18},{12,20},{14,22},{16,8},... | collective-permute-start | bytes 196616 | tf_op jit(solution)/shard_map/ppermute | solution.py:302

commit v5 on v4

--- a/solution.py
+++ b/solution.py
@@ -166,8 +166,8 @@
         inv = 1.0 / jnp.sum(total, axis=0, keepdims=True)
         att = (mul(v_col[:, window], p_buf[...]) * inv).astype(BF)
         d_wide = d_col.astype(F32)
-        delta = jnp.sum(att.astype(F32) * d_wide, axis=0, keepdims=True) * inv
         d_low = (d_wide * inv).astype(BF)
+        delta = jnp.sum(att.astype(F32) * d_low.astype(F32), axis=0, keepdims=True)
         dv_acc[window, :] += mul(p_buf[...], d_low.T)
         for j in range(span):
             rows = slice(j * LANE, (j + 1) * LANE)

time: 109 us -> 109 us (level)
  no operation moved by 1% of the time
where the time goes in v5:
time: 109 us
  waiting for transfers between devices  50.7 us (47%)
  starting transfers between devices  32.5 us (30%)
  Pallas kernels  23.2 us (21%)
    ppermute x17, waiting for transfers between devices, along(): return lax.ppermute(value, 'view', pairs)  29.7 us
    ppermute x17, starting transfers between devices, along(): return lax.ppermute(value, 'view', pairs)  23.6 us
    pallas_call x8, Pallas kernels, call(): pl.pallas_call(run, out_shape=[jax.ShapeDtypeStruct(dims, dtype) for dims...  23.2 us
    all_to_all x1, waiting for transfers between devices, split_body(): packed = lax.all_to_all(packed, 'view', 0, 0, tiled=True)  21 us
    all_to_all x1, starting transfers between devices, split_body(): packed = lax.all_to_all(packed, 'view', 0, 0, tiled=True)  8.32 us
  transfers between devices with their start and end apart: 24, of which 11 were waited for; matrix products, arithmetic and copies ran while one was open for 0% of the time, Pallas kernels for 18%

profile of v5, /device:TPU:0, one launch (start us, length us, event | category | flops | bytes accessed | tf_op | source)
XLA Modules:
  0.0 108.8 jit_solution(2305810962143307204)
XLA Ops:
  0.7 3.2 %pack.1 = bf16[16,256,128]{2,1,0:T(8,128)(2,1)} custom-call(s32[1]{0:T(128)} %constant.35.clone.1.pos_ref, bf16[2,1,128,512]{3,2,1,0:T(8,128)(2,1)} %refs_0_.3, bf16[2,1,128,512]{3,2,1,0:T(8,128)(2,1)} %refs_1_.3, bf16[2,1,128,512]{3,2,1,0:T(8,128)(2,1)} %refs_2_.1, bf16[2,1,128,1024]{3,2,1,0:T(8,128)(2,1)} %refs_5_.1, bf16[512,1024]{1,0:T(8,128)(2,1)} %refs_4_.2), custom_call_target="tpu_custom_call" | custom-call | flops 1100000000 | bytes 1048576 | tf_op jit(solution)/shard_map/pack/pallas_call | solution.py:37
  3.9 8.3 %all-to-all-start = ((bf16[16,256,128]{2,1,0:T(8,128)(2,1)}), bf16[16,256,128]{2,1,0:T(8,128)(2,1)S(1)}, u32[]{:S(2)}, u32[]{:S(2)}) async-start(bf16[16,256,128]{2,1,0:T(8,128)(2,1)} %pack.1), calls=%async_computation | async-start | bytes 2097152 | tf_op jit(solution)/shard_map/all_to_all | solution.py:327
  13.0 0.7 copy-done.3
  13.7 1.9 %collective-permute-start.6 = (bf16[256,1024]{1,0:T(8,128)(2,1)S(1)}, bf16[256,1024]{1,0:T(8,128)(2,1)S(1)}, u32[]{:S(2)}, u32[]{:S(2)}) collective-permute-start(bf16[256,1024]{1,0:T(8,128)(2,1)S(1)} %get-tuple-element.36), channel_id=1, source_target_pairs={{0,8},{2,10},{4,12},{6,14},{8,0},{10,2},{12,4},{14,6},{16,24},{18,... | collective-permute-start | bytes 1572872 | tf_op jit(solution)/shard_map/ppermute | solution.py:302
  15.6 21.0 %all-to-all-done.refs_2_ = bf16[16,256,128]{2,1,0:T(8,128)(2,1)S(1)} async-done(((bf16[16,256,128]{2,1,0:T(8,128)(2,1)}), bf16[16,256,128]{2,1,0:T(8,128)(2,1)S(1)}, u32[]{:S(2)}, u32[]{:S(2)}) %all-to-all-start) | async-done | bytes 1048608 | tf_op jit(solution)/shard_map/all_to_all | solution.py:327
  36.7 2.7 %collective-permute-start.8 = (bf16[128,1024]{1,0:T(8,128)(2,1)}, bf16[128,1024]{1,0:T(8,128)(2,1)S(1)}, u32[]{:S(2)}, u32[]{:S(2)}) collective-permute-start(bf16[128,1024]{1,0:T(8,128)(2,1)} %copy-done.3), channel_id=1, source_target_pairs={{0,16},{2,18},{4,20},{6,22},{8,24},{10,26},{12,28},{14,30},{16,0},... | collective-permute-start | bytes 786440 | tf_op jit(solution)/shard_map/ppermute | solution.py:302
  39.6 12.9 %attend.1 = (bf16[4,256,128]{2,1,0:T(8,128)(2,1)S(1)}, bf16[4,256,128]{2,1,0:T(8,128)(2,1)S(1)}, bf16[4,256,128]{2,1,0:T(8,128)(2,1)S(1)}, bf16[4,256,128]{2,1,0:T(8,128)(2,1)S(1)}) custom-call(s32[3]{0:T(128)S(1)} %pad_add_fusion.pos_ref, s32[16,8]{1,0:T(8,128)S(1)} %copy.12.refs_0_, s32[16]{0:T(128)S(1)} %copy-done.4, ...), custom_call_target="tpu_custom_call" | custom-call | flops 5500000256 | bytes 1048576 | tf_op jit(solution)/shard_map/attend/pallas_call | solution.py:37
  52.5 1.3 %collective-permute-start = (bf16[4,256,128]{2,1,0:T(8,128)(2,1)S(1)}, bf16[4,256,128]{2,1,0:T(8,128)(2,1)S(1)}, u32[]{:S(2)}, u32[]{:S(2)}) collective-permute-start(bf16[4,256,128]{2,1,0:T(8,128)(2,1)S(1)} %get-tuple-element.30), channel_id=1, source_target_pairs={{0,2},{2,0},{4,6},{6,4},{8,10},{10,8},{12,14},{14,12},{16,18},{18,... | collective-permute-start | bytes 786440 | tf_op jit(solution)/shard_map/ppermute | solution.py:302
  53.9 1.3 %collective-permute-start.1 = (bf16[4,256,128]{2,1,0:T(8,128)(2,1)S(1)}, bf16[4,256,128]{2,1,0:T(8,128)(2,1)S(1)}, u32[]{:S(2)}, u32[]{:S(2)}) collective-permute-start(bf16[4,256,128]{2,1,0:T(8,128)(2,1)S(1)} %get-tuple-element.31), channel_id=1, source_target_pairs={{0,4},{2,6},{4,0},{6,2},{8,12},{10,14},{12,8},{14,10},{16,20},{18,... | collective-permute-start | bytes 786440 | tf_op jit(solution)/shard_map/ppermute | solution.py:302
  55.1 3.1 %collective-permute-done.8.refs_8_ = bf16[128,1024]{1,0:T(8,128)(2,1)S(1)} collective-permute-done((bf16[128,1024]{1,0:T(8,128)(2,1)}, bf16[128,1024]{1,0:T(8,128)(2,1)S(1)}, u32[]{:S(2)}, u32[]{:S(2)}) %collective-permute-start.8) | collective-permute-done | bytes 262176 | tf_op jit(solution)/shard_map/ppermute | solution.py:302
  58.2 1.8 %collective-permute-start.2 = (bf16[4,256,128]{2,1,0:T(8,128)(2,1)S(1)}, bf16[4,256,128]{2,1,0:T(8,128)(2,1)S(1)}, u32[]{:S(2)}, u32[]{:S(2)}) collective-permute-start(bf16[4,256,128]{2,1,0:T(8,128)(2,1)S(1)} %get-tuple-element.32), channel_id=1, source_target_pairs={{0,6},{2,4},{4,2},{6,0},{8,14},{10,12},{12,10},{14,8},{16,22},{18,... | collective-permute-start | bytes 786440 | tf_op jit(solution)/shard_map/ppermute | solution.py:302
  60.1 1.8 %collective-permute-done.12.refs_12_ = bf16[128,1024]{1,0:T(8,128)(2,1)S(1)} collective-permute-done((bf16[128,1024]{1,0:T(8,128)(2,1)S(1)}, bf16[128,1024]{1,0:T(8,128)(2,1)S(1)}, u32[]{:S(2)}, u32[]{:S(2)}) %collective-permute-start.12) | collective-permute-done | bytes 262176 | tf_op jit(solution)/shard_map/ppermute | solution.py:302
  61.9 2.0 %collective-permute-start.14 = (bf16[128,1024]{1,0:T(8,128)(2,1)S(1)}, bf16[128,1024]{1,0:T(8,128)(2,1)S(1)}, u32[]{:S(2)}, u32[]{:S(2)}) collective-permute-start(bf16[128,1024]{1,0:T(8,128)(2,1)S(1)} %collective-permute-done.12.refs_12_), channel_id=1, source_target_pairs={{0,8},{2,10},{4,12},{6,14},{8,0},{10,2},{12,4},{14,6},{16,24},{18,... | collective-permute-start | bytes 786440 | tf_op jit(solution)/shard_map/ppermute | solution.py:302
  63.9 4.3 %collective-permute-done.1.refs_2_ = bf16[4,256,128]{2,1,0:T(8,128)(2,1)S(1)} collective-permute-done((bf16[4,256,128]{2,1,0:T(8,128)(2,1)S(1)}, bf16[4,256,128]{2,1,0:T(8,128)(2,1)S(1)}, u32[]{:S(2)}, u32[]{:S(2)}) %collective-permute-start.1) | collective-permute-done | bytes 262176 | tf_op jit(solution)/shard_map/ppermute | solution.py:302
  68.7 2.3 %collective-permute-done.10.refs_10_ = bf16[128,1024]{1,0:T(8,128)(2,1)S(1)} collective-permute-done((bf16[128,1024]{1,0:T(8,128)(2,1)S(1)}, bf16[128,1024]{1,0:T(8,128)(2,1)S(1)}, u32[]{:S(2)}, u32[]{:S(2)}) %collective-permute-start.10) | collective-permute-done | bytes 262176 | tf_op jit(solution)/shard_map/ppermute | solution.py:302
  71.0 2.8 %collective-permute-done.14.refs_14_ = bf16[128,1024]{1,0:T(8,128)(2,1)S(1)} collective-permute-done((bf16[128,1024]{1,0:T(8,128)(2,1)S(1)}, bf16[128,1024]{1,0:T(8,128)(2,1)S(1)}, u32[]{:S(2)}, u32[]{:S(2)}) %collective-permute-start.14) | collective-permute-done | bytes 262176 | tf_op jit(solution)/shard_map/ppermute | solution.py:302
  74.8 1.3 %collective-permute-start.4 = (bf16[4,192,128]{2,1,0:T(8,128)(2,1)S(1)}, bf16[4,192,128]{2,1,0:T(8,128)(2,1)S(1)}, u32[]{:S(2)}, u32[]{:S(2)}) collective-permute-start(bf16[4,192,128]{2,1,0:T(8,128)(2,1)S(1)} %get-tuple-element.34), channel_id=1, source_target_pairs={{0,16},{2,18},{4,20},{6,22},{8,24},{10,26},{12,28},{14,30},{16,0},... | collective-permute-start | bytes 589832 | tf_op jit(solution)/shard_map/ppermute | solution.py:302
  76.2 2.8 %collective-permute-start.5 = (bf16[4,192,128]{2,1,0:T(8,128)(2,1)S(1)}, bf16[4,192,128]{2,1,0:T(8,128)(2,1)S(1)}, u32[]{:S(2)}, u32[]{:S(2)}) collective-permute-start(bf16[4,192,128]{2,1,0:T(8,128)(2,1)S(1)} %get-tuple-element.35), channel_id=1, source_target_pairs={{0,24},{2,26},{4,28},{6,30},{8,16},{10,18},{12,20},{14,22},{16,8},... | collective-permute-start | bytes 589832 | tf_op jit(solution)/shard_map/ppermute | solution.py:302
  78.9 2.2 %weights.1 = (bf16[256,512]{1,0:T(8,128)(2,1)S(1)}, bf16[256,512]{1,0:T(8,128)(2,1)S(1)}, bf16[256,512]{1,0:T(8,128)(2,1)S(1)}, bf16[256,512]{1,0:T(8,128)(2,1)S(1)}) custom-call(s32[3]{0:T(128)S(1)} %pad_add_fusion.pos_ref, bf16[4,256,128]{2,1,0:T(8,128)(2,1)S(1)} %get-tuple-element.29.refs_0_, bf16[4,256,128]{2,1,0:T(8,128)(2,1)S(1)} %collective-permute-done.refs_1_, ...), custom_call_target="tpu_custom_call" | custom-call | flops 3300000000 | bytes 1048576 | tf_op jit(solution)/shard_map/weights/pallas_call | solution.py:37
  81.1 1.8 %collective-permute-start.17 = (bf16[256,512]{1,0:T(8,128)(2,1)S(1)}, bf16[256,512]{1,0:T(8,128)(2,1)S(1)}, u32[]{:S(2)}, u32[]{:S(2)}) collective-permute-start(bf16[256,512]{1,0:T(8,128)(2,1)S(1)} %get-tuple-element.46), channel_id=1, source_target_pairs={{0,2},{2,0},{4,6},{6,4},{8,10},{10,8},{12,14},{14,12},{16,18},{18,... | collective-permute-start | bytes 786440 | tf_op jit(solution)/shard_map/ppermute | solution.py:302
  82.9 1.5 %collective-permute-done.3.refs_4_ = bf16[4,192,128]{2,1,0:T(8,128)(2,1)S(1)} collective-permute-done((bf16[4,192,128]{2,1,0:T(8,128)(2,1)S(1)}, bf16[4,192,128]{2,1,0:T(8,128)(2,1)S(1)}, u32[]{:S(2)}, u32[]{:S(2)}) %collective-permute-start.3) | collective-permute-done | bytes 196640 | tf_op jit(solution)/shard_map/ppermute | solution.py:302
  84.4 1.6 %collective-permute-start.19 = (bf16[256,512]{1,0:T(8,128)(2,1)S(1)}, bf16[256,512]{1,0:T(8,128)(2,1)S(1)}, u32[]{:S(2)}, u32[]{:S(2)}) collective-permute-start(bf16[256,512]{1,0:T(8,128)(2,1)S(1)} %get-tuple-element.48), channel_id=1, source_target_pairs={{0,6},{2,4},{4,2},{6,0},{8,14},{10,12},{12,10},{14,8},{16,22},{18,... | collective-permute-start | bytes 786440 | tf_op jit(solution)/shard_map/ppermute | solution.py:302
  86.0 5.9 %collective-permute-done.4.refs_5_ = bf16[4,192,128]{2,1,0:T(8,128)(2,1)S(1)} collective-permute-done((bf16[4,192,128]{2,1,0:T(8,128)(2,1)S(1)}, bf16[4,192,128]{2,1,0:T(8,128)(2,1)S(1)}, u32[]{:S(2)}, u32[]{:S(2)}) %collective-permute-start.4) | collective-permute-done | bytes 196640 | tf_op jit(solution)/shard_map/ppermute | solution.py:302
  91.9 1.6 %inputs.1 = (f32[256,512]{1,0:T(8,128)S(1)}, f32[256,512]{1,0:T(8,128)S(1)}) custom-call(s32[3]{0:T(128)S(1)} %pad_add_fusion.pos_ref, bf16[4,256,128]{2,1,0:T(8,128)(2,1)S(1)} %get-tuple-element.29.refs_0_, bf16[4,256,128]{2,1,0:T(8,128)(2,1)S(1)} %collective-permute-done.refs_1_, bf16[4,256,128]{2,1,0:T(8,128)(2,1)S(1)} %collective-permute-done.1.refs_2_, ...), custom_call_target="tpu_custom_call" | custom-call | flops 2200000000 | bytes 1048576 | tf_op jit(solution)/shard_map/inputs/pallas_call | solution.py:37
  93.6 2.5 %collective-permute-done.18.refs_2_ = bf16[256,512]{1,0:T(8,128)(2,1)S(1)} collective-permute-done((bf16[256,512]{1,0:T(8,128)(2,1)S(1)}, bf16[256,512]{1,0:T(8,128)(2,1)S(1)}, u32[]{:S(2)}, u32[]{:S(2)}) %collective-permute-start.18) | collective-permute-done | bytes 262176 | tf_op jit(solution)/shard_map/ppermute | solution.py:302
  96.1 0.7 plane_sum.1
  96.8 1.8 %collective-permute-start.20 = (bf16[64,512]{1,0:T(8,128)(2,1)S(1)}, bf16[64,512]{1,0:T(8,128)(2,1)S(1)}, u32[]{:S(2)}, u32[]{:S(2)}) collective-permute-start(bf16[64,512]{1,0:T(8,128)(2,1)S(1)} %get-tuple-element.50), channel_id=1, source_target_pairs={{0,8},{2,10},{4,12},{6,14},{8,0},{10,2},{12,4},{14,6},{16,24},{18,... | collective-permute-start | bytes 196616 | tf_op jit(solution)/shard_map/ppermute | solution.py:302
  98.6 1.3 %collective-permute-start.21 = (bf16[64,512]{1,0:T(8,128)(2,1)S(1)}, bf16[64,512]{1,0:T(8,128)(2,1)S(1)}, u32[]{:S(2)}, u32[]{:S(2)}) collective-permute-start(bf16[64,512]{1,0:T(8,128)(2,1)S(1)} %get-tuple-element.51), channel_id=1, source_target_pairs={{0,16},{2,18},{4,20},{6,22},{8,24},{10,26},{12,28},{14,30},{16,0},... | collective-permute-start | bytes 196616 | tf_op jit(solution)/shard_map/ppermute | solution.py:302
  99.8 1.4 %collective-permute-start.22 = (bf16[64,512]{1,0:T(8,128)(2,1)S(1)}, bf16[64,512]{1,0:T(8,128)(2,1)S(1)}, u32[]{:S(2)}, u32[]{:S(2)}) collective-permute-start(bf16[64,512]{1,0:T(8,128)(2,1)S(1)} %get-tuple-element.52), channel_id=1, source_target_pairs={{0,24},{2,26},{4,28},{6,30},{8,16},{10,18},{12,20},{14,22},{16,8},... | collective-permute-start | bytes 196616 | tf_op jit(solution)/shard_map/ppermute | solution.py:302
  101.3 5.4 %collective-permute-done.21.refs_2_ = bf16[64,512]{1,0:T(8,128)(2,1)S(1)} collective-permute-done((bf16[64,512]{1,0:T(8,128)(2,1)S(1)}, bf16[64,512]{1,0:T(8,128)(2,1)S(1)}, u32[]{:S(2)}, u32[]{:S(2)}) %collective-permute-start.21) | collective-permute-done | bytes 65568 | tf_op jit(solution)/shard_map/ppermute | solution.py:302
  106.7 1.4 %finish.1 = (f32[3,64,512]{2,1,0:T(8,128)}, f32[64,512]{1,0:T(8,128)}) custom-call(s32[3]{0:T(128)S(1)} %pad_add_fusion.pos_ref, bf16[64,512]{1,0:T(8,128)(2,1)S(1)} %get-tuple-element.49.refs_0_, bf16[64,512]{1,0:T(8,128)(2,1)S(1)} %collective-permute-done.20.refs_1_, bf16[64,512]{1,0:T(8,128)(2,1)S(1)} %collective-permute-done.21.refs_2_, ...), custom_call_target="tpu_custom_call" | custom-call | flops 1100000000 | bytes 1048576 | tf_op jit(solution)/shard_map/finish/pallas_call | solution.py:37
  108.1 0.8 add_convert_fusion
  (39 shorter events, 2.7 us)
Async XLA Ops:
  0.6 11.7 %copy-start.1 = (bf16[2,1,128,1024]{3,2,1,0:T(8,128)(2,1)S(1)}, bf16[2,1,128,1024]{3,2,1,0:T(8,128)(2,1)}, u32[]{:S(2)}) copy-start(bf16[2,1,128,1024]{3,2,1,0:T(8,128)(2,1)} %refs_5_.1) | copy-start | bytes 1572868
  0.6 11.7 %copy-start.2 = (bf16[2,1,128,1024]{3,2,1,0:T(8,128)(2,1)S(1)}, bf16[2,1,128,1024]{3,2,1,0:T(8,128)(2,1)}, u32[]{:S(2)}) copy-start(bf16[2,1,128,1024]{3,2,1,0:T(8,128)(2,1)} %refs_4_.3) | copy-start | bytes 1572868
  3.9 11.7 %copy-start.5 = (s32[16,8]{0,1:T(8,128)S(1)}, s32[16,8]{0,1:T(8,128)}, u32[]{:S(2)}) copy-start(s32[16,8]{0,1:T(8,128)} %param.16) | copy-start | bytes 1540
  3.9 35.7 %copy-start.4 = (s32[16]{0:T(128)S(1)}, s32[16]{0:T(128)}, u32[]{:S(2)}) copy-start(s32[16]{0:T(128)} %refs_1_.4) | copy-start | bytes 196
  3.9 32.8 %all-to-all-start = ((bf16[16,256,128]{2,1,0:T(8,128)(2,1)}), bf16[16,256,128]{2,1,0:T(8,128)(2,1)S(1)}, u32[]{:S(2)}, u32[]{:S(2)}) async-start(bf16[16,256,128]{2,1,0:T(8,128)(2,1)} %pack.1), calls=%async_computation | async-start | bytes 2097152 | tf_op jit(solution)/shard_map/all_to_all | solution.py:327
  13.0 0.7 copy-start.3
  13.7 40.2 %collective-permute-start.6 = (bf16[256,1024]{1,0:T(8,128)(2,1)S(1)}, bf16[256,1024]{1,0:T(8,128)(2,1)S(1)}, u32[]{:S(2)}, u32[]{:S(2)}) collective-permute-start(bf16[256,1024]{1,0:T(8,128)(2,1)S(1)} %get-tuple-element.36), channel_id=1, source_target_pairs={{0,8},{2,10},{4,12},{6,14},{8,0},{10,2},{12,4},{14,6},{16,24},{18,... | collective-permute-start | bytes 1572872 | tf_op jit(solution)/shard_map/ppermute | solution.py:302
  36.7 21.6 %collective-permute-start.8 = (bf16[128,1024]{1,0:T(8,128)(2,1)}, bf16[128,1024]{1,0:T(8,128)(2,1)S(1)}, u32[]{:S(2)}, u32[]{:S(2)}) collective-permute-start(bf16[128,1024]{1,0:T(8,128)(2,1)} %copy-done.3), channel_id=1, source_target_pairs={{0,16},{2,18},{4,20},{6,22},{8,24},{10,26},{12,28},{14,30},{16,0},... | collective-permute-start | bytes 786440 | tf_op jit(solution)/shard_map/ppermute | solution.py:302
  39.3 22.5 %collective-permute-start.12 = (bf16[128,1024]{1,0:T(8,128)(2,1)S(1)}, bf16[128,1024]{1,0:T(8,128)(2,1)S(1)}, u32[]{:S(2)}, u32[]{:S(2)}) collective-permute-start(bf16[128,1024]{1,0:T(8,128)(2,1)S(1)} %get-tuple-element.41), channel_id=1, source_target_pairs={{0,16},{2,18},{4,20},{6,22},{8,24},{10,26},{12,28},{14,30},{16,0},... | collective-permute-start | bytes 786440 | tf_op jit(solution)/shard_map/ppermute | solution.py:302
  52.5 9.4 %collective-permute-start = (bf16[4,256,128]{2,1,0:T(8,128)(2,1)S(1)}, bf16[4,256,128]{2,1,0:T(8,128)(2,1)S(1)}, u32[]{:S(2)}, u32[]{:S(2)}) collective-permute-start(bf16[4,256,128]{2,1,0:T(8,128)(2,1)S(1)} %get-tuple-element.30), channel_id=1, source_target_pairs={{0,2},{2,0},{4,6},{6,4},{8,10},{10,8},{12,14},{14,12},{16,18},{18,... | collective-permute-start | bytes 786440 | tf_op jit(solution)/shard_map/ppermute | solution.py:302
  53.9 20.6 %collective-permute-start.7 = (bf16[256,1024]{1,0:T(8,128)(2,1)S(1)}, bf16[256,1024]{1,0:T(8,128)(2,1)S(1)}, u32[]{:S(2)}, u32[]{:S(2)}) collective-permute-start(bf16[256,1024]{1,0:T(8,128)(2,1)S(1)} %collective-permute-done.6.refs_6_), channel_id=1, source_target_pairs={{0,1},{1,0},{2,3},{3,2},{4,5},{5,4},{6,7},{7,6},{8,9},{9,8},{10,11... | collective-permute-start | bytes 1572872 | tf_op jit(solution)/shard_map/ppermute | solution.py:320
  53.9 14.3 %collective-permute-start.1 = (bf16[4,256,128]{2,1,0:T(8,128)(2,1)S(1)}, bf16[4,256,128]{2,1,0:T(8,128)(2,1)S(1)}, u32[]{:S(2)}, u32[]{:S(2)}) collective-permute-start(bf16[4,256,128]{2,1,0:T(8,128)(2,1)S(1)} %get-tuple-element.31), channel_id=1, source_target_pairs={{0,4},{2,6},{4,0},{6,2},{8,12},{10,14},{12,8},{14,10},{16,20},{18,... | collective-permute-start | bytes 786440 | tf_op jit(solution)/shard_map/ppermute | solution.py:302
  58.2 10.0 %collective-permute-start.2 = (bf16[4,256,128]{2,1,0:T(8,128)(2,1)S(1)}, bf16[4,256,128]{2,1,0:T(8,128)(2,1)S(1)}, u32[]{:S(2)}, u32[]{:S(2)}) collective-permute-start(bf16[4,256,128]{2,1,0:T(8,128)(2,1)S(1)} %get-tuple-element.32), channel_id=1, source_target_pairs={{0,6},{2,4},{4,2},{6,0},{8,14},{10,12},{12,10},{14,8},{16,22},{18,... | collective-permute-start | bytes 786440 | tf_op jit(solution)/shard_map/ppermute | solution.py:302
  61.9 9.2 %collective-permute-start.10 = (bf16[128,1024]{1,0:T(8,128)(2,1)S(1)}, bf16[128,1024]{1,0:T(8,128)(2,1)S(1)}, u32[]{:S(2)}, u32[]{:S(2)}) collective-permute-start(bf16[128,1024]{1,0:T(8,128)(2,1)S(1)} %collective-permute-done.8.refs_8_), channel_id=1, source_target_pairs={{0,8},{2,10},{4,12},{6,14},{8,0},{10,2},{12,4},{14,6},{16,24},{18,... | collective-permute-start | bytes 786440 | tf_op jit(solution)/shard_map/ppermute | solution.py:302
  61.9 12.0 %collective-permute-start.14 = (bf16[128,1024]{1,0:T(8,128)(2,1)S(1)}, bf16[128,1024]{1,0:T(8,128)(2,1)S(1)}, u32[]{:S(2)}, u32[]{:S(2)}) collective-permute-start(bf16[128,1024]{1,0:T(8,128)(2,1)S(1)} %collective-permute-done.12.refs_12_), channel_id=1, source_target_pairs={{0,8},{2,10},{4,12},{6,14},{8,0},{10,2},{12,4},{14,6},{16,24},{18,... | collective-permute-start | bytes 786440 | tf_op jit(solution)/shard_map/ppermute | solution.py:302
  68.2 6.6 %collective-permute-start.13 = (bf16[128,1024]{1,0:T(8,128)(2,1)S(1)}, bf16[128,1024]{1,0:T(8,128)(2,1)S(1)}, u32[]{:S(2)}, u32[]{:S(2)}) collective-permute-start(bf16[128,1024]{1,0:T(8,128)(2,1)S(1)} %collective-permute-done.12.refs_12_), channel_id=1, source_target_pairs={{0,1},{1,0},{2,3},{3,2},{4,5},{5,4},{6,7},{7,6},{8,9},{9,8},{10,11... | collective-permute-start | bytes 786440 | tf_op jit(solution)/shard_map/ppermute | solution.py:320
  68.2 7.9 %collective-permute-start.9 = (bf16[128,1024]{1,0:T(8,128)(2,1)S(1)}, bf16[128,1024]{1,0:T(8,128)(2,1)S(1)}, u32[]{:S(2)}, u32[]{:S(2)}) collective-permute-start(bf16[128,1024]{1,0:T(8,128)(2,1)S(1)} %collective-permute-done.8.refs_8_), channel_id=1, source_target_pairs={{0,1},{1,0},{2,3},{3,2},{4,5},{5,4},{6,7},{7,6},{8,9},{9,8},{10,11... | collective-permute-start | bytes 786440 | tf_op jit(solution)/shard_map/ppermute | solution.py:320
  71.0 7.9 %collective-permute-start.11 = (bf16[128,1024]{1,0:T(8,128)(2,1)S(1)}, bf16[128,1024]{1,0:T(8,128)(2,1)S(1)}, u32[]{:S(2)}, u32[]{:S(2)}) collective-permute-start(bf16[128,1024]{1,0:T(8,128)(2,1)S(1)} %collective-permute-done.10.refs_10_), channel_id=1, source_target_pairs={{0,1},{1,0},{2,3},{3,2},{4,5},{5,4},{6,7},{7,6},{8,9},{9,8},{10,11... | collective-permute-start | bytes 786440 | tf_op jit(solution)/shard_map/ppermute | solution.py:320
  73.9 5.1 %collective-permute-start.15 = (bf16[128,1024]{1,0:T(8,128)(2,1)S(1)}, bf16[128,1024]{1,0:T(8,128)(2,1)S(1)}, u32[]{:S(2)}, u32[]{:S(2)}) collective-permute-start(bf16[128,1024]{1,0:T(8,128)(2,1)S(1)} %collective-permute-done.14.refs_14_), channel_id=1, source_target_pairs={{0,1},{1,0},{2,3},{3,2},{4,5},{5,4},{6,7},{7,6},{8,9},{9,8},{10,11... | collective-permute-start | bytes 786440 | tf_op jit(solution)/shard_map/ppermute | solution.py:320
  74.5 10.0 %collective-permute-start.3 = (bf16[4,192,128]{2,1,0:T(8,128)(2,1)S(1)}, bf16[4,192,128]{2,1,0:T(8,128)(2,1)S(1)}, u32[]{:S(2)}, u32[]{:S(2)}) collective-permute-start(bf16[4,192,128]{2,1,0:T(8,128)(2,1)S(1)} %get-tuple-element.33), channel_id=1, source_target_pairs={{0,8},{2,10},{4,12},{6,14},{8,0},{10,2},{12,4},{14,6},{16,24},{18,... | collective-permute-start | bytes 589832 | tf_op jit(solution)/shard_map/ppermute | solution.py:302
  74.8 17.1 %collective-permute-start.4 = (bf16[4,192,128]{2,1,0:T(8,128)(2,1)S(1)}, bf16[4,192,128]{2,1,0:T(8,128)(2,1)S(1)}, u32[]{:S(2)}, u32[]{:S(2)}) collective-permute-start(bf16[4,192,128]{2,1,0:T(8,128)(2,1)S(1)} %get-tuple-element.34), channel_id=1, source_target_pairs={{0,16},{2,18},{4,20},{6,22},{8,24},{10,26},{12,28},{14,30},{16,0},... | collective-permute-start | bytes 589832 | tf_op jit(solution)/shard_map/ppermute | solution.py:302
  76.2 15.8 %copy-start = (bf16[3,1024,512]{2,1,0:T(8,128)(2,1)S(1)}, bf16[3,1024,512]{2,1,0:T(8,128)(2,1)}, u32[]{:S(2)}) copy-start(bf16[3,1024,512]{2,1,0:T(8,128)(2,1)} %refs_7_.1) | copy-start | bytes 9437188
  76.2 15.8 %collective-permute-start.5 = (bf16[4,192,128]{2,1,0:T(8,128)(2,1)S(1)}, bf16[4,192,128]{2,1,0:T(8,128)(2,1)S(1)}, u32[]{:S(2)}, u32[]{:S(2)}) collective-permute-start(bf16[4,192,128]{2,1,0:T(8,128)(2,1)S(1)} %get-tuple-element.35), channel_id=1, source_target_pairs={{0,24},{2,26},{4,28},{6,30},{8,16},{10,18},{12,20},{14,22},{16,8},... | collective-permute-start | bytes 589832 | tf_op jit(solution)/shard_map/ppermute | solution.py:302
  81.1 12.5 %collective-permute-start.17 = (bf16[256,512]{1,0:T(8,128)(2,1)S(1)}, bf16[256,512]{1,0:T(8,128)(2,1)S(1)}, u32[]{:S(2)}, u32[]{:S(2)}) collective-permute-start(bf16[256,512]{1,0:T(8,128)(2,1)S(1)} %get-tuple-element.46), channel_id=1, source_target_pairs={{0,2},{2,0},{4,6},{6,4},{8,10},{10,8},{12,14},{14,12},{16,18},{18,... | collective-permute-start | bytes 786440 | tf_op jit(solution)/shard_map/ppermute | solution.py:302
  82.9 13.2 %collective-permute-start.18 = (bf16[256,512]{1,0:T(8,128)(2,1)S(1)}, bf16[256,512]{1,0:T(8,128)(2,1)S(1)}, u32[]{:S(2)}, u32[]{:S(2)}) collective-permute-start(bf16[256,512]{1,0:T(8,128)(2,1)S(1)} %get-tuple-element.47), channel_id=1, source_target_pairs={{0,4},{2,6},{4,0},{6,2},{8,12},{10,14},{12,8},{14,10},{16,20},{18,... | collective-permute-start | bytes 786440 | tf_op jit(solution)/shard_map/ppermute | solution.py:302
  84.4 11.7 %collective-permute-start.19 = (bf16[256,512]{1,0:T(8,128)(2,1)S(1)}, bf16[256,512]{1,0:T(8,128)(2,1)S(1)}, u32[]{:S(2)}, u32[]{:S(2)}) collective-permute-start(bf16[256,512]{1,0:T(8,128)(2,1)S(1)} %get-tuple-element.48), channel_id=1, source_target_pairs={{0,6},{2,4},{4,2},{6,0},{8,14},{10,12},{12,10},{14,8},{16,22},{18,... | collective-permute-start | bytes 786440 | tf_op jit(solution)/shard_map/ppermute | solution.py:302
  93.5 14.5 %collective-permute-start.16 = (f32[256,512]{1,0:T(8,128)S(1)}, f32[256,512]{1,0:T(8,128)S(1)}, u32[]{:S(2)}, u32[]{:S(2)}) collective-permute-start(f32[256,512]{1,0:T(8,128)S(1)} %get-tuple-element.45), channel_id=1, source_target_pairs={{0,1},{1,0},{2,3},{3,2},{4,5},{5,4},{6,7},{7,6},{8,9},{9,8},{10,11... | collective-permute-start | bytes 1572872 | tf_op jit(solution)/shard_map/ppermute | solution.py:320
  96.8 4.5 %collective-permute-start.20 = (bf16[64,512]{1,0:T(8,128)(2,1)S(1)}, bf16[64,512]{1,0:T(8,128)(2,1)S(1)}, u32[]{:S(2)}, u32[]{:S(2)}) collective-permute-start(bf16[64,512]{1,0:T(8,128)(2,1)S(1)} %get-tuple-element.50), channel_id=1, source_target_pairs={{0,8},{2,10},{4,12},{6,14},{8,0},{10,2},{12,4},{14,6},{16,24},{18,... | collective-permute-start | bytes 196616 | tf_op jit(solution)/shard_map/ppermute | solution.py:302
  98.6 8.1 %collective-permute-start.21 = (bf16[64,512]{1,0:T(8,128)(2,1)S(1)}, bf16[64,512]{1,0:T(8,128)(2,1)S(1)}, u32[]{:S(2)}, u32[]{:S(2)}) collective-permute-start(bf16[64,512]{1,0:T(8,128)(2,1)S(1)} %get-tuple-element.51), channel_id=1, source_target_pairs={{0,16},{2,18},{4,20},{6,22},{8,24},{10,26},{12,28},{14,30},{16,0},... | collective-permute-start | bytes 196616 | tf_op jit(solution)/shard_map/ppermute | solution.py:302
  99.8 6.8 %collective-permute-start.22 = (bf16[64,512]{1,0:T(8,128)(2,1)S(1)}, bf16[64,512]{1,0:T(8,128)(2,1)S(1)}, u32[]{:S(2)}, u32[]{:S(2)}) collective-permute-start(bf16[64,512]{1,0:T(8,128)(2,1)S(1)} %get-tuple-element.52), channel_id=1, source_target_pairs={{0,24},{2,26},{4,28},{6,30},{8,16},{10,18},{12,20},{14,22},{16,8},... | collective-permute-start | bytes 196616 | tf_op jit(solution)/shard_map/ppermute | solution.py:302

commit v6 on v5

--- a/solution.py
+++ b/solution.py
@@ -41,7 +41,7 @@
         out_specs=out_specs,
         scratch_shapes=[pltpu.VMEM(dims, dtype) for dims, dtype in scratch] + [pltpu.SemaphoreType.DMA(())] * sems,
         compiler_params=pltpu.CompilerParams(vmem_limit_bytes=mib * MIB),
-        cost_estimate=pl.CostEstimate(flops=int(us * 1.1e9), bytes_accessed=MIB, transcendentals=0),
+        cost_estimate=pl.CostEstimate(flops=int({'attend': 0.2, 'weights': 8, 'early': 1, 'turn': 8, 'inputs': 8, 'plane_sum': 8, 'finish': 1, 'pack': 3, 'fetch': 8}.get(name, us) * 1.1e9), bytes_accessed=MIB, transcendentals=0),
         name=name,
     )(pos, *args, *after)
 
@@ -89,8 +89,8 @@
         both[n * LANE : (n + 1) * LANE] = out[...]
 
 
-def gate(value, after):
-    return lax.optimization_barrier((value, after))[0]
+def gate(value, *after):
+    return lax.optimization_barrier((value, *after))[0]
 
 
 def places(refs, mine):
@@ -337,16 +337,19 @@
             ((span, rows, 2 * rows), F32), ((span * rows, 2 * rows), BF), ((span * rows, 2 * rows), BF),
             ((cameras, HD, rows), BF), ((cameras, HD, rows), BF),
         ],
-        32, 5, scalars=2, after=[],
+        32, 13, scalars=2, after=[],
     )(pos)
     done = blocks[0]
     blocks = over_plane(blocks)
     first = over_column([gate(own[1], packed)], 2)[0]
     second = over_column([gate(own[2], packed)], 2)[0]
-    for far in (first, second):
-        column += [far, other_core(far)]
-        far = over_column([gate(far, done)], 1)[0]
-        column += [far, other_core(far)]
+    column += [first, other_core(first)]
+    first = over_column([gate(first, done)], 1)[0]
+    grads = call(functools.partial(turn_kernel, planes), "turn", [((QUAD, 3 * HD, rows), BF)] * (planes - 1), blocks, after=())(pos)
+    column += [first, other_core(first)]
+    column += [second, other_core(second)]
+    second = over_column([gate(second, done)], 1)[0]
+    column += [second, other_core(second)]
 
     depth = 2 * planes * rows
     terms = call(
@@ -363,11 +366,10 @@
         over_column(terms),
     )(pos)
 
-    grads = call(functools.partial(turn_kernel, planes), "turn", [((QUAD, 3 * HD, rows), BF)] * (planes - 1), blocks, after=())(pos)
     args = blocks + over_column(grads, 1) + [w_qkv]
     mine, theirs = call(
         functools.partial(inputs_kernel, planes), "inputs", [((scenes * rows, model // 2), F32)] * 2, args,
-        [((scenes, 3, width, rows), BF)], 32, 2, after=started,
+        [((scenes, 3, width, rows), BF)], 32, 2,
     )(pos)
     d_tokens = (mine + other_core(theirs)).astype(BF).reshape(scenes, 1, rows, model // 2)
     return (d_tokens, d_wqkv, d_wo.T)

time: 109 us -> 108 us (level)
  waiting for transfers between devices: 50.7 us -> 49 us
  transfers between devices with their start and end apart: 24 -> 24, of which waited for: 11 -> 10; matrix products, arithmetic and copies ran while one was open for 0% -> 1% of each run, Pallas kernels for 18% -> 18%
where the time goes in v6:
time: 108 us
  waiting for transfers between devices  49 us (45%)
  starting transfers between devices  32.4 us (30%)
  Pallas kernels  23.5 us (22%)
  local copies, waits for them, and re-layouts  1.49 us (1%)
    ppermute x17, waiting for transfers between devices, along(): return lax.ppermute(value, 'view', pairs)  28.7 us
    pallas_call x8, Pallas kernels, call(): pl.pallas_call(run, out_shape=[jax.ShapeDtypeStruct(dims, dtype) for dims...  23.5 us
    ppermute x17, starting transfers between devices, along(): return lax.ppermute(value, 'view', pairs)  23.5 us
    all_to_all x1, waiting for transfers between devices, split_body(): packed = lax.all_to_all(packed, 'view', 0, 0, tiled=True)  20.4 us
    all_to_all x1, starting transfers between devices, split_body(): packed = lax.all_to_all(packed, 'view', 0, 0, tiled=True)  8.32 us
  transfers between devices with their start and end apart: 24, of which 10 were waited for; matrix products, arithmetic and copies ran while one was open for 1% of the time, Pallas kernels for 18%

profile of v6, /device:TPU:0, one launch (start us, length us, event | category | flops | bytes accessed | tf_op | source)
XLA Modules:
  0.0 108.1 jit_solution(361012362932310460)
XLA Ops:
  0.7 3.2 %pack.1 = bf16[16,256,128]{2,1,0:T(8,128)(2,1)} custom-call(s32[1]{0:T(128)} %constant.35.clone.1.pos_ref, bf16[2,1,128,512]{3,2,1,0:T(8,128)(2,1)} %refs_0_.3, bf16[2,1,128,512]{3,2,1,0:T(8,128)(2,1)} %refs_1_.3, bf16[2,1,128,512]{3,2,1,0:T(8,128)(2,1)} %refs_2_.1, bf16[2,1,128,1024]{3,2,1,0:T(8,128)(2,1)} %refs_5_.1, bf16[512,1024]{1,0:T(8,128)(2,1)} %refs_4_.2), custom_call_target="tpu_custom_call" | custom-call | flops 3300000000 | bytes 1048576 | tf_op jit(solution)/shard_map/pack/pallas_call | solution.py:37
  3.9 8.3 %all-to-all-start = ((bf16[16,256,128]{2,1,0:T(8,128)(2,1)}), bf16[16,256,128]{2,1,0:T(8,128)(2,1)S(1)}, u32[]{:S(2)}, u32[]{:S(2)}) async-start(bf16[16,256,128]{2,1,0:T(8,128)(2,1)} %pack.1), calls=%async_computation | async-start | bytes 2097152 | tf_op jit(solution)/shard_map/all_to_all | solution.py:327
  13.0 0.7 copy-done.4
  13.7 0.7 copy-done.5
  14.4 1.9 %collective-permute-start.7 = (bf16[256,1024]{1,0:T(8,128)(2,1)S(1)}, bf16[256,1024]{1,0:T(8,128)(2,1)S(1)}, u32[]{:S(2)}, u32[]{:S(2)}) collective-permute-start(bf16[256,1024]{1,0:T(8,128)(2,1)S(1)} %get-tuple-element.38), channel_id=1, source_target_pairs={{0,8},{2,10},{4,12},{6,14},{8,0},{10,2},{12,4},{14,6},{16,24},{18,... | collective-permute-start | bytes 1572872 | tf_op jit(solution)/shard_map/ppermute | solution.py:302
  16.3 20.4 %all-to-all-done.refs_2_ = bf16[16,256,128]{2,1,0:T(8,128)(2,1)S(1)} async-done(((bf16[16,256,128]{2,1,0:T(8,128)(2,1)}), bf16[16,256,128]{2,1,0:T(8,128)(2,1)S(1)}, u32[]{:S(2)}, u32[]{:S(2)}) %all-to-all-start) | async-done | bytes 1048608 | tf_op jit(solution)/shard_map/all_to_all | solution.py:327
  36.6 2.7 %collective-permute-start.9 = (bf16[128,1024]{1,0:T(8,128)(2,1)}, bf16[128,1024]{1,0:T(8,128)(2,1)S(1)}, u32[]{:S(2)}, u32[]{:S(2)}) collective-permute-start(bf16[128,1024]{1,0:T(8,128)(2,1)} %copy-done.5), channel_id=1, source_target_pairs={{0,16},{2,18},{4,20},{6,22},{8,24},{10,26},{12,28},{14,30},{16,0},... | collective-permute-start | bytes 786440 | tf_op jit(solution)/shard_map/ppermute | solution.py:302
  39.6 12.9 %attend.1 = (bf16[4,256,128]{2,1,0:T(8,128)(2,1)S(1)}, bf16[4,256,128]{2,1,0:T(8,128)(2,1)S(1)}, bf16[4,256,128]{2,1,0:T(8,128)(2,1)S(1)}, bf16[4,256,128]{2,1,0:T(8,128)(2,1)S(1)}) custom-call(s32[3]{0:T(128)S(1)} %pad_add_fusion.pos_ref, s32[16,8]{1,0:T(8,128)S(1)} %copy.12.refs_0_, s32[16]{0:T(128)S(1)} %copy-done, ...), custom_call_target="tpu_custom_call" | custom-call | flops 220000000 | bytes 1048576 | tf_op jit(solution)/shard_map/attend/pallas_call | solution.py:37
  52.5 1.3 %collective-permute-start = (bf16[4,256,128]{2,1,0:T(8,128)(2,1)S(1)}, bf16[4,256,128]{2,1,0:T(8,128)(2,1)S(1)}, u32[]{:S(2)}, u32[]{:S(2)}) collective-permute-start(bf16[4,256,128]{2,1,0:T(8,128)(2,1)S(1)} %get-tuple-element.30), channel_id=1, source_target_pairs={{0,2},{2,0},{4,6},{6,4},{8,10},{10,8},{12,14},{14,12},{16,18},{18,... | collective-permute-start | bytes 786440 | tf_op jit(solution)/shard_map/ppermute | solution.py:302
  53.8 1.3 %collective-permute-start.1 = (bf16[4,256,128]{2,1,0:T(8,128)(2,1)S(1)}, bf16[4,256,128]{2,1,0:T(8,128)(2,1)S(1)}, u32[]{:S(2)}, u32[]{:S(2)}) collective-permute-start(bf16[4,256,128]{2,1,0:T(8,128)(2,1)S(1)} %get-tuple-element.31), channel_id=1, source_target_pairs={{0,4},{2,6},{4,0},{6,2},{8,12},{10,14},{12,8},{14,10},{16,20},{18,... | collective-permute-start | bytes 786440 | tf_op jit(solution)/shard_map/ppermute | solution.py:302
  55.1 3.1 %collective-permute-done.9.refs_8_ = bf16[128,1024]{1,0:T(8,128)(2,1)S(1)} collective-permute-done((bf16[128,1024]{1,0:T(8,128)(2,1)}, bf16[128,1024]{1,0:T(8,128)(2,1)S(1)}, u32[]{:S(2)}, u32[]{:S(2)}) %collective-permute-start.9) | collective-permute-done | bytes 262176 | tf_op jit(solution)/shard_map/ppermute | solution.py:302
  58.2 1.8 %collective-permute-start.2 = (bf16[4,256,128]{2,1,0:T(8,128)(2,1)S(1)}, bf16[4,256,128]{2,1,0:T(8,128)(2,1)S(1)}, u32[]{:S(2)}, u32[]{:S(2)}) collective-permute-start(bf16[4,256,128]{2,1,0:T(8,128)(2,1)S(1)} %get-tuple-element.32), channel_id=1, source_target_pairs={{0,6},{2,4},{4,2},{6,0},{8,14},{10,12},{12,10},{14,8},{16,22},{18,... | collective-permute-start | bytes 786440 | tf_op jit(solution)/shard_map/ppermute | solution.py:302
  60.1 1.9 %collective-permute-done.13.refs_12_ = bf16[128,1024]{1,0:T(8,128)(2,1)} collective-permute-done((bf16[128,1024]{1,0:T(8,128)(2,1)}, bf16[128,1024]{1,0:T(8,128)(2,1)}, u32[]{:S(2)}, u32[]{:S(2)}) %collective-permute-start.13) | collective-permute-done | bytes 262176 | tf_op jit(solution)/shard_map/ppermute | solution.py:302
  62.0 2.0 %collective-permute-start.15 = (bf16[128,1024]{1,0:T(8,128)(2,1)}, bf16[128,1024]{1,0:T(8,128)(2,1)S(1)}, u32[]{:S(2)}, u32[]{:S(2)}) collective-permute-start(bf16[128,1024]{1,0:T(8,128)(2,1)} %collective-permute-done.13.refs_12_), channel_id=1, source_target_pairs={{0,8},{2,10},{4,12},{6,14},{8,0},{10,2},{12,4},{14,6},{16,24},{18,... | collective-permute-start | bytes 786440 | tf_op jit(solution)/shard_map/ppermute | solution.py:302
  64.0 2.1 %collective-permute-done.1.refs_2_ = bf16[4,256,128]{2,1,0:T(8,128)(2,1)S(1)} collective-permute-done((bf16[4,256,128]{2,1,0:T(8,128)(2,1)S(1)}, bf16[4,256,128]{2,1,0:T(8,128)(2,1)S(1)}, u32[]{:S(2)}, u32[]{:S(2)}) %collective-permute-start.1) | collective-permute-done | bytes 262176 | tf_op jit(solution)/shard_map/ppermute | solution.py:302
  66.6 4.5 %collective-permute-done.11.refs_10_ = bf16[128,1024]{1,0:T(8,128)(2,1)S(1)} collective-permute-done((bf16[128,1024]{1,0:T(8,128)(2,1)S(1)}, bf16[128,1024]{1,0:T(8,128)(2,1)S(1)}, u32[]{:S(2)}, u32[]{:S(2)}) %collective-permute-start.11) | collective-permute-done | bytes 262176 | tf_op jit(solution)/shard_map/ppermute | solution.py:302
  71.1 2.8 %collective-permute-done.15.refs_14_ = bf16[128,1024]{1,0:T(8,128)(2,1)S(1)} collective-permute-done((bf16[128,1024]{1,0:T(8,128)(2,1)}, bf16[128,1024]{1,0:T(8,128)(2,1)S(1)}, u32[]{:S(2)}, u32[]{:S(2)}) %collective-permute-start.15) | collective-permute-done | bytes 262176 | tf_op jit(solution)/shard_map/ppermute | solution.py:302
  74.9 1.3 %collective-permute-start.4 = (bf16[4,192,128]{2,1,0:T(8,128)(2,1)S(1)}, bf16[4,192,128]{2,1,0:T(8,128)(2,1)S(1)}, u32[]{:S(2)}, u32[]{:S(2)}) collective-permute-start(bf16[4,192,128]{2,1,0:T(8,128)(2,1)S(1)} %get-tuple-element.34), channel_id=1, source_target_pairs={{0,16},{2,18},{4,20},{6,22},{8,24},{10,26},{12,28},{14,30},{16,0},... | collective-permute-start | bytes 589832 | tf_op jit(solution)/shard_map/ppermute | solution.py:302
  76.2 2.8 %collective-permute-start.5 = (bf16[4,192,128]{2,1,0:T(8,128)(2,1)S(1)}, bf16[4,192,128]{2,1,0:T(8,128)(2,1)S(1)}, u32[]{:S(2)}, u32[]{:S(2)}) collective-permute-start(bf16[4,192,128]{2,1,0:T(8,128)(2,1)S(1)} %get-tuple-element.35), channel_id=1, source_target_pairs={{0,24},{2,26},{4,28},{6,30},{8,16},{10,18},{12,20},{14,22},{16,8},... | collective-permute-start | bytes 589832 | tf_op jit(solution)/shard_map/ppermute | solution.py:302
  79.0 2.6 %weights.1 = (bf16[256,512]{1,0:T(8,128)(2,1)S(1)}, bf16[256,512]{1,0:T(8,128)(2,1)S(1)}, bf16[256,512]{1,0:T(8,128)(2,1)S(1)}, bf16[256,512]{1,0:T(8,128)(2,1)S(1)}) custom-call(s32[3]{0:T(128)S(1)} %pad_add_fusion.pos_ref, bf16[4,256,128]{2,1,0:T(8,128)(2,1)S(1)} %get-tuple-element.29.refs_0_, bf16[4,256,128]{2,1,0:T(8,128)(2,1)S(1)} %collective-permute-done.refs_1_, ...), custom_call_target="tpu_custom_call" | custom-call | flops 8800000000 | bytes 1048576 | tf_op jit(solution)/shard_map/weights/pallas_call | solution.py:37
  81.6 1.8 %collective-permute-start.17 = (bf16[256,512]{1,0:T(8,128)(2,1)S(1)}, bf16[256,512]{1,0:T(8,128)(2,1)S(1)}, u32[]{:S(2)}, u32[]{:S(2)}) collective-permute-start(bf16[256,512]{1,0:T(8,128)(2,1)S(1)} %get-tuple-element.46), channel_id=1, source_target_pairs={{0,2},{2,0},{4,6},{6,4},{8,10},{10,8},{12,14},{14,12},{16,18},{18,... | collective-permute-start | bytes 786440 | tf_op jit(solution)/shard_map/ppermute | solution.py:302
  83.4 1.1 %collective-permute-done.3.refs_4_ = bf16[4,192,128]{2,1,0:T(8,128)(2,1)S(1)} collective-permute-done((bf16[4,192,128]{2,1,0:T(8,128)(2,1)S(1)}, bf16[4,192,128]{2,1,0:T(8,128)(2,1)S(1)}, u32[]{:S(2)}, u32[]{:S(2)}) %collective-permute-start.3) | collective-permute-done | bytes 196640 | tf_op jit(solution)/shard_map/ppermute | solution.py:302
  84.5 1.5 %collective-permute-start.19 = (bf16[256,512]{1,0:T(8,128)(2,1)S(1)}, bf16[256,512]{1,0:T(8,128)(2,1)S(1)}, u32[]{:S(2)}, u32[]{:S(2)}) collective-permute-start(bf16[256,512]{1,0:T(8,128)(2,1)S(1)} %get-tuple-element.48), channel_id=1, source_target_pairs={{0,6},{2,4},{4,2},{6,0},{8,14},{10,12},{12,10},{14,8},{16,22},{18,... | collective-permute-start | bytes 786440 | tf_op jit(solution)/shard_map/ppermute | solution.py:302
  86.0 6.0 %collective-permute-done.4.refs_5_ = bf16[4,192,128]{2,1,0:T(8,128)(2,1)S(1)} collective-permute-done((bf16[4,192,128]{2,1,0:T(8,128)(2,1)S(1)}, bf16[4,192,128]{2,1,0:T(8,128)(2,1)S(1)}, u32[]{:S(2)}, u32[]{:S(2)}) %collective-permute-start.4) | collective-permute-done | bytes 196640 | tf_op jit(solution)/shard_map/ppermute | solution.py:302
  92.0 1.6 %inputs.1 = (f32[256,512]{1,0:T(8,128)S(1)}, f32[256,512]{1,0:T(8,128)S(1)}) custom-call(s32[3]{0:T(128)S(1)} %pad_add_fusion.pos_ref, bf16[4,256,128]{2,1,0:T(8,128)(2,1)S(1)} %get-tuple-element.29.refs_0_, bf16[4,256,128]{2,1,0:T(8,128)(2,1)S(1)} %collective-permute-done.refs_1_, bf16[4,256,128]{2,1,0:T(8,128)(2,1)S(1)} %collective-permute-done.1.refs_2_, ...), custom_call_target="tpu_custom_call" | custom-call | flops 8800000000 | bytes 1048576 | tf_op jit(solution)/shard_map/inputs/pallas_call | solution.py:37
  93.7 2.9 %collective-permute-done.18.refs_2_ = bf16[256,512]{1,0:T(8,128)(2,1)S(1)} collective-permute-done((bf16[256,512]{1,0:T(8,128)(2,1)S(1)}, bf16[256,512]{1,0:T(8,128)(2,1)S(1)}, u32[]{:S(2)}, u32[]{:S(2)}) %collective-permute-start.18) | collective-permute-done | bytes 262176 | tf_op jit(solution)/shard_map/ppermute | solution.py:302
  97.3 1.4 %collective-permute-start.20 = (bf16[64,512]{1,0:T(8,128)(2,1)S(1)}, bf16[64,512]{1,0:T(8,128)(2,1)S(1)}, u32[]{:S(2)}, u32[]{:S(2)}) collective-permute-start(bf16[64,512]{1,0:T(8,128)(2,1)S(1)} %get-tuple-element.50), channel_id=1, source_target_pairs={{0,8},{2,10},{4,12},{6,14},{8,0},{10,2},{12,4},{14,6},{16,24},{18,... | collective-permute-start | bytes 196616 | tf_op jit(solution)/shard_map/ppermute | solution.py:302
  98.6 1.7 %collective-permute-start.21 = (bf16[64,512]{1,0:T(8,128)(2,1)S(1)}, bf16[64,512]{1,0:T(8,128)(2,1)S(1)}, u32[]{:S(2)}, u32[]{:S(2)}) collective-permute-start(bf16[64,512]{1,0:T(8,128)(2,1)S(1)} %get-tuple-element.51), channel_id=1, source_target_pairs={{0,16},{2,18},{4,20},{6,22},{8,24},{10,26},{12,28},{14,30},{16,0},... | collective-permute-start | bytes 196616 | tf_op jit(solution)/shard_map/ppermute | solution.py:302
  100.3 1.4 %collective-permute-start.22 = (bf16[64,512]{1,0:T(8,128)(2,1)S(1)}, bf16[64,512]{1,0:T(8,128)(2,1)S(1)}, u32[]{:S(2)}, u32[]{:S(2)}) collective-permute-start(bf16[64,512]{1,0:T(8,128)(2,1)S(1)} %get-tuple-element.52), channel_id=1, source_target_pairs={{0,24},{2,26},{4,28},{6,30},{8,16},{10,18},{12,20},{14,22},{16,8},... | collective-permute-start | bytes 196616 | tf_op jit(solution)/shard_map/ppermute | solution.py:302
  101.7 0.8 add_convert_fusion
  102.5 4.2 %collective-permute-done.21.refs_2_ = bf16[64,512]{1,0:T(8,128)(2,1)S(1)} collective-permute-done((bf16[64,512]{1,0:T(8,128)(2,1)S(1)}, bf16[64,512]{1,0:T(8,128)(2,1)S(1)}, u32[]{:S(2)}, u32[]{:S(2)}) %collective-permute-start.21) | collective-permute-done | bytes 65568 | tf_op jit(solution)/shard_map/ppermute | solution.py:302
  106.7 1.4 %finish.1 = (f32[3,64,512]{2,1,0:T(8,128)}, f32[64,512]{1,0:T(8,128)}) custom-call(s32[3]{0:T(128)S(1)} %pad_add_fusion.pos_ref, bf16[64,512]{1,0:T(8,128)(2,1)S(1)} %get-tuple-element.49.refs_0_, bf16[64,512]{1,0:T(8,128)(2,1)S(1)} %collective-permute-done.20.refs_1_, bf16[64,512]{1,0:T(8,128)(2,1)S(1)} %collective-permute-done.21.refs_2_, ...), custom_call_target="tpu_custom_call" | custom-call | flops 1100000000 | bytes 1048576 | tf_op jit(solution)/shard_map/finish/pallas_call | solution.py:37
  (41 shorter events, 3.3 us)
Async XLA Ops:
  0.6 11.7 %copy-start.2 = (bf16[2,1,128,1024]{3,2,1,0:T(8,128)(2,1)S(1)}, bf16[2,1,128,1024]{3,2,1,0:T(8,128)(2,1)}, u32[]{:S(2)}) copy-start(bf16[2,1,128,1024]{3,2,1,0:T(8,128)(2,1)} %refs_5_.1) | copy-start | bytes 1572868
  0.6 11.6 %copy-start.3 = (bf16[2,1,128,1024]{3,2,1,0:T(8,128)(2,1)S(1)}, bf16[2,1,128,1024]{3,2,1,0:T(8,128)(2,1)}, u32[]{:S(2)}) copy-start(bf16[2,1,128,1024]{3,2,1,0:T(8,128)(2,1)} %refs_4_.3) | copy-start | bytes 1572868
  3.9 32.8 %all-to-all-start = ((bf16[16,256,128]{2,1,0:T(8,128)(2,1)}), bf16[16,256,128]{2,1,0:T(8,128)(2,1)S(1)}, u32[]{:S(2)}, u32[]{:S(2)}) async-start(bf16[16,256,128]{2,1,0:T(8,128)(2,1)} %pack.1), calls=%async_computation | async-start | bytes 2097152 | tf_op jit(solution)/shard_map/all_to_all | solution.py:327
  12.3 27.3 %copy-start.6 = (s32[16,8]{0,1:T(8,128)S(1)}, s32[16,8]{0,1:T(8,128)}, u32[]{:S(2)}) copy-start(s32[16,8]{0,1:T(8,128)} %param.16) | copy-start | bytes 1540
  12.3 27.3 %copy-start = (s32[16]{0:T(128)S(1)}, s32[16]{0:T(128)}, u32[]{:S(2)}) copy-start(s32[16]{0:T(128)} %refs_1_.4) | copy-start | bytes 196
  12.9 0.7 copy-start.4
  13.7 0.7 copy-start.5
  14.4 47.6 %collective-permute-start.7 = (bf16[256,1024]{1,0:T(8,128)(2,1)S(1)}, bf16[256,1024]{1,0:T(8,128)(2,1)S(1)}, u32[]{:S(2)}, u32[]{:S(2)}) collective-permute-start(bf16[256,1024]{1,0:T(8,128)(2,1)S(1)} %get-tuple-element.38), channel_id=1, source_target_pairs={{0,8},{2,10},{4,12},{6,14},{8,0},{10,2},{12,4},{14,6},{16,24},{18,... | collective-permute-start | bytes 1572872 | tf_op jit(solution)/shard_map/ppermute | solution.py:302
  36.6 21.6 %collective-permute-start.9 = (bf16[128,1024]{1,0:T(8,128)(2,1)}, bf16[128,1024]{1,0:T(8,128)(2,1)S(1)}, u32[]{:S(2)}, u32[]{:S(2)}) collective-permute-start(bf16[128,1024]{1,0:T(8,128)(2,1)} %copy-done.5), channel_id=1, source_target_pairs={{0,16},{2,18},{4,20},{6,22},{8,24},{10,26},{12,28},{14,30},{16,0},... | collective-permute-start | bytes 786440 | tf_op jit(solution)/shard_map/ppermute | solution.py:302
  39.3 22.6 %collective-permute-start.13 = (bf16[128,1024]{1,0:T(8,128)(2,1)}, bf16[128,1024]{1,0:T(8,128)(2,1)}, u32[]{:S(2)}, u32[]{:S(2)}) collective-permute-start(bf16[128,1024]{1,0:T(8,128)(2,1)} %copy-done.4), channel_id=1, source_target_pairs={{0,16},{2,18},{4,20},{6,22},{8,24},{10,26},{12,28},{14,30},{16,0},... | collective-permute-start | bytes 786440 | tf_op jit(solution)/shard_map/ppermute | solution.py:302
  52.5 11.5 %collective-permute-start = (bf16[4,256,128]{2,1,0:T(8,128)(2,1)S(1)}, bf16[4,256,128]{2,1,0:T(8,128)(2,1)S(1)}, u32[]{:S(2)}, u32[]{:S(2)}) collective-permute-start(bf16[4,256,128]{2,1,0:T(8,128)(2,1)S(1)} %get-tuple-element.30), channel_id=1, source_target_pairs={{0,2},{2,0},{4,6},{6,4},{8,10},{10,8},{12,14},{14,12},{16,18},{18,... | collective-permute-start | bytes 786440 | tf_op jit(solution)/shard_map/ppermute | solution.py:302
  53.8 12.2 %collective-permute-start.1 = (bf16[4,256,128]{2,1,0:T(8,128)(2,1)S(1)}, bf16[4,256,128]{2,1,0:T(8,128)(2,1)S(1)}, u32[]{:S(2)}, u32[]{:S(2)}) collective-permute-start(bf16[4,256,128]{2,1,0:T(8,128)(2,1)S(1)} %get-tuple-element.31), channel_id=1, source_target_pairs={{0,4},{2,6},{4,0},{6,2},{8,12},{10,14},{12,8},{14,10},{16,20},{18,... | collective-permute-start | bytes 786440 | tf_op jit(solution)/shard_map/ppermute | solution.py:302
  58.2 7.9 %collective-permute-start.2 = (bf16[4,256,128]{2,1,0:T(8,128)(2,1)S(1)}, bf16[4,256,128]{2,1,0:T(8,128)(2,1)S(1)}, u32[]{:S(2)}, u32[]{:S(2)}) collective-permute-start(bf16[4,256,128]{2,1,0:T(8,128)(2,1)S(1)} %get-tuple-element.32), channel_id=1, source_target_pairs={{0,6},{2,4},{4,2},{6,0},{8,14},{10,12},{12,10},{14,8},{16,22},{18,... | collective-permute-start | bytes 786440 | tf_op jit(solution)/shard_map/ppermute | solution.py:302
  62.0 9.2 %collective-permute-start.11 = (bf16[128,1024]{1,0:T(8,128)(2,1)S(1)}, bf16[128,1024]{1,0:T(8,128)(2,1)S(1)}, u32[]{:S(2)}, u32[]{:S(2)}) collective-permute-start(bf16[128,1024]{1,0:T(8,128)(2,1)S(1)} %collective-permute-done.9.refs_8_), channel_id=1, source_target_pairs={{0,8},{2,10},{4,12},{6,14},{8,0},{10,2},{12,4},{14,6},{16,24},{18,... | collective-permute-start | bytes 786440 | tf_op jit(solution)/shard_map/ppermute | solution.py:302
  62.0 12.0 %collective-permute-start.15 = (bf16[128,1024]{1,0:T(8,128)(2,1)}, bf16[128,1024]{1,0:T(8,128)(2,1)S(1)}, u32[]{:S(2)}, u32[]{:S(2)}) collective-permute-start(bf16[128,1024]{1,0:T(8,128)(2,1)} %collective-permute-done.13.refs_12_), channel_id=1, source_target_pairs={{0,8},{2,10},{4,12},{6,14},{8,0},{10,2},{12,4},{14,6},{16,24},{18,... | collective-permute-start | bytes 786440 | tf_op jit(solution)/shard_map/ppermute | solution.py:302
  64.0 10.5 %collective-permute-start.8 = (bf16[256,1024]{1,0:T(8,128)(2,1)S(1)}, bf16[256,1024]{1,0:T(8,128)(2,1)S(1)}, u32[]{:S(2)}, u32[]{:S(2)}) collective-permute-start(bf16[256,1024]{1,0:T(8,128)(2,1)S(1)} %collective-permute-done.7.refs_6_), channel_id=1, source_target_pairs={{0,1},{1,0},{2,3},{3,2},{4,5},{5,4},{6,7},{7,6},{8,9},{9,8},{10,11... | collective-permute-start | bytes 1572872 | tf_op jit(solution)/shard_map/ppermute | solution.py:320
  66.1 8.8 %collective-permute-start.10 = (bf16[128,1024]{1,0:T(8,128)(2,1)S(1)}, bf16[128,1024]{1,0:T(8,128)(2,1)S(1)}, u32[]{:S(2)}, u32[]{:S(2)}) collective-permute-start(bf16[128,1024]{1,0:T(8,128)(2,1)S(1)} %collective-permute-done.9.refs_8_), channel_id=1, source_target_pairs={{0,1},{1,0},{2,3},{3,2},{4,5},{5,4},{6,7},{7,6},{8,9},{9,8},{10,11... | collective-permute-start | bytes 786440 | tf_op jit(solution)/shard_map/ppermute | solution.py:320
  66.1 10.1 %collective-permute-start.14 = (bf16[128,1024]{1,0:T(8,128)(2,1)}, bf16[128,1024]{1,0:T(8,128)(2,1)S(1)}, u32[]{:S(2)}, u32[]{:S(2)}) collective-permute-start(bf16[128,1024]{1,0:T(8,128)(2,1)} %collective-permute-done.13.refs_12_), channel_id=1, source_target_pairs={{0,1},{1,0},{2,3},{3,2},{4,5},{5,4},{6,7},{7,6},{8,9},{9,8},{10,11... | collective-permute-start | bytes 786440 | tf_op jit(solution)/shard_map/ppermute | solution.py:320
  71.1 7.9 %collective-permute-start.12 = (bf16[128,1024]{1,0:T(8,128)(2,1)S(1)}, bf16[128,1024]{1,0:T(8,128)(2,1)S(1)}, u32[]{:S(2)}, u32[]{:S(2)}) collective-permute-start(bf16[128,1024]{1,0:T(8,128)(2,1)S(1)} %collective-permute-done.11.refs_10_), channel_id=1, source_target_pairs={{0,1},{1,0},{2,3},{3,2},{4,5},{5,4},{6,7},{7,6},{8,9},{9,8},{10,11... | collective-permute-start | bytes 786440 | tf_op jit(solution)/shard_map/ppermute | solution.py:320
  73.9 5.1 %collective-permute-start.16 = (bf16[128,1024]{1,0:T(8,128)(2,1)S(1)}, bf16[128,1024]{1,0:T(8,128)(2,1)S(1)}, u32[]{:S(2)}, u32[]{:S(2)}) collective-permute-start(bf16[128,1024]{1,0:T(8,128)(2,1)S(1)} %collective-permute-done.15.refs_14_), channel_id=1, source_target_pairs={{0,1},{1,0},{2,3},{3,2},{4,5},{5,4},{6,7},{7,6},{8,9},{9,8},{10,11... | collective-permute-start | bytes 786440 | tf_op jit(solution)/shard_map/ppermute | solution.py:320
  74.5 9.9 %collective-permute-start.3 = (bf16[4,192,128]{2,1,0:T(8,128)(2,1)S(1)}, bf16[4,192,128]{2,1,0:T(8,128)(2,1)S(1)}, u32[]{:S(2)}, u32[]{:S(2)}) collective-permute-start(bf16[4,192,128]{2,1,0:T(8,128)(2,1)S(1)} %get-tuple-element.33), channel_id=1, source_target_pairs={{0,8},{2,10},{4,12},{6,14},{8,0},{10,2},{12,4},{14,6},{16,24},{18,... | collective-permute-start | bytes 589832 | tf_op jit(solution)/shard_map/ppermute | solution.py:302
  74.9 17.1 %collective-permute-start.4 = (bf16[4,192,128]{2,1,0:T(8,128)(2,1)S(1)}, bf16[4,192,128]{2,1,0:T(8,128)(2,1)S(1)}, u32[]{:S(2)}, u32[]{:S(2)}) collective-permute-start(bf16[4,192,128]{2,1,0:T(8,128)(2,1)S(1)} %get-tuple-element.34), channel_id=1, source_target_pairs={{0,16},{2,18},{4,20},{6,22},{8,24},{10,26},{12,28},{14,30},{16,0},... | collective-permute-start | bytes 589832 | tf_op jit(solution)/shard_map/ppermute | solution.py:302
  76.2 15.8 %copy-start.1 = (bf16[3,1024,512]{2,1,0:T(8,128)(2,1)S(1)}, bf16[3,1024,512]{2,1,0:T(8,128)(2,1)}, u32[]{:S(2)}) copy-start(bf16[3,1024,512]{2,1,0:T(8,128)(2,1)} %refs_7_.1) | copy-start | bytes 9437188
  76.2 15.8 %collective-permute-start.5 = (bf16[4,192,128]{2,1,0:T(8,128)(2,1)S(1)}, bf16[4,192,128]{2,1,0:T(8,128)(2,1)S(1)}, u32[]{:S(2)}, u32[]{:S(2)}) collective-permute-start(bf16[4,192,128]{2,1,0:T(8,128)(2,1)S(1)} %get-tuple-element.35), channel_id=1, source_target_pairs={{0,24},{2,26},{4,28},{6,30},{8,16},{10,18},{12,20},{14,22},{16,8},... | collective-permute-start | bytes 589832 | tf_op jit(solution)/shard_map/ppermute | solution.py:302
  81.6 12.1 %collective-permute-start.17 = (bf16[256,512]{1,0:T(8,128)(2,1)S(1)}, bf16[256,512]{1,0:T(8,128)(2,1)S(1)}, u32[]{:S(2)}, u32[]{:S(2)}) collective-permute-start(bf16[256,512]{1,0:T(8,128)(2,1)S(1)} %get-tuple-element.46), channel_id=1, source_target_pairs={{0,2},{2,0},{4,6},{6,4},{8,10},{10,8},{12,14},{14,12},{16,18},{18,... | collective-permute-start | bytes 786440 | tf_op jit(solution)/shard_map/ppermute | solution.py:302
  83.3 13.2 %collective-permute-start.18 = (bf16[256,512]{1,0:T(8,128)(2,1)S(1)}, bf16[256,512]{1,0:T(8,128)(2,1)S(1)}, u32[]{:S(2)}, u32[]{:S(2)}) collective-permute-start(bf16[256,512]{1,0:T(8,128)(2,1)S(1)} %get-tuple-element.47), channel_id=1, source_target_pairs={{0,4},{2,6},{4,0},{6,2},{8,12},{10,14},{12,8},{14,10},{16,20},{18,... | collective-permute-start | bytes 786440 | tf_op jit(solution)/shard_map/ppermute | solution.py:302
  84.5 12.1 %collective-permute-start.19 = (bf16[256,512]{1,0:T(8,128)(2,1)S(1)}, bf16[256,512]{1,0:T(8,128)(2,1)S(1)}, u32[]{:S(2)}, u32[]{:S(2)}) collective-permute-start(bf16[256,512]{1,0:T(8,128)(2,1)S(1)} %get-tuple-element.48), channel_id=1, source_target_pairs={{0,6},{2,4},{4,2},{6,0},{8,14},{10,12},{12,10},{14,8},{16,22},{18,... | collective-permute-start | bytes 786440 | tf_op jit(solution)/shard_map/ppermute | solution.py:302
  93.6 8.1 %collective-permute-start.6 = (f32[256,512]{1,0:T(8,128)S(1)}, f32[256,512]{1,0:T(8,128)S(1)}, u32[]{:S(2)}, u32[]{:S(2)}) collective-permute-start(f32[256,512]{1,0:T(8,128)S(1)} %get-tuple-element.37), channel_id=1, source_target_pairs={{0,1},{1,0},{2,3},{3,2},{4,5},{5,4},{6,7},{7,6},{8,9},{9,8},{10,11... | collective-permute-start | bytes 1572872 | tf_op jit(solution)/shard_map/ppermute | solution.py:320
  97.3 5.2 %collective-permute-start.20 = (bf16[64,512]{1,0:T(8,128)(2,1)S(1)}, bf16[64,512]{1,0:T(8,128)(2,1)S(1)}, u32[]{:S(2)}, u32[]{:S(2)}) collective-permute-start(bf16[64,512]{1,0:T(8,128)(2,1)S(1)} %get-tuple-element.50), channel_id=1, source_target_pairs={{0,8},{2,10},{4,12},{6,14},{8,0},{10,2},{12,4},{14,6},{16,24},{18,... | collective-permute-start | bytes 196616 | tf_op jit(solution)/shard_map/ppermute | solution.py:302
  98.6 8.1 %collective-permute-start.21 = (bf16[64,512]{1,0:T(8,128)(2,1)S(1)}, bf16[64,512]{1,0:T(8,128)(2,1)S(1)}, u32[]{:S(2)}, u32[]{:S(2)}) collective-permute-start(bf16[64,512]{1,0:T(8,128)(2,1)S(1)} %get-tuple-element.51), channel_id=1, source_target_pairs={{0,16},{2,18},{4,20},{6,22},{8,24},{10,26},{12,28},{14,30},{16,0},... | collective-permute-start | bytes 196616 | tf_op jit(solution)/shard_map/ppermute | solution.py:302
  100.3 6.4 %collective-permute-start.22 = (bf16[64,512]{1,0:T(8,128)(2,1)S(1)}, bf16[64,512]{1,0:T(8,128)(2,1)S(1)}, u32[]{:S(2)}, u32[]{:S(2)}) collective-permute-start(bf16[64,512]{1,0:T(8,128)(2,1)S(1)} %get-tuple-element.52), channel_id=1, source_target_pairs={{0,24},{2,26},{4,28},{6,30},{8,16},{10,18},{12,20},{14,22},{16,8},... | collective-permute-start | bytes 196616 | tf_op jit(solution)/shard_map/ppermute | solution.py:302
